TPU v7x, 32 devices: a whole 2x2x4 slice. The times are simulated.
32 devices in a mesh: dp: 8 (over y, x, core), seq: 4 (over z).
Axes of the slice: x: 2, y: 2, z: 4, core: 2. Of those that a mesh axis runs over, the one named last changes fastest.
Arguments:
- tokens: bfloat16 [4096, 2048], P(('dp', 'seq')), may hold values from -6 to 6
- cotangent: bfloat16 [4096, 2048], P(('dp', 'seq')), may hold values from -6 to 6
- lengths: int32 [8, 8], P('dp'), may hold values from 1 to 448, 512 in all within a row
- norm_attn: float32 [2048], replicated, may hold values from 0.1 to 1.9
- w_query: bfloat16 [2048, 2048], P(('dp', 'seq')), may hold values from -0.125 to 0.125
- w_key: bfloat16 [2048, 2048], P(('dp', 'seq')), may hold values from -0.125 to 0.125
- w_value: bfloat16 [2048, 2048], P(('dp', 'seq')), may hold values from -0.125 to 0.125
- w_out: bfloat16 [2048, 2048], P(('dp', 'seq')), may hold values from -1 to 1
- norm_ffn: float32 [2048], replicated, may hold values from 0.1 to 1.9
- w_gate: bfloat16 [2048, 5632], P(('dp', 'seq')), may hold values from -0.125 to 0.125
- w_up: bfloat16 [2048, 5632], P(('dp', 'seq')), may hold values from -0.125 to 0.125
- w_down: bfloat16 [5632, 2048], P(('dp', 'seq')), may hold values from -0.078125 to 0.078125
Outputs:
- activations: bfloat16 [4096, 2048], P(('dp', 'seq'))
- token_grad: float32 [4096, 2048], P(('dp', 'seq'))
- grad_norm_attn: float32 [2048], replicated
- grad_w_query: float32 [2048, 2048], P(('dp', 'seq'))
- grad_w_key: float32 [2048, 2048], P(('dp', 'seq'))
- grad_w_value: float32 [2048, 2048], P(('dp', 'seq'))
- grad_w_out: float32 [2048, 2048], P(('dp', 'seq'))
- grad_norm_ffn: float32 [2048], replicated
- grad_w_gate: float32 [2048, 5632], P(('dp', 'seq'))
- grad_w_up: float32 [2048, 5632], P(('dp', 'seq'))
- grad_w_down: float32 [5632, 2048], P(('dp', 'seq'))
Inputs may be any that keep to these rules, and one draw needn't show every extreme that they name: Each row's lengths add up to 512, and in every row one document is 448 long.
All inputs are finite; a program needn't handle non-finite values.
Results may differ from a plain program's by a relative error of at most 0.014.
Values may be sent and summed in bfloat16 or wider, within the bound.
No kernel may reach another device: no remote copies, remote signals or barrier semaphores. Data moves between devices by JAX's collectives and lax.ppermute only.
A program may use at most 512 MiB of HBM per device.

v0:
```python
import math

import jax
import jax.numpy as jnp
from jax import lax
from jax.sharding import PartitionSpec as P

HEADS = 16
HEAD = 128
WINDOW = 64


norm_eps = 1e-05
masked_score = -1e30


def shifted(x, axis, by):
    length = lax.axis_size(axis)
    pairs = [(i, i + by) for i in range(length) if 0 <= i + by < length]
    return lax.ppermute(x, axis, pairs)


def doc_number(positions, doc_ends):
    counted = jnp.sum((positions[:, None] >= doc_ends[None, :]).astype(jnp.int32), axis=1)
    return jnp.where(positions < 0, -1, counted)


def band_window(values, blocks, extent):
    shaped = values.reshape((blocks + 1, extent) + values.shape[1:])
    return jnp.concatenate([shaped[:-1], shaped[1:]], axis=1)


def allowed_pairs(doc_query, doc_keys, blocks, extent):
    offset_query = jnp.arange(extent)[:, None]
    offset_key = jnp.arange(2 * extent)[None, :]
    causal_band = (offset_key > offset_query) & (offset_key <= offset_query + extent)
    same_doc = (
        doc_query.reshape(blocks, extent)[:, :, None]
        == band_window(doc_keys, blocks, extent)[:, None, :]
    )
    return (causal_band[None] & same_doc)[:, None]


def fold_window(window_grads, blocks):
    zero_block = jnp.zeros((1, WINDOW) + window_grads.shape[2:], jnp.float32)
    lower = jnp.concatenate([window_grads[:, :WINDOW], zero_block], axis=0)
    upper = jnp.concatenate([zero_block, window_grads[:, WINDOW:]], axis=0)
    return (lower + upper).reshape((blocks + 1) * WINDOW, HEADS * HEAD)


def rms_parts(values):
    inverse = lax.rsqrt(jnp.mean(values * values, axis=1, keepdims=True) + norm_eps)
    return (values * inverse, inverse)


def norm_back(grad_normed, gain, normed, inverse):
    scaled = grad_normed * gain
    back = inverse * (scaled - normed * jnp.mean(scaled * normed, axis=1, keepdims=True))
    return (back, jnp.sum(grad_normed * normed, axis=0))


def column_product(left, piece):
    return jnp.dot(left, piece, preferred_element_type=jnp.float32)


def transposed_product(left, piece):
    return lax.dot_general(
        left, piece, (((1,), (1,)), ((), ())), preferred_element_type=jnp.float32
    )


def row_gradient(left, right):
    return lax.dot_general(
        left, right, (((0,), (0,)), ((), ())), preferred_element_type=jnp.float32
    )


def masked_scores(query_blocks, key_window, allowed, score_scale):
    raw = (
        jnp.einsum("bqhd,bkhd->bhqk", query_blocks, key_window, preferred_element_type=jnp.float32)
        * score_scale
    )
    return jnp.where(allowed, raw, masked_score)


def body(
    tokens,
    cotangent,
    lengths,
    norm_attn,
    w_query,
    w_key,
    w_value,
    w_out,
    norm_ffn,
    w_gate,
    w_up,
    w_down,
):
    rows_dev = tokens.shape[0]
    model_width = tokens.shape[1]
    hidden_width = w_gate.shape[1]
    blocks = rows_dev // WINDOW
    score_scale = 1.0 / math.sqrt(HEAD)
    inputs = tokens.astype(jnp.float32)
    normed_attn, inverse_attn = rms_parts(inputs)
    normed_attn_b = (normed_attn * norm_attn).astype(jnp.bfloat16)
    pieces = (
        lax.all_gather(w_query, ("dp", "seq"), axis=0, tiled=True),
        lax.all_gather(w_key, ("dp", "seq"), axis=0, tiled=True),
        lax.all_gather(w_value, ("dp", "seq"), axis=0, tiled=True),
    )
    query = column_product(normed_attn_b, pieces[0])
    key_proj = column_product(normed_attn_b, pieces[1])
    value_proj = column_product(normed_attn_b, pieces[2])
    query_b = query.astype(jnp.bfloat16)
    key_b = key_proj.astype(jnp.bfloat16)
    value_b = value_proj.astype(jnp.bfloat16)
    rim_key, rim_value = shifted(
        (key_b[rows_dev - WINDOW :], value_b[rows_dev - WINDOW :]), "seq", 1
    )
    key_window = band_window(jnp.concatenate([rim_key, key_b], axis=0), blocks, WINDOW).reshape(
        blocks, 2 * WINDOW, HEADS, HEAD
    )
    value_window = band_window(
        jnp.concatenate([rim_value, value_b], axis=0), blocks, WINDOW
    ).reshape(blocks, 2 * WINDOW, HEADS, HEAD)
    query_blocks = query_b.reshape(blocks, WINDOW, HEADS, HEAD)
    doc_ends = jnp.cumsum(lengths[0])
    first_pos = lax.axis_index("seq") * rows_dev
    doc_query = doc_number(first_pos + jnp.arange(rows_dev, dtype=jnp.int32), doc_ends)
    doc_keys = doc_number(
        first_pos - WINDOW + jnp.arange(rows_dev + WINDOW, dtype=jnp.int32), doc_ends
    )
    allowed = allowed_pairs(doc_query, doc_keys, blocks, WINDOW)
    limited = masked_scores(query_blocks, key_window, allowed, score_scale)
    row_top = jnp.max(limited, axis=-1, keepdims=True)
    exp_scores = jnp.exp(limited - row_top)
    row_total = jnp.sum(exp_scores, axis=-1, keepdims=True)
    probs_b = (exp_scores / row_total).astype(jnp.bfloat16)
    log_total = row_top + jnp.log(row_total)
    attended_b = (
        jnp.einsum("bhqk,bkhd->bqhd", probs_b, value_window, preferred_element_type=jnp.float32)
        .reshape(rows_dev, model_width)
        .astype(jnp.bfloat16)
    )
    branch = column_product(attended_b, lax.all_gather(w_out, ("dp", "seq"), axis=0, tiled=True))
    middle = inputs + branch
    normed_ffn, inverse_ffn = rms_parts(middle)
    normed_ffn_b = (normed_ffn * norm_ffn).astype(jnp.bfloat16)
    pieces = (
        lax.all_gather(w_gate, ("dp", "seq"), axis=0, tiled=True),
        lax.all_gather(w_up, ("dp", "seq"), axis=0, tiled=True),
    )
    gate = column_product(normed_ffn_b, pieces[0])
    up_proj = column_product(normed_ffn_b, pieces[1])
    sigmoid_gate = jax.nn.sigmoid(gate)
    hidden_b = (gate * sigmoid_gate * up_proj).astype(jnp.bfloat16)
    ffn_out = column_product(hidden_b, lax.all_gather(w_down, ("dp", "seq"), axis=0, tiled=True))
    activations = (middle + ffn_out).astype(jnp.bfloat16)
    grad_w_down = lax.psum_scatter(
        row_gradient(hidden_b, cotangent), ("dp", "seq"), scatter_dimension=0, tiled=True
    )
    grad_hidden = transposed_product(
        cotangent, lax.all_gather(w_down, ("dp", "seq"), axis=0, tiled=True)
    )
    gate_back, up_back, sigmoid_back = (gate, up_proj, sigmoid_gate)
    grad_gate_b = (
        grad_hidden * up_back * sigmoid_back * (1.0 + gate_back * (1.0 - sigmoid_back))
    ).astype(jnp.bfloat16)
    grad_up_b = (grad_hidden * gate_back * sigmoid_back).astype(jnp.bfloat16)
    pieces = lax.all_gather((w_gate, w_up), ("dp", "seq"), axis=0, tiled=True)
    grad_normed_ffn = transposed_product(grad_gate_b, pieces[0]) + transposed_product(
        grad_up_b, pieces[1]
    )
    back_ffn, gain_ffn_part = norm_back(grad_normed_ffn, norm_ffn, normed_ffn, inverse_ffn)
    grad_middle = cotangent.astype(jnp.float32) + back_ffn
    grad_branch_b = grad_middle.astype(jnp.bfloat16)
    grad_attended_b = transposed_product(
        grad_branch_b, lax.all_gather(w_out, ("dp", "seq"), axis=0, tiled=True)
    ).astype(jnp.bfloat16)
    grad_blocks = grad_attended_b.reshape(blocks, WINDOW, HEADS, HEAD)
    grad_probs = jnp.einsum(
        "bqhd,bkhd->bhqk", grad_blocks, value_window, preferred_element_type=jnp.float32
    )
    probs_again = jnp.exp(masked_scores(query_blocks, key_window, allowed, score_scale) - log_total)
    grad_scores_b = (
        probs_again * (grad_probs - jnp.sum(probs_again * grad_probs, axis=-1, keepdims=True))
    ).astype(jnp.bfloat16)
    grad_query_b = (
        (
            jnp.einsum(
                "bhqk,bkhd->bqhd", grad_scores_b, key_window, preferred_element_type=jnp.float32
            )
            * score_scale
        )
        .reshape(rows_dev, model_width)
        .astype(jnp.bfloat16)
    )
    key_grads = fold_window(
        jnp.einsum(
            "bhqk,bqhd->bkhd", grad_scores_b, query_blocks, preferred_element_type=jnp.float32
        )
        * score_scale,
        blocks,
    )
    value_grads = fold_window(
        jnp.einsum("bhqk,bqhd->bkhd", probs_b, grad_blocks, preferred_element_type=jnp.float32),
        blocks,
    )
    back_key, back_value = (
        shifted(key_grads[:WINDOW].astype(jnp.bfloat16), "seq", -1).astype(jnp.float32),
        shifted(value_grads[:WINDOW].astype(jnp.bfloat16), "seq", -1).astype(jnp.float32),
    )
    own_key = key_grads[WINDOW:]
    own_value = value_grads[WINDOW:]
    grad_key_b = jnp.concatenate(
        [own_key[: rows_dev - WINDOW], own_key[rows_dev - WINDOW :] + back_key], axis=0
    ).astype(jnp.bfloat16)
    grad_value_b = jnp.concatenate(
        [own_value[: rows_dev - WINDOW], own_value[rows_dev - WINDOW :] + back_value], axis=0
    ).astype(jnp.bfloat16)
    pieces = lax.all_gather((w_query, w_key, w_value), ("dp", "seq"), axis=0, tiled=True)
    grad_normed_attn = (
        transposed_product(grad_query_b, pieces[0])
        + transposed_product(grad_key_b, pieces[1])
        + transposed_product(grad_value_b, pieces[2])
    )
    back_attn, gain_attn_part = norm_back(grad_normed_attn, norm_attn, normed_attn, inverse_attn)
    token_grad = grad_middle + back_attn
    grad_norm_attn, grad_norm_ffn = lax.psum((gain_attn_part, gain_ffn_part), ("dp", "seq"))
    wide = lax.psum_scatter(
        jnp.concatenate(
            [
                row_gradient(normed_attn_b, grad_query_b),
                row_gradient(normed_attn_b, grad_key_b),
                row_gradient(normed_attn_b, grad_value_b),
                row_gradient(attended_b, grad_branch_b),
                row_gradient(normed_ffn_b, grad_gate_b),
                row_gradient(normed_ffn_b, grad_up_b),
            ],
            axis=1,
        ),
        ("dp", "seq"),
        scatter_dimension=0,
        tiled=True,
    )
    grad_w_query = wide[:, :model_width]
    grad_w_key = wide[:, model_width : 2 * model_width]
    grad_w_value = wide[:, 2 * model_width : 3 * model_width]
    grad_w_out = wide[:, 3 * model_width : 4 * model_width]
    grad_w_gate = wide[:, 4 * model_width : 4 * model_width + hidden_width]
    grad_w_up = wide[:, 4 * model_width + hidden_width :]
    return (
        activations,
        token_grad,
        grad_norm_attn,
        grad_w_query,
        grad_w_key,
        grad_w_value,
        grad_w_out,
        grad_norm_ffn,
        grad_w_gate,
        grad_w_up,
        grad_w_down,
    )


def solution(mesh):
    placed = (
        P(("dp", "seq"), None),
        P(("dp", "seq"), None),
        P("dp", None),
        P(),
        P(("dp", "seq"), None),
        P(("dp", "seq"), None),
        P(("dp", "seq"), None),
        P(("dp", "seq"), None),
        P(),
        P(("dp", "seq"), None),
        P(("dp", "seq"), None),
        P(("dp", "seq"), None),
    )
    return jax.shard_map(
        body,
        mesh=mesh,
        in_specs=placed,
        out_specs=(
            P(("dp", "seq"), None),
            P(("dp", "seq"), None),
            P(),
            P(("dp", "seq"), None),
            P(("dp", "seq"), None),
            P(("dp", "seq"), None),
            P(("dp", "seq"), None),
            P(),
            P(("dp", "seq"), None),
            P(("dp", "seq"), None),
            P(("dp", "seq"), None),
        ),
        check_vma=False,
    )
```

profile of v0, /device:TPU:0, one launch (start us, length us, event | category | flops | bytes accessed | tf_op | source)
XLA Modules:
  0.0 5220.4 jit_solution(164188819503981143)
XLA Ops:
  14.7 76.4 %all-gather.12.cloned.1.call-done = bf16[2048,2048]{1,0:T(8,128)(2,1)} async-done(((bf16[64,2048]{1,0:T(8,128)(2,1)}), bf16[2048,2048]{1,0:T(8,128)(2,1)}) %all-gather.12.cloned.1.call-update) | async-done | bytes 8388624 | tf_op jit(solution)/shard_map/all_gather | solution.py:110
  91.1 4.9 convolution_convert_fusion.1
  100.1 70.7 %all-gather.8.cloned.1.call-done = bf16[2048,2048]{1,0:T(8,128)(2,1)} async-done(((bf16[64,2048]{1,0:T(8,128)(2,1)}), bf16[2048,2048]{1,0:T(8,128)(2,1)}) %all-gather.8.cloned.1.call-update) | async-done | bytes 8388624 | tf_op jit(solution)/shard_map/all_gather | solution.py:111
  170.8 4.7 convolution_convert_fusion.3
  176.2 4.1 collective-permute-start
  180.4 70.2 %all-gather.10.cloned.1.call-done = bf16[2048,2048]{1,0:T(8,128)(2,1)} async-done(((bf16[64,2048]{1,0:T(8,128)(2,1)}), bf16[2048,2048]{1,0:T(8,128)(2,1)}) %all-gather.10.cloned.1.call-update) | async-done | bytes 8388624 | tf_op jit(solution)/shard_map/all_gather | solution.py:109
  250.5 4.7 fusion.11
  260.7 68.6 %all-gather.14.cloned.1.call-done = bf16[2048,2048]{1,0:T(8,128)(2,1)} async-done(((bf16[64,2048]{1,0:T(8,128)(2,1)}), bf16[2048,2048]{1,0:T(8,128)(2,1)}) %all-gather.14.cloned.1.call-update) | async-done | bytes 8388624 | tf_op jit(solution)/shard_map/all_gather | solution.py:147
  329.3 4.8 multiply_reduce_fusion.3
  334.3 140.9 %all-gather.18.cloned.1.call-done = bf16[2048,5632]{1,0:T(8,128)(2,1)} async-done(((bf16[64,5632]{1,0:T(8,128)(2,1)}), bf16[2048,5632]{1,0:T(8,128)(2,1)}) %all-gather.18.cloned.1.call-update) | async-done | bytes 23068688 | tf_op jit(solution)/shard_map/all_gather | solution.py:153
  475.2 12.3 fusion.64
  487.5 133.2 %all-gather.16.cloned.1.call-done = bf16[2048,5632]{1,0:T(8,128)(2,1)} async-done(((bf16[64,5632]{1,0:T(8,128)(2,1)}), bf16[2048,5632]{1,0:T(8,128)(2,1)}) %all-gather.16.cloned.1.call-update) | async-done | bytes 23068688 | tf_op jit(solution)/shard_map/all_gather | solution.py:152
  620.7 12.3 fusion.63
  633.0 133.4 %all-gather.20.cloned.1.call-done = bf16[5632,2048]{1,0:T(8,128)(2,1)} async-done(((bf16[176,2048]{1,0:T(8,128)(2,1)}), bf16[5632,2048]{1,0:T(8,128)(2,1)}) %all-gather.20.cloned.1.call-update) | async-done | bytes 23068688 | tf_op jit(solution)/shard_map/all_gather | solution.py:159
  766.4 15.0 multiply_convert_fusion
  781.4 12.6 fusion.65
  794.0 13.8 multiply_reduce_fusion
  809.6 6.3 fusion.12
  825.5 8.3 convolution_dynamic-update-slice_fusion.5
  834.4 3.6 collective-permute-done.2
  838.2 8.6 convolution_dynamic-update-slice_fusion.4
  847.1 8.3 convolution_dynamic-update-slice_fusion.3
  855.4 8.3 convolution_dynamic-update-slice_fusion.2
  863.7 18.3 convolution_dynamic-update-slice_fusion.1
  882.0 18.2 convolution_dynamic-update-slice_fusion
  901.2 19.4 fusion.66
  921.7 6.4 fusion.26
  928.2 11.8 fusion
  946.2 44.1 all-reduce.4
  991.6 3246.3 %reduce-scatter.3.cloned.1.call-done = f32[64,19456]{1,0:T(8,128)} async-done(((f32[2048,19456]{1,0:T(8,128)}), f32[64,19456]{1,0:T(8,128)}) %reduce-scatter.3.cloned.1.call-update) | async-done | bytes 4980752 | tf_op jit(solution)/shard_map/reduce_scatter | solution.py:232
  4240.8 3.6 fusion.55
  4244.4 969.0 %reduce-scatter.5.cloned.1.call-done = f32[176,2048]{1,0:T(8,128)} async-done(((f32[5632,2048]{1,0:T(8,128)}), f32[176,2048]{1,0:T(8,128)}) %reduce-scatter.5.cloned.1.call-update) | async-done | bytes 1441808 | tf_op jit(solution)/shard_map/reduce_scatter | solution.py:161
  (158 shorter events, 42.2 us)
Async XLA Ops:
  7.2 83.9 %all-gather.12.cloned.1.call-start = ((), (), s32[]{:S(2)}) async-start(), calls=%async_computation.4 | async-start | bytes 8650752 | tf_op jit(solution)/shard_map/all_gather | solution.py:110
  7.9 162.9 %all-gather.8.cloned.1.call-start = ((), (), s32[]{:S(2)}) async-start(), calls=%async_computation.2 | async-start | bytes 8650752 | tf_op jit(solution)/shard_map/all_gather | solution.py:111
  8.7 241.9 %all-gather.10.cloned.1.call-start = ((), (), s32[]{:S(2)}) async-start(), calls=%async_computation.3 | async-start | bytes 8650752 | tf_op jit(solution)/shard_map/all_gather | solution.py:109
  9.4 319.9 %all-gather.14.cloned.1.call-start = ((), (), s32[]{:S(2)}) async-start(), calls=%async_computation.5 | async-start | bytes 8650752 | tf_op jit(solution)/shard_map/all_gather | solution.py:147
  10.0 465.3 %all-gather.18.cloned.1.call-start = ((), (), s32[]{:S(2)}) async-start(), calls=%async_computation.7 | async-start | bytes 23789568 | tf_op jit(solution)/shard_map/all_gather | solution.py:153
  10.6 610.2 %all-gather.16.cloned.1.call-start = ((), (), s32[]{:S(2)}) async-start(), calls=%async_computation.6 | async-start | bytes 23789568 | tf_op jit(solution)/shard_map/all_gather | solution.py:152
  11.1 755.2 %all-gather.20.cloned.1.call-start = ((), (), s32[]{:S(2)}) async-start(), calls=%async_computation.8 | async-start | bytes 23789568 | tf_op jit(solution)/shard_map/all_gather | solution.py:159
  11.9 4226.1 %reduce-scatter.3.cloned.1.call-start = ((), (), s32[]{:S(2)}) async-start(), calls=%async_computation.9 | async-start | bytes 164364288 | tf_op jit(solution)/shard_map/reduce_scatter | solution.py:232
  14.4 156.4 %copy-start = (bf16[128,2048]{1,0:T(8,128)(2,1)S(1)}, bf16[128,2048]{1,0:T(8,128)(2,1)}, u32[]{:S(2)}) copy-start(bf16[128,2048]{1,0:T(8,128)(2,1)} %param.12) | copy-start | bytes 1572868
  14.4 156.4 %copy-start.14 = (f32[2048]{0:T(1024)S(1)}, f32[2048]{0:T(1024)}, u32[]{:S(2)}) copy-start(f32[2048]{0:T(1024)} %param.15) | copy-start | bytes 24580
  96.7 158.9 %collective-permute-start.1 = (bf16[64,2048]{1,0:T(8,128)(2,1)}, bf16[64,2048]{1,0:T(8,128)(2,1)S(1)}, u32[]{:S(2)}, u32[]{:S(2)}) collective-permute-start(bf16[64,2048]{1,0:T(8,128)(2,1)} %slice.128), channel_id=1, source_target_pairs={{0,1},{1,2},{2,3},{4,5},{5,6},{6,7},{8,9},{9,10},{10,11},{12,13},{... | collective-permute-start | bytes 786440 | tf_op jit(solution)/shard_map/ppermute | solution.py:20
  176.2 79.6 %collective-permute-start = (bf16[64,2048]{1,0:T(8,128)(2,1)}, bf16[64,2048]{1,0:T(8,128)(2,1)}, u32[]{:S(2)}, u32[]{:S(2)}) collective-permute-start(bf16[64,2048]{1,0:T(8,128)(2,1)} %slice.129), channel_id=1, source_target_pairs={{0,1},{1,2},{2,3},{4,5},{5,6},{6,7},{8,9},{9,10},{10,11},{12,13},{... | collective-permute-start | bytes 786440 | tf_op jit(solution)/shard_map/ppermute | solution.py:20
  259.2 70.2 %copy-start.21 = (bf16[2,128,16,128]{3,1,2,0:T(8,128)(2,1)}, bf16[2,128,16,128]{3,1,2,0:T(8,128)(2,1)S(1)}, u32[]{:S(2)}) copy-start(bf16[2,128,16,128]{3,1,2,0:T(8,128)(2,1)S(1)} %copy_dynamic-update-slice_fusion.2) | copy-start | bytes 3145732
  260.4 73.8 %copy-start.25 = (f32[2048]{0:T(1024)S(1)}, f32[2048]{0:T(1024)}, u32[]{:S(2)}) copy-start(f32[2048]{0:T(1024)} %param.20) | copy-start | bytes 24580
  260.7 73.6 %copy-start.6 = (bf16[2,64,16,128]{3,2,1,0:T(8,128)(2,1)}, bf16[2,64,16,128]{3,2,1,0:T(8,128)(2,1)S(1)}, u32[]{:S(2)}) copy-start(bf16[2,64,16,128]{3,2,1,0:T(8,128)(2,1)S(1)} %copy.60) | copy-start | bytes 1572868
  487.5 278.8 %copy-start.23 = (bf16[128,2048]{1,0:T(8,128)(2,1)S(1)}, bf16[128,2048]{1,0:T(8,128)(2,1)}, u32[]{:S(2)}) copy-start(bf16[128,2048]{1,0:T(8,128)(2,1)} %param.13) | copy-start | bytes 1572868
  781.4 12.6 copy-start.3
  821.2 12.6 copy-start.10
  822.0 24.8 collective-permute-start.3
  824.0 14.0 collective-permute-start.2
  834.0 12.9 copy-start.15
  838.2 8.7 copy-start.17
  847.1 8.3 copy-start.19
  847.1 8.3 copy-start.7
  855.4 8.3 copy-start.4
  900.2 4313.2 %reduce-scatter.5.cloned.1.call-start = ((), (), s32[]{:S(2)}) async-start(), calls=%async_computation.10 | async-start | bytes 47579136 | tf_op jit(solution)/shard_map/reduce_scatter | solution.py:161
  921.7 18.3 slice-start
  921.7 21.3 slice-start.2
  928.2 11.9 slice-start.1
  928.2 11.9 copy-start.16
  928.2 11.8 copy-start.18
  928.2 14.8 slice-start.3
  (12 other events, 38.9 us)
Sparse Core Ops, SparseCore 0:
  10.9 80.0 all-gather.11
  94.0 76.7 all-gather.7
  173.8 76.7 all-gather.9
  253.3 75.9 all-gather.13
  332.0 143.1 all-gather.17
  477.9 142.7 all-gather.15
  623.6 142.7 all-gather.19
  900.3 3337.5 reduce-scatter.2
  4241.0 972.3 reduce-scatter.4
where the time goes:
time: 5230 us; the launch traced here: 5220 us
  waiting for transfers between devices  4920 us (94%)
  matrix products  211 us (4%)
    reduce_scatter x1, waiting for transfers between devices, body(): lax.psum_scatter(jnp.concatenate([row_gradient(normed_attn_b, grad_query_...  3250 us
    reduce_scatter x1, waiting for transfers between devices, body(): lax.psum_scatter(row_gradient(hidden_b, cotangent), ('dp', 'seq'), scatte...  969 us
    all_gather x1, waiting for transfers between devices, body(): lax.all_gather(w_up, ('dp', 'seq'), axis=0, tiled=True)  141 us
    all_gather x1, waiting for transfers between devices, body(): lax.all_gather(w_down, ('dp', 'seq'), axis=0, tiled=True)  133 us
    all_gather x1, waiting for transfers between devices, body(): lax.all_gather(w_gate, ('dp', 'seq'), axis=0, tiled=True)  133 us
  transfers between devices with their start and end apart: 13, of which 10 were waited for; matrix products, arithmetic and copies ran while one was open for 2% of the time, Pallas kernels for 0%

commit v1 on v0

v1 whole, which is shorter than its diff:
```python
import math

import jax
import jax.numpy as jnp
from jax import lax
from jax.sharding import Mesh
from jax.sharding import PartitionSpec as P

HEADS = 16
HEAD = 128
WINDOW = 64

ALL = ("y", "x", "c", "z")
norm_eps = 1e-05
masked_score = -1e30
f32 = jnp.float32
bf16 = jnp.bfloat16


def dot(left, right, dims=((1,), (0,))):
    return lax.dot_general(left, right, (dims, ((), ())), preferred_element_type=f32)


def dot_nt(left, right):
    return dot(left, right, ((1,), (1,)))


def dot_tn(left, right):
    return dot(left, right, ((0,), (0,)))


def swap(x, axis):
    return lax.ppermute(x, axis, [(0, 1), (1, 0)])


def ring_order(n):
    return list(range(1, n, 2)) + list(range(n - 2, -1, -2)) if n > 1 else [0]


def ring_pairs(n):
    order = ring_order(n)
    return [(order[i], order[(i + 1) % n]) for i in range(n)]


def hop(x):
    return lax.ppermute(x, "z", ring_pairs(lax.axis_size("z")))


def ring_sources(n):
    order = ring_order(n)
    spot = {place: at for at, place in enumerate(order)}
    return [[order[(spot[z] - k) % n] for k in range(n)] for z in range(n)]


def pick(options, which):
    out = options[0]
    for i in range(1, len(options)):
        out = jnp.where(which == i, options[i], out)
    return out


def both_cores(x):
    return jnp.stack([x, swap(x, "c")])


def core_order(mine, other, at):
    first = lax.axis_index("c") == 0
    return jnp.stack([jnp.where(first, mine, other), jnp.where(first, other, mine)], axis=at)


def ring_gather(x):
    n = lax.axis_size("z")
    parts = [x]
    for _ in range(n - 1):
        parts.append(hop(parts[-1]))
    return [both_cores(part) for part in parts]


def ring_scatter(partials):
    n = len(partials)

    def reduced(k):
        return partials[k][0] + swap(partials[k][1].astype(bf16), "c").astype(f32)

    total = reduced(1 % n)
    for s in range(n - 1):
        total = hop(total.astype(bf16)).astype(f32) + reduced((s + 2) % n)
    return total


def gather_plane(x):
    return lax.all_gather(x, ("y", "x"), axis=0, tiled=False)


def scatter_axis(x, axis):
    n = lax.axis_size(axis)
    if n != 2:
        return lax.psum_scatter(x.astype(bf16), axis, scatter_dimension=0, tiled=False).astype(f32)
    me = lax.axis_index(axis)
    own = lax.dynamic_index_in_dim(x, me, 0, keepdims=False)
    sent = lax.dynamic_index_in_dim(x, 1 - me, 0, keepdims=False)
    return own + swap(sent.astype(bf16), axis).astype(f32)


def scatter_plane(x):
    ny, nx = lax.axis_size("y"), lax.axis_size("x")
    half = (x.shape[-1] // 2) // 128 * 128
    x = x.reshape((ny, nx) + x.shape[1:])
    left, right = x[..., :half], x[..., half:]
    left = scatter_axis(scatter_axis(left, "y"), "x")
    right = scatter_axis(scatter_axis(jnp.swapaxes(right, 0, 1), "x"), "y")
    return jnp.concatenate([left, right], axis=-1)


def exchange(x):
    me = lax.axis_index("c")
    own = lax.dynamic_index_in_dim(x, me, 0, keepdims=False)
    other = swap(lax.dynamic_index_in_dim(x, 1 - me, 0, keepdims=False), "c")
    both = core_order(own, other, 1)
    return jnp.swapaxes(lax.all_to_all(both, "z", 0, 0, tiled=True), 0, 1)


def butterfly(x):
    for axis in ALL:
        n = lax.axis_size(axis)
        step = 1
        while step < n:
            x = x + lax.ppermute(x, axis, [(i, i ^ step) for i in range(n)])
            step *= 2
    return x


def doc_number(positions, doc_ends):
    counted = jnp.sum((positions[:, None] >= doc_ends[None, :]).astype(jnp.int32), axis=1)
    return jnp.where(positions < 0, -1, counted)


def windows(x, fill):
    pad = jnp.full((WINDOW,) + x.shape[1:], fill, x.dtype)
    shaped = jnp.concatenate([pad, x], axis=0).reshape((-1, WINDOW) + x.shape[1:])
    return jnp.concatenate([shaped[:-1], shaped[1:]], axis=1)


def unwindows(x):
    blocks = x.shape[0]
    zero = jnp.zeros((1, WINDOW) + x.shape[2:], x.dtype)
    below = jnp.concatenate([x[1:, :WINDOW], zero], axis=0)
    return (x[:, WINDOW:] + below).reshape((blocks * WINDOW,) + x.shape[2:])


def allowed_pairs(lengths, length):
    doc_ends = jnp.cumsum(lengths)
    docs = doc_number(jnp.arange(length, dtype=jnp.int32), doc_ends)
    offset_query = jnp.arange(WINDOW)[:, None]
    offset_key = jnp.arange(2 * WINDOW)[None, :]
    band = (offset_key > offset_query) & (offset_key <= offset_query + WINDOW)
    same = docs.reshape(-1, WINDOW)[:, :, None] == windows(docs, -1)[:, None, :]
    return (band[None] & same)[:, None]


def attention(query, key, value, lengths):
    length = query.shape[0]
    scale = 1.0 / math.sqrt(HEAD)
    allowed = allowed_pairs(lengths, length)
    query_blocks = query.reshape(-1, WINDOW, *query.shape[1:])
    key_window, value_window = windows(key, 0), windows(value, 0)
    raw = jnp.einsum("bqhd,bkhd->bhqk", query_blocks, key_window, preferred_element_type=f32)
    limited = jnp.where(allowed, raw * scale, masked_score)
    top = jnp.max(limited, axis=-1, keepdims=True)
    exped = jnp.exp(limited - top)
    probs = exped / jnp.sum(exped, axis=-1, keepdims=True)
    probs_b = probs.astype(bf16)
    mixed = jnp.einsum("bhqk,bkhd->bqhd", probs_b, value_window, preferred_element_type=f32)
    return mixed.reshape(query.shape).astype(bf16), probs


def attention_back(query, key, value, probs, grad):
    scale = 1.0 / math.sqrt(HEAD)
    probs_b = probs.astype(bf16)
    query_blocks = query.reshape(-1, WINDOW, *query.shape[1:])
    grad_blocks = grad.reshape(-1, WINDOW, *query.shape[1:])
    key_window, value_window = windows(key, 0), windows(value, 0)
    grad_probs = jnp.einsum(
        "bqhd,bkhd->bhqk", grad_blocks, value_window, preferred_element_type=f32
    )
    inner = jnp.sum(probs * grad_probs, axis=-1, keepdims=True)
    grad_scores = (probs * (grad_probs - inner)).astype(bf16)
    grad_query = (
        jnp.einsum("bhqk,bkhd->bqhd", grad_scores, key_window, preferred_element_type=f32) * scale
    )
    grad_key = (
        jnp.einsum("bhqk,bqhd->bkhd", grad_scores, query_blocks, preferred_element_type=f32) * scale
    )
    grad_value = jnp.einsum("bhqk,bqhd->bkhd", probs_b, grad_blocks, preferred_element_type=f32)
    return (
        grad_query.reshape(query.shape).astype(bf16),
        unwindows(grad_key).astype(bf16),
        unwindows(grad_value).astype(bf16),
    )


def rms_parts(values):
    inverse = lax.rsqrt(jnp.mean(values * values, axis=1, keepdims=True) + norm_eps)
    return (values * inverse, inverse)


def norm_back(grad_normed, gain, normed, inverse):
    scaled = grad_normed * gain
    back = inverse * (scaled - normed * jnp.mean(scaled * normed, axis=1, keepdims=True))
    return (back, jnp.sum(grad_normed * normed, axis=0))


def body(
    tokens,
    cotangent,
    lengths,
    norm_attn,
    w_query,
    w_key,
    w_value,
    w_out,
    norm_ffn,
    w_gate,
    w_up,
    w_down,
):
    t, width = tokens.shape
    own_rows, hidden_width = w_gate.shape
    nz = lax.axis_size("z")
    plane = lax.axis_size("y") * lax.axis_size("x")
    z = lax.axis_index("z")
    sources = jnp.asarray(ring_sources(nz), jnp.int32)[z]
    feats = width // (2 * nz)
    heads_here = feats // HEAD
    block = hidden_width // (plane * 2 * nz)
    units = plane * block

    qkv = jnp.stack([w_query, w_key, w_value]).reshape(3, own_rows, 2, nz, feats)
    qkv = exchange(qkv.transpose(2, 3, 0, 1, 4))
    qkv = gather_plane(qkv.transpose(2, 0, 1, 3, 4))
    w_qkv = [qkv[:, i].reshape(width, feats) for i in range(3)]

    inputs = tokens.astype(f32)
    normed_attn, inverse_attn = rms_parts(inputs)
    normed_attn_b = (normed_attn * norm_attn).astype(bf16)
    attn_in = [part.reshape(2 * t, width) for part in ring_gather(normed_attn_b)]

    lengths_both = both_cores(lengths[0])
    w_out_all = lax.all_gather(w_out, ALL, axis=0, tiled=True)
    gate_up = jnp.stack([w_gate, w_up]).reshape(2, own_rows, plane, 2, nz, block)
    gate_up = exchange(
        gate_up.transpose(3, 4, 0, 1, 2, 5).reshape(2, nz, 2, own_rows, units)
    )
    gate_up = gather_plane(gate_up.transpose(2, 0, 1, 3, 4))
    w_gate_here, w_up_here = (gate_up[:, i].reshape(width, units) for i in range(2))
    w_down_here = gather_plane(w_down).reshape(units, width)
    cot = [part.reshape(2 * t, width) for part in ring_gather(cotangent)]

    projected = []
    for i in range(3):
        placed = jnp.zeros((nz, 2, t, feats), bf16)
        for k in range(nz):
            piece = dot(attn_in[k], w_qkv[i]).astype(bf16).reshape(1, 2, t, feats)
            placed = lax.dynamic_update_slice(placed, piece, (sources[k], 0, 0, 0))
        projected.append(
            placed.transpose(1, 0, 2, 3).reshape(2, nz * t, heads_here, HEAD)
        )
    query, key, value = projected
    attended, probs = zip(
        *[attention(query[r], key[r], value[r], lengths_both[r]) for r in range(2)], strict=True
    )
    mine = attended[0].reshape(nz, t, feats)
    other = swap(attended[1].reshape(nz, t, feats), "c")
    mixed = lax.all_to_all(core_order(mine, other, 2), "z", 0, 0, tiled=True)
    attended_b = mixed.transpose(1, 2, 0, 3).reshape(t, width)

    middle = inputs + dot(attended_b, w_out_all)
    normed_ffn, inverse_ffn = rms_parts(middle)
    normed_ffn_b = (normed_ffn * norm_ffn).astype(bf16)

    ffn_in = [part.reshape(2 * t, width) for part in ring_gather(normed_ffn_b)]
    hidden, grad_gate, grad_up, out_parts, grad_parts = [], [], [], [], []
    for k in range(nz):
        gate = dot(ffn_in[k], w_gate_here)
        up = dot(ffn_in[k], w_up_here)
        sig = jax.nn.sigmoid(gate)
        silu = gate * sig
        hidden_k = (silu * up).astype(bf16)
        grad_hidden = dot_nt(cot[k], w_down_here)
        grad_gate_k = (grad_hidden * up * sig * (1.0 + gate * (1.0 - sig))).astype(bf16)
        grad_up_k = (grad_hidden * silu).astype(bf16)
        hidden.append(hidden_k)
        grad_gate.append(grad_gate_k)
        grad_up.append(grad_up_k)
        out_parts.append(dot(hidden_k, w_down_here).reshape(2, t, width))
        grad_parts.append(
            (dot_nt(grad_gate_k, w_gate_here) + dot_nt(grad_up_k, w_up_here)).reshape(2, t, width)
        )
    grad_normed_ffn = ring_scatter(grad_parts)
    back_ffn, gain_ffn_part = norm_back(grad_normed_ffn, norm_ffn, normed_ffn, inverse_ffn)
    grad_middle = cotangent.astype(f32) + back_ffn
    grad_branch_b = grad_middle.astype(bf16)

    grad_att = dot_nt(grad_branch_b, w_out_all).astype(bf16).reshape(t, 2, nz, feats)
    grad_att = lax.all_to_all(grad_att.transpose(2, 1, 0, 3), "z", 0, 0, tiled=True)
    me = lax.axis_index("c")
    grad_own = lax.dynamic_index_in_dim(grad_att, me, 1, keepdims=False)
    grad_other = swap(lax.dynamic_index_in_dim(grad_att, 1 - me, 1, keepdims=False), "c")
    grad_rows = [
        part.reshape(nz * t, heads_here, HEAD) for part in (grad_own, grad_other)
    ]
    grads = [
        attention_back(query[r], key[r], value[r], probs[r], grad_rows[r]) for r in range(2)
    ]
    grad_qkv = [
        jnp.stack([grads[r][i].reshape(nz, t, feats) for r in range(2)], axis=1)
        for i in range(3)
    ]
    grad_qkv = [
        [
            lax.dynamic_index_in_dim(part, sources[k], 0, keepdims=False).reshape(2 * t, feats)
            for k in range(nz)
        ]
        for part in grad_qkv
    ]
    grad_normed_attn = ring_scatter(
        [
            sum(dot_nt(grad_qkv[i][k], w_qkv[i]) for i in range(3)).reshape(2, t, width)
            for k in range(nz)
        ]
    )
    back_attn, gain_attn_part = norm_back(grad_normed_attn, norm_attn, normed_attn, inverse_attn)
    token_grad = grad_middle + back_attn
    gains = butterfly(jnp.stack([gain_attn_part, gain_ffn_part]))

    activations = (middle + ring_scatter(out_parts)).astype(bf16)

    cot_all = jnp.concatenate(cot)
    ffn_all = jnp.concatenate(ffn_in)
    attn_all = jnp.concatenate(attn_in)
    grad_w_down = scatter_plane(dot_tn(jnp.concatenate(hidden), cot_all).reshape(plane, block, width))

    grad_w_out = dot_tn(attended_b, grad_branch_b).reshape(plane, 2, nz * own_rows, width)
    grad_w_out = grad_w_out.transpose(1, 0, 2, 3)
    grad_w_out = scatter_plane(scatter_axis(grad_w_out, "c")).reshape(nz, own_rows, width)
    total = lax.dynamic_index_in_dim(grad_w_out, sources[1 % nz], 0, keepdims=False)
    for s in range(nz - 1):
        total = hop(total.astype(bf16)).astype(f32) + lax.dynamic_index_in_dim(
            grad_w_out, sources[(s + 2) % nz], 0, keepdims=False
        )
    grad_w_out = total

    def columns_home(parts, wide):
        parts = jnp.stack(
            [part.reshape(plane, 2, nz, own_rows, wide) for part in parts], axis=3
        )
        parts = scatter_plane(parts).astype(bf16)
        return exchange(parts)

    grad_gu = columns_home(
        [dot_tn(ffn_all, jnp.concatenate(grad_gate)), dot_tn(ffn_all, jnp.concatenate(grad_up))],
        units,
    ).reshape(2, nz, 2, own_rows, plane, block)
    grad_gu = grad_gu.transpose(2, 3, 4, 0, 1, 5).reshape(2, own_rows, hidden_width).astype(f32)
    grad_three = columns_home(
        [dot_tn(attn_all, jnp.concatenate(grad_qkv[i])) for i in range(3)], feats
    )
    grad_three = grad_three.transpose(2, 3, 0, 1, 4).reshape(3, own_rows, width).astype(f32)
    return (
        activations,
        token_grad,
        gains[0],
        grad_three[0],
        grad_three[1],
        grad_three[2],
        grad_w_out,
        gains[1],
        grad_gu[0],
        grad_gu[1],
        grad_w_down,
    )


def solution(mesh):
    dp, seq = mesh.shape["dp"], mesh.shape["seq"]
    grid = Mesh(mesh.devices.reshape(dp // 4, 2, 2, seq), ALL)
    split = P(ALL, None)
    return jax.shard_map(
        body,
        mesh=grid,
        in_specs=(split, split, P(("y", "x", "c"), None), P())
        + (split,) * 4
        + (P(),)
        + (split,) * 3,
        out_specs=(split, split, P(), split, split, split, split, P(), split, split, split),
        check_vma=False,
    )
```

time: 5230 us -> 786 us (0.15)
  waiting for transfers between devices: 4920 us -> 296 us
  local copies, waits for them, and re-layouts: 14.2 us -> 117 us
  matrix products: 211 us -> 118 us
  other arithmetic: 9.05 us -> 77.5 us
  starting transfers between devices: 10.6 us -> 74.6 us
    reduce_scatter x2 -> x0, waiting for transfers between devices: 4220 us -> none  [the longest x1 3250 us: body(): lax.psum_scatter(jnp.concatenate([row_gradient(normed_attn_b, grad_query_...]
    all_gather x7 -> x4, waiting for transfers between devices: 693 us -> 65.1 us  [the longest x3 65.1 us: gather_plane(): return lax.all_gather(x, ('y', 'x'), axis=0, tiled=False)]
    ppermute x4 -> x74, waiting for transfers between devices: 3.64 us -> 224 us  [the longest x21 129 us: hop(): return lax.ppermute(x, 'z', ring_pairs(lax.axis_size('z')))]
    dot_general x27 -> x69, matrix products: 211 us -> 118 us  [the longest x57 96.4 us: dot(): lax.dot_general(left, right, (dims, ((), ())), preferred_element_type=f32)]
    all_to_all x0 -> x2, blocking collectives: none -> 67.5 us  [exchange(): return jnp.swapaxes(lax.all_to_all(both, 'z', 0, 0, tiled=True), 0, 1)]
  transfers between devices with their start and end apart: 13 -> 82, of which waited for: 10 -> 34; matrix products, arithmetic and copies ran while one was open for 2% -> 38% of each run, Pallas kernels for 0% -> 0%
where the time goes in v1:
time: 786 us; the launch traced here: 776 us
  waiting for transfers between devices  296 us (38%)
  matrix products  118 us (15%)
  local copies, waits for them, and re-layouts  117 us (15%)
  other arithmetic  77.5 us (10%)
  starting transfers between devices  74.6 us (9%)
  blocking collectives  67.5 us (9%)
  between operations  25 us (3%)
    ppermute x21, waiting for transfers between devices, hop(): return lax.ppermute(x, 'z', ring_pairs(lax.axis_size('z')))  129 us
    dot_general x57, matrix products, dot(): lax.dot_general(left, right, (dims, ((), ())), preferred_element_type=f32)  96.4 us
    ppermute x48, waiting for transfers between devices, swap(): return lax.ppermute(x, axis, [(0, 1), (1, 0)])  80.9 us
    all_to_all x2, blocking collectives, exchange(): return jnp.swapaxes(lax.all_to_all(both, 'z', 0, 0, tiled=True), 0, 1)  67.5 us
    all_gather x3, waiting for transfers between devices, gather_plane(): return lax.all_gather(x, ('y', 'x'), axis=0, tiled=False)  65.1 us
    ppermute x21, starting transfers between devices, hop(): return lax.ppermute(x, 'z', ring_pairs(lax.axis_size('z')))  24.3 us
    ppermute x48, starting transfers between devices, swap(): return lax.ppermute(x, axis, [(0, 1), (1, 0)])  23.9 us
    another operation x14, other arithmetic, both_cores(): return jnp.stack([x, swap(x, 'c')])  18.4 us
  transfers between devices with their start and end apart: 82, of which 34 were waited for; matrix products, arithmetic and copies ran while one was open for 38% of the time, Pallas kernels for 0%

profile of v1, /device:TPU:0, one launch (start us, length us, event | category | flops | bytes accessed | tf_op | source)
XLA Modules:
  0.0 775.5 jit_solution(9494916888970027262)
XLA Ops:
  14.1 26.6 %all_to_all.30 = bf16[4,2,3,64,256]{4,3,2,1,0:T(8,128)(2,1)S(1)} all-to-all(bf16[4,2,3,64,256]{4,3,2,1,0:T(8,128)(2,1)S(1)} %copy.287), channel_id=1, replica_groups=mesh['y'=2,'x'=2,'c'=2,'z'=4] {'z'}, dimensions={0} | all-to-all | bytes 1572864 | tf_op jit(solution)/shard_map/all_to_all | solution.py:120
  59.2 40.9 %all_to_all.31 = bf16[4,2,2,64,704]{4,3,2,1,0:T(8,128)(2,1)} all-to-all(bf16[4,2,2,64,704]{4,3,2,1,0:T(8,128)(2,1)S(1)} %copy.321), channel_id=1, replica_groups=mesh['y'=2,'x'=2,'c'=2,'z'=4] {'z'}, dimensions={0} | all-to-all | bytes 2883584 | tf_op jit(solution)/shard_map/all_to_all | solution.py:120
  112.4 7.1 collective-permute-done.2
  119.7 21.9 %collective-permute-done.25 = bf16[128,2048]{1,0:T(8,128)(2,1)S(1)} collective-permute-done((bf16[128,2048]{1,0:T(8,128)(2,1)S(1)}, bf16[128,2048]{1,0:T(8,128)(2,1)S(1)}, u32[]{:S(2)}, u32[]{:S(2)}) %collective-permute-start.25) | collective-permute-done | bytes 524320 | tf_op jit(solution)/shard_map/ppermute | solution.py:46
  142.3 10.7 %collective-permute-done.4 = bf16[128,2048]{1,0:T(8,128)(2,1)} collective-permute-done((bf16[128,2048]{1,0:T(8,128)(2,1)}, bf16[128,2048]{1,0:T(8,128)(2,1)}, u32[]{:S(2)}, u32[]{:S(2)}) %collective-permute-start.4) | collective-permute-done | bytes 524320 | tf_op jit(solution)/shard_map/ppermute | solution.py:46
  153.8 10.4 %collective-permute-done.29 = bf16[128,2048]{1,0:T(8,128)(2,1)} collective-permute-done((bf16[128,2048]{1,0:T(8,128)(2,1)S(1)}, bf16[128,2048]{1,0:T(8,128)(2,1)}, u32[]{:S(2)}, u32[]{:S(2)}) %collective-permute-start.29) | collective-permute-done | bytes 524320 | tf_op jit(solution)/shard_map/ppermute | solution.py:46
  165.1 10.4 %collective-permute-done.6 = bf16[128,2048]{1,0:T(8,128)(2,1)} collective-permute-done((bf16[128,2048]{1,0:T(8,128)(2,1)}, bf16[128,2048]{1,0:T(8,128)(2,1)}, u32[]{:S(2)}, u32[]{:S(2)}) %collective-permute-start.6) | collective-permute-done | bytes 524320 | tf_op jit(solution)/shard_map/ppermute | solution.py:46
  178.7 7.8 %collective-permute-done.33 = bf16[128,2048]{1,0:T(8,128)(2,1)} collective-permute-done((bf16[128,2048]{1,0:T(8,128)(2,1)}, bf16[128,2048]{1,0:T(8,128)(2,1)}, u32[]{:S(2)}, u32[]{:S(2)}) %collective-permute-start.33) | collective-permute-done | bytes 524320 | tf_op jit(solution)/shard_map/ppermute | solution.py:46
  244.0 5.9 all-to-all-done.1
  250.3 4.9 multiply_reduce_fusion.2
  257.1 32.9 %all-gather.12.cloned.1.call-done = bf16[8,2,4,64,704]{4,3,0,1,2:T(8,128)(2,1)} async-done(((bf16[2,2,4,64,704]{4,3,0,1,2:T(8,128)(2,1)}), bf16[8,2,4,64,704]{4,3,0,1,2:T(8,128)(2,1)}) %all-gather.12.cloned.1.call-update) | async-done | bytes 5767184 | tf_op jit(solution)/shard_map/all_gather | solution.py:92
  301.3 32.2 %all-gather.14.cloned.1.call-done = bf16[704,2048]{1,0:T(8,128)(2,1)} async-done(((bf16[176,2048]{1,0:T(8,128)(2,1)}), bf16[704,2048]{1,0:T(8,128)(2,1)}) %all-gather.14.cloned.1.call-update) | async-done | bytes 2883600 | tf_op jit(solution)/shard_map/all_gather | solution.py:92
  350.6 7.2 collective-permute-done.15
  384.8 5.6 fusion.8
  390.5 5.0 fusion.27
  411.4 5.6 fusion.35
  432.3 9.1 %collective-permute-done.72 = bf16[2,176,1024]{2,1,0:T(8,128)(2,1)S(1)} collective-permute-done((bf16[2,176,1024]{2,1,0:T(8,128)(2,1)S(1)}, bf16[2,176,1024]{2,1,0:T(8,128)(2,1)S(1)}, u32[]{:S(2)}, u32[]{:S(2)}) %collective-permute-start.72) | collective-permute-done | bytes 720928 | tf_op jit(solution)/shard_map/ppermute | solution.py:33
  442.8 6.4 collective-permute-done.70
  452.4 4.8 collective-permute-done.36
  459.8 7.0 collective-permute-done.22
  481.4 8.1 %fusion.143 = f32[4,2,256,2048]{3,2,1,0:T(8,128)} fusion(bf16[4,2,256,128]{3,2,1,0:T(8,128)(2,1)S(1)} %bitcast.550, f32[128,2048]{1,0:T(8,128)S(1)} %get-tuple-element.51), kind=kOutput, calls=%fused_computation.309 | convolution fusion | flops 1074003968 | bytes 18350080 | tf_op jit(solution)/shard_map/dot_general | solution.py:21
  489.5 6.1 fusion.2
  496.9 10.7 %collective-permute-done.71 = bf16[176,1024]{1,0:T(8,128)(2,1)} collective-permute-done((bf16[176,1024]{1,0:T(8,128)(2,1)}, bf16[176,1024]{1,0:T(8,128)(2,1)}, u32[]{:S(2)}, u32[]{:S(2)}) %collective-permute-start.71) | collective-permute-done | bytes 360480 | tf_op jit(solution)/shard_map/ppermute | solution.py:33
  598.7 7.2 collective-permute-done.53
  611.9 5.7 collective-permute-done.55
  618.4 5.2 collective-permute-done.45
  639.9 11.7 %collective-permute-done.50 = f32[2,2048]{1,0:T(2,128)S(1)} collective-permute-done((f32[2,2048]{1,0:T(2,128)S(1)}, f32[2,2048]{1,0:T(2,128)S(1)}, u32[]{:S(2)}, u32[]{:S(2)}) %collective-permute-start.50) | collective-permute-done | bytes 16416 | tf_op jit(solution)/shard_map/ppermute | solution.py:128
  651.6 4.7 collective-permute-start.51
  656.3 5.9 bitcast_add_fusion
  671.4 19.8 %collective-permute-done.60 = bf16[2,256,1024]{2,1,0:T(8,128)(2,1)S(1)} collective-permute-done((bf16[2,256,1024]{2,1,0:T(8,128)(2,1)S(1)}, bf16[2,256,1024]{2,1,0:T(8,128)(2,1)S(1)}, u32[]{:S(2)}, u32[]{:S(2)}) %collective-permute-start.60) | collective-permute-done | bytes 1048608 | tf_op jit(solution)/shard_map/ppermute | solution.py:33
  705.2 7.3 collective-permute-done.59
  721.1 19.2 %collective-permute-done.62 = bf16[64,2048]{1,0:T(8,128)(2,1)} collective-permute-done((bf16[64,2048]{1,0:T(8,128)(2,1)S(1)}, bf16[64,2048]{1,0:T(8,128)(2,1)}, u32[]{:S(2)}, u32[]{:S(2)}) %collective-permute-start.62) | collective-permute-done | bytes 262176 | tf_op jit(solution)/shard_map/ppermute | solution.py:46
  (704 shorter events, 376.4 us)
Async XLA Ops:
  7.2 183.6 %all-gather.10.cloned.1.call-start = ((), (), s32[]{:S(2)}) async-start(), calls=%async_computation.7 | async-start | bytes 3932160 | tf_op jit(solution)/shard_map/all_gather | solution.py:92
  41.6 208.6 %all-gather.8.cloned.1.call-start = ((), (), s32[]{:S(2)}) async-start(), calls=%async_computation.6 | async-start | bytes 8650752 | tf_op jit(solution)/shard_map/all_gather | solution.py:249
  42.4 247.6 %all-gather.12.cloned.1.call-start = ((), (), s32[]{:S(2)}) async-start(), calls=%async_computation.8 | async-start | bytes 7864320 | tf_op jit(solution)/shard_map/all_gather | solution.py:92
  100.1 233.4 %all-gather.14.cloned.1.call-start = ((), (), s32[]{:S(2)}) async-start(), calls=%async_computation.9 | async-start | bytes 3604480 | tf_op jit(solution)/shard_map/all_gather | solution.py:92
  100.6 64.5 %collective-permute-start = (bf16[128,2048]{1,0:T(8,128)(2,1)S(1)}, bf16[128,2048]{1,0:T(8,128)(2,1)S(1)}, u32[]{:S(2)}, u32[]{:S(2)}) collective-permute-start(bf16[128,2048]{1,0:T(8,128)(2,1)S(1)} %fusion.64), channel_id=1, source_target_pairs={{0,4},{4,0},{1,5},{5,1},{2,6},{6,2},{3,7},{7,3},{8,12},{12,8},{9,1... | collective-permute-start | bytes 1572872 | tf_op jit(solution)/shard_map/ppermute | solution.py:33
  101.2 40.5 %collective-permute-start.25 = (bf16[128,2048]{1,0:T(8,128)(2,1)S(1)}, bf16[128,2048]{1,0:T(8,128)(2,1)S(1)}, u32[]{:S(2)}, u32[]{:S(2)}) collective-permute-start(bf16[128,2048]{1,0:T(8,128)(2,1)S(1)} %copy-done.57), channel_id=1, source_target_pairs={{1,3},{3,2},{2,0},{0,1},{5,7},{7,6},{6,4},{4,5},{9,11},{11,10},{10... | collective-permute-start | bytes 1572872 | tf_op jit(solution)/shard_map/ppermute | solution.py:46
  119.4 33.5 %collective-permute-start.4 = (bf16[128,2048]{1,0:T(8,128)(2,1)}, bf16[128,2048]{1,0:T(8,128)(2,1)}, u32[]{:S(2)}, u32[]{:S(2)}) collective-permute-start(bf16[128,2048]{1,0:T(8,128)(2,1)} %collective-permute-done.2), channel_id=1, source_target_pairs={{1,3},{3,2},{2,0},{0,1},{5,7},{7,6},{6,4},{4,5},{9,11},{11,10},{10... | collective-permute-start | bytes 1572872 | tf_op jit(solution)/shard_map/ppermute | solution.py:46
  165.1 70.0 %collective-permute-start.37 = (bf16[128,2048]{1,0:T(8,128)(2,1)S(1)}, bf16[128,2048]{1,0:T(8,128)(2,1)}, u32[]{:S(2)}, u32[]{:S(2)}) collective-permute-start(bf16[128,2048]{1,0:T(8,128)(2,1)S(1)} %copy-done.57), channel_id=1, source_target_pairs={{0,4},{4,0},{1,5},{5,1},{2,6},{6,2},{3,7},{7,3},{8,12},{12,8},{9,1... | collective-permute-start | bytes 1572872 | tf_op jit(solution)/shard_map/ppermute | solution.py:33
  176.6 60.5 %collective-permute-start.26 = (bf16[128,2048]{1,0:T(8,128)(2,1)}, bf16[128,2048]{1,0:T(8,128)(2,1)}, u32[]{:S(2)}, u32[]{:S(2)}) collective-permute-start(bf16[128,2048]{1,0:T(8,128)(2,1)} %copy-done.84), channel_id=1, source_target_pairs={{0,4},{4,0},{1,5},{5,1},{2,6},{6,2},{3,7},{7,3},{8,12},{12,8},{9,1... | collective-permute-start | bytes 1572872 | tf_op jit(solution)/shard_map/ppermute | solution.py:33
  178.4 61.0 %collective-permute-start.30 = (bf16[128,2048]{1,0:T(8,128)(2,1)}, bf16[128,2048]{1,0:T(8,128)(2,1)}, u32[]{:S(2)}, u32[]{:S(2)}) collective-permute-start(bf16[128,2048]{1,0:T(8,128)(2,1)} %collective-permute-done.29), channel_id=1, source_target_pairs={{0,4},{4,0},{1,5},{5,1},{2,6},{6,2},{3,7},{7,3},{8,12},{12,8},{9,1... | collective-permute-start | bytes 1572872 | tf_op jit(solution)/shard_map/ppermute | solution.py:33
  186.5 55.2 %collective-permute-start.34 = (bf16[128,2048]{1,0:T(8,128)(2,1)}, bf16[128,2048]{1,0:T(8,128)(2,1)}, u32[]{:S(2)}, u32[]{:S(2)}) collective-permute-start(bf16[128,2048]{1,0:T(8,128)(2,1)} %collective-permute-done.33), channel_id=1, source_target_pairs={{0,4},{4,0},{1,5},{5,1},{2,6},{6,2},{3,7},{7,3},{8,12},{12,8},{9,1... | collective-permute-start | bytes 1572872 | tf_op jit(solution)/shard_map/ppermute | solution.py:33
  257.1 38.6 %collective-permute-start.23 = (bf16[128,2048]{1,0:T(8,128)(2,1)}, bf16[128,2048]{1,0:T(8,128)(2,1)}, u32[]{:S(2)}, u32[]{:S(2)}) collective-permute-start(bf16[128,2048]{1,0:T(8,128)(2,1)} %multiply_convert_fusion), channel_id=1, source_target_pairs={{0,4},{4,0},{1,5},{5,1},{2,6},{6,2},{3,7},{7,3},{8,12},{12,8},{9,1... | collective-permute-start | bytes 1572872 | tf_op jit(solution)/shard_map/ppermute | solution.py:33
  293.8 45.4 %collective-permute-start.10 = (bf16[128,2048]{1,0:T(8,128)(2,1)}, bf16[128,2048]{1,0:T(8,128)(2,1)}, u32[]{:S(2)}, u32[]{:S(2)}) collective-permute-start(bf16[128,2048]{1,0:T(8,128)(2,1)} %multiply_convert_fusion), channel_id=1, source_target_pairs={{1,3},{3,2},{2,0},{0,1},{5,7},{7,6},{6,4},{4,5},{9,11},{11,10},{10... | collective-permute-start | bytes 1572872 | tf_op jit(solution)/shard_map/ppermute | solution.py:46
  339.2 119.9 %collective-permute-start.24 = (bf16[128,2048]{1,0:T(8,128)(2,1)}, bf16[128,2048]{1,0:T(8,128)(2,1)}, u32[]{:S(2)}, u32[]{:S(2)}) collective-permute-start(bf16[128,2048]{1,0:T(8,128)(2,1)} %slice.587), channel_id=1, source_target_pairs={{0,4},{4,0},{1,5},{5,1},{2,6},{6,2},{3,7},{7,3},{8,12},{12,8},{9,1... | collective-permute-start | bytes 1572872 | tf_op jit(solution)/shard_map/ppermute | solution.py:33
  365.0 33.2 %collective-permute-start.14 = (bf16[128,2048]{1,0:T(8,128)(2,1)}, bf16[128,2048]{1,0:T(8,128)(2,1)S(1)}, u32[]{:S(2)}, u32[]{:S(2)}) collective-permute-start(bf16[128,2048]{1,0:T(8,128)(2,1)} %fusion.94), channel_id=1, source_target_pairs={{1,3},{3,2},{2,0},{0,1},{5,7},{7,6},{6,4},{4,5},{9,11},{11,10},{10... | collective-permute-start | bytes 1572872 | tf_op jit(solution)/shard_map/ppermute | solution.py:46
  371.4 26.9 %collective-permute-start.17 = (bf16[128,2048]{1,0:T(8,128)(2,1)}, bf16[128,2048]{1,0:T(8,128)(2,1)}, u32[]{:S(2)}, u32[]{:S(2)}) collective-permute-start(bf16[128,2048]{1,0:T(8,128)(2,1)} %slice.589), channel_id=1, source_target_pairs={{0,4},{4,0},{1,5},{5,1},{2,6},{6,2},{3,7},{7,3},{8,12},{12,8},{9,1... | collective-permute-start | bytes 1572872 | tf_op jit(solution)/shard_map/ppermute | solution.py:33
  372.3 32.7 %collective-permute-start.28 = (bf16[128,2048]{1,0:T(8,128)(2,1)}, bf16[128,2048]{1,0:T(8,128)(2,1)S(1)}, u32[]{:S(2)}, u32[]{:S(2)}) collective-permute-start(bf16[128,2048]{1,0:T(8,128)(2,1)} %fusion.86), channel_id=1, source_target_pairs={{1,3},{3,2},{2,0},{0,1},{5,7},{7,6},{6,4},{4,5},{9,11},{11,10},{10... | collective-permute-start | bytes 1572872 | tf_op jit(solution)/shard_map/ppermute | solution.py:46
  379.4 25.6 %collective-permute-start.31 = (bf16[128,2048]{1,0:T(8,128)(2,1)}, bf16[128,2048]{1,0:T(8,128)(2,1)}, u32[]{:S(2)}, u32[]{:S(2)}) collective-permute-start(bf16[128,2048]{1,0:T(8,128)(2,1)} %slice.585), channel_id=1, source_target_pairs={{0,4},{4,0},{1,5},{5,1},{2,6},{6,2},{3,7},{7,3},{8,12},{12,8},{9,1... | collective-permute-start | bytes 1572872 | tf_op jit(solution)/shard_map/ppermute | solution.py:33
  422.8 28.1 %collective-permute-start.38 = (bf16[128,2048]{1,0:T(8,128)(2,1)S(1)}, bf16[128,2048]{1,0:T(8,128)(2,1)S(1)}, u32[]{:S(2)}, u32[]{:S(2)}) collective-permute-start(bf16[128,2048]{1,0:T(8,128)(2,1)S(1)} %copy-done.83), channel_id=1, source_target_pairs={{0,4},{4,0},{1,5},{5,1},{2,6},{6,2},{3,7},{7,3},{8,12},{12,8},{9,1... | collective-permute-start | bytes 1572872 | tf_op jit(solution)/shard_map/ppermute | solution.py:33
  431.5 46.0 %collective-permute-start.65 = (bf16[2,2,4,2,64,256]{5,4,2,1,3,0:T(8,128)(2,1)}, bf16[2,2,4,2,64,256]{5,4,2,1,3,0:T(8,128)(2,1)}, u32[]{:S(2)}, u32[]{:S(2)}) collective-permute-start(bf16[2,2,4,2,64,256]{5,4,2,1,3,0:T(8,128)(2,1)} %fusion.74), channel_id=1, source_target_pairs={{0,16},{16,0},{1,17},{17,1},{2,18},{18,2},{3,19},{19,3},{4,20},{20... | collective-permute-start | bytes 3145736 | tf_op jit(solution)/shard_map/ppermute | solution.py:33
  450.9 63.7 %collective-permute-start.67 = (bf16[2,2,4,2,64,448]{5,4,2,1,0,3:T(8,128)(2,1)}, bf16[2,2,4,2,64,448]{5,4,2,1,0,3:T(8,128)(2,1)}, u32[]{:S(2)}, u32[]{:S(2)}) collective-permute-start(bf16[2,2,4,2,64,448]{5,4,2,1,0,3:T(8,128)(2,1)} %fusion.18), channel_id=1, source_target_pairs={{0,8},{8,0},{1,9},{9,1},{2,10},{10,2},{3,11},{11,3},{4,12},{12,4},... | collective-permute-start | bytes 5505032 | tf_op jit(solution)/shard_map/ppermute | solution.py:33
  457.2 38.4 %collective-permute-start.73 = (bf16[176,1024]{1,0:T(8,128)(2,1)}, bf16[176,1024]{1,0:T(8,128)(2,1)}, u32[]{:S(2)}, u32[]{:S(2)}) collective-permute-start(bf16[176,1024]{1,0:T(8,128)(2,1)} %fusion.156), channel_id=1, source_target_pairs={{0,16},{16,0},{1,17},{17,1},{2,18},{18,2},{3,19},{19,3},{4,20},{20... | collective-permute-start | bytes 1081352 | tf_op jit(solution)/shard_map/ppermute | solution.py:33
  459.1 48.4 %collective-permute-start.71 = (bf16[176,1024]{1,0:T(8,128)(2,1)}, bf16[176,1024]{1,0:T(8,128)(2,1)}, u32[]{:S(2)}, u32[]{:S(2)}) collective-permute-start(bf16[176,1024]{1,0:T(8,128)(2,1)} %fusion.155), channel_id=1, source_target_pairs={{0,8},{8,0},{1,9},{9,1},{2,10},{10,2},{3,11},{11,3},{4,12},{12,4},... | collective-permute-start | bytes 1081352 | tf_op jit(solution)/shard_map/ppermute | solution.py:33
  473.6 48.1 %all-to-all-start.3 = ((bf16[4,2,128,256]{3,2,1,0:T(8,128)(2,1)}), bf16[4,2,128,256]{3,2,1,0:T(8,128)(2,1)S(1)}, u32[]{:S(2)}, u32[]{:S(2)}) async-start(bf16[4,2,128,256]{3,2,1,0:T(8,128)(2,1)} %bitcast.464), calls=%async_computation.3 | async-start | bytes 1048576 | tf_op jit(solution)/shard_map/all_to_all | solution.py:305
  479.8 33.9 %collective-permute-start.66 = (bf16[2,4,2,64,256]{4,3,1,0,2:T(8,128)(2,1)S(1)}, bf16[2,4,2,64,256]{4,3,1,0,2:T(8,128)(2,1)S(1)}, u32[]{:S(2)}, u32[]{:S(2)}) collective-permute-start(bf16[2,4,2,64,256]{4,3,1,0,2:T(8,128)(2,1)S(1)} %fusion.114), channel_id=1, source_target_pairs={{0,8},{8,0},{1,9},{9,1},{2,10},{10,2},{3,11},{11,3},{4,12},{12,4},... | collective-permute-start | bytes 1572872 | tf_op jit(solution)/shard_map/ppermute | solution.py:33
  495.6 160.7 %collective-permute-start.57 = (bf16[4,256,2048]{2,1,0:T(8,128)(2,1)}, bf16[4,256,2048]{2,1,0:T(8,128)(2,1)}, u32[]{:S(2)}, u32[]{:S(2)}) collective-permute-start(bf16[4,256,2048]{2,1,0:T(8,128)(2,1)} %fusion.2), channel_id=1, source_target_pairs={{0,4},{4,0},{1,5},{5,1},{2,6},{6,2},{3,7},{7,3},{8,12},{12,8},{9,1... | collective-permute-start | bytes 12582920 | tf_op jit(solution)/shard_map/ppermute | solution.py:33
  520.2 59.4 %collective-permute-start.68 = (bf16[2,4,2,64,448]{4,3,1,0,2:T(8,128)(2,1)}, bf16[2,4,2,64,448]{4,3,1,0,2:T(8,128)(2,1)}, u32[]{:S(2)}, u32[]{:S(2)}) collective-permute-start(bf16[2,4,2,64,448]{4,3,1,0,2:T(8,128)(2,1)} %fusion.73), channel_id=1, source_target_pairs={{0,16},{16,0},{1,17},{17,1},{2,18},{18,2},{3,19},{19,3},{4,20},{20... | collective-permute-start | bytes 2752520 | tf_op jit(solution)/shard_map/ppermute | solution.py:33
  570.3 25.6 %collective-permute-start.54 = (bf16[2,2,4,3,64,128]{5,4,3,2,1,0:T(8,128)(2,1)S(1)}, bf16[2,2,4,3,64,128]{5,4,3,2,1,0:T(8,128)(2,1)S(1)}, u32[]{:S(2)}, u32[]{:S(2)}) collective-permute-start(bf16[2,2,4,3,64,128]{5,4,3,2,1,0:T(8,128)(2,1)S(1)} %fusion.97), channel_id=1, source_target_pairs={{0,8},{8,0},{1,9},{9,1},{2,10},{10,2},{3,11},{11,3},{4,12},{12,4},... | collective-permute-start | bytes 2359304 | tf_op jit(solution)/shard_map/ppermute | solution.py:33
  589.6 28.8 %collective-permute-start.46 = (bf16[128,2048]{1,0:T(8,128)(2,1)S(1)}, bf16[128,2048]{1,0:T(8,128)(2,1)S(1)}, u32[]{:S(2)}, u32[]{:S(2)}) collective-permute-start(bf16[128,2048]{1,0:T(8,128)(2,1)S(1)} %slice.579), channel_id=1, source_target_pairs={{0,4},{4,0},{1,5},{5,1},{2,6},{6,2},{3,7},{7,3},{8,12},{12,8},{9,1... | collective-permute-start | bytes 1572872 | tf_op jit(solution)/shard_map/ppermute | solution.py:33
  633.5 61.4 %all-to-all-start.4 = ((bf16[4,2,3,64,256]{4,3,2,1,0:T(8,128)(2,1)}), bf16[4,2,3,64,256]{4,3,2,1,0:T(8,128)(2,1)S(1)}, u32[]{:S(2)}, u32[]{:S(2)}) async-start(bf16[4,2,3,64,256]{4,3,2,1,0:T(8,128)(2,1)} %copy.343), calls=%async_computation.4 | async-start | bytes 1572864 | tf_op jit(solution)/shard_map/all_to_all | solution.py:120
  694.9 46.5 %all-to-all-start.5 = ((bf16[4,2,2,64,704]{4,3,2,1,0:T(8,128)(2,1)}), bf16[4,2,2,64,704]{4,3,2,1,0:T(8,128)(2,1)}, u32[]{:S(2)}, u32[]{:S(2)}) async-start(bf16[4,2,2,64,704]{4,3,2,1,0:T(8,128)(2,1)} %copy.352), calls=%async_computation.5 | async-start | bytes 3145728 | tf_op jit(solution)/shard_map/all_to_all | solution.py:120
  712.9 27.4 %collective-permute-start.62 = (bf16[64,2048]{1,0:T(8,128)(2,1)S(1)}, bf16[64,2048]{1,0:T(8,128)(2,1)}, u32[]{:S(2)}, u32[]{:S(2)}) collective-permute-start(bf16[64,2048]{1,0:T(8,128)(2,1)S(1)} %fusion.157), channel_id=1, source_target_pairs={{1,3},{3,2},{2,0},{0,1},{5,7},{7,6},{6,4},{4,5},{9,11},{11,10},{10... | collective-permute-start | bytes 786440 | tf_op jit(solution)/shard_map/ppermute | solution.py:46
  (172 other events, 1874.5 us)
Sparse Core Ops, SparseCore 0:
  41.7 43.0 all-gather.9
  87.8 131.5 all-gather.7
  221.2 68.7 all-gather.11
  291.7 41.7 all-gather.13

commit v2 on v1

v2 whole, which is shorter than its diff:
```python
import functools
import math

import jax
import jax.numpy as jnp
from jax import lax
from jax.experimental import pallas as pl
from jax.experimental.pallas import tpu as pltpu
from jax.sharding import Mesh
from jax.sharding import PartitionSpec as P

HEADS = 16
HEAD = 128
WINDOW = 64
BLOCK = 128

ALL = ("p", "c", "z")
norm_eps = 1e-05
masked_score = -1e30
f32 = jnp.float32
bf16 = jnp.bfloat16


def dot(left, right, dims=((1,), (0,))):
    return lax.dot_general(left, right, (dims, ((), ())), preferred_element_type=f32)


def dot_nt(left, right):
    return dot(left, right, ((1,), (1,)))


def dot_tn(left, right):
    return dot(left, right, ((0,), (0,)))


def cross(x, axis, by):
    n = lax.axis_size(axis)
    return lax.ppermute(x, axis, [(i, i ^ by) for i in range(n)])


def ring_order(n):
    return list(range(1, n, 2)) + list(range(n - 2, -1, -2)) if n > 1 else [0]


def hop(x):
    n = lax.axis_size("z")
    order = ring_order(n)
    return lax.ppermute(x, "z", [(order[i], order[(i + 1) % n]) for i in range(n)])


def ring_sources(n):
    order = ring_order(n)
    spot = {place: at for at, place in enumerate(order)}
    return [[order[(spot[z] - k) % n] for k in range(n)] for z in range(n)]


def placed(parts, sources):
    out = jnp.zeros((len(parts),) + parts[0].shape, parts[0].dtype)
    for k, part in enumerate(parts):
        out = lax.dynamic_update_slice(out, part[None], (sources[k],) + (0,) * part.ndim)
    return out.reshape((-1,) + parts[0].shape[1:])


def gather_rows(x):
    return lax.all_gather(x, ("c", "p"), axis=0, tiled=False)


def indexed(x, at, axis):
    return lax.dynamic_index_in_dim(x, at, axis, keepdims=False)


def after(x, *others):
    return lax.optimization_barrier((x, others))[0]


def blocks_in_order(x, order):
    wide = x.shape[1] // len(order)
    return jnp.concatenate([x[:, i * wide : (i + 1) * wide] for i in order], axis=1)


def regrouped(x, n):
    return blocks_in_order(x, [2 * i + c for c in range(2) for i in range(n)])


def ungrouped(x, n):
    return blocks_in_order(x, [c * n + i for i in range(n) for c in range(2)])


def tick(jobs, also=()):
    operands = lax.optimization_barrier([operand for _, operand in jobs])
    results = [job(operand) for (job, _), operand in zip(jobs, operands, strict=True)]
    return lax.optimization_barrier((results, also))


def crossing(axis, by):
    return lambda x: cross(x, axis, by)


def exchange(x):
    return lax.all_to_all(x, "z", 0, 0, tiled=True)


def half_rows(left, right, at):
    half = left.shape[1] // 2
    return dot_tn(lax.dynamic_slice_in_dim(left, at * half, half, 1), right)


def plus(kept, came):
    return kept.astype(f32) + came.astype(f32)


def plane_open(x):
    n, me = lax.axis_size("p"), lax.axis_index("p")
    if n != 4:
        x = x.reshape((n, -1) + x.shape[1:])
        sent = [indexed(x, me ^ by, 0) for by in range(1, n)]
        return [(crossing("p", by), sent[by - 1]) for by in range(1, n)], indexed(x, me, 0)
    half = x.shape[1] // 256 * 128
    x = x.reshape((2, 2, -1) + x.shape[1:])
    left, right = x[..., :half], x[..., half:]
    high, low = me // 2, me % 2
    return [
        (crossing("p", 2), indexed(left, 1 - high, 0)),
        (crossing("p", 1), indexed(right, 1 - low, 1)),
    ], (indexed(left, high, 0), indexed(right, low, 1))


def plane_turn(came, kept):
    n, me = lax.axis_size("p"), lax.axis_index("p")
    if n != 4:
        return [], sum(part.astype(f32) for part in [kept, *came])
    high, low = me // 2, me % 2
    left, right = (plus(keep, part).astype(bf16) for keep, part in zip(kept, came, strict=True))
    return [
        (crossing("p", 1), indexed(left, 1 - low, 0)),
        (crossing("p", 2), indexed(right, 1 - high, 0)),
    ], (indexed(left, low, 0), indexed(right, high, 0))


def plane_close(came, kept):
    if not came:
        return kept
    return jnp.concatenate([plus(keep, part) for keep, part in zip(kept, came, strict=True)], axis=-1)


def butterfly(x):
    for axis in ALL:
        step = 1
        while step < lax.axis_size(axis):
            x = x + cross(x, axis, step)
            step *= 2
    return x


def doc_number(positions, doc_ends):
    return jnp.sum((positions[:, None] >= doc_ends[None, :]).astype(jnp.int32), axis=1)


def allowed_pairs(at, low, count, docs_down_ref, docs_across_ref):
    query_at = at + lax.broadcasted_iota(jnp.int32, (BLOCK, count), 0)
    key_at = low + lax.broadcasted_iota(jnp.int32, (BLOCK, count), 1)
    same = docs_down_ref[at : at + BLOCK, :] == docs_across_ref[:, low : low + count]
    return (key_at <= query_at) & (key_at > query_at - WINDOW) & same


def softmax(query, key, allowed):
    scores = jnp.where(allowed, dot_nt(query, key) * (1.0 / math.sqrt(HEAD)), masked_score)
    exped = jnp.exp(scores - jnp.max(scores, axis=-1, keepdims=True))
    return exped / jnp.sum(exped, axis=-1, keepdims=True)


def attention_kernel(qkv_ref, docs_down_ref, docs_across_ref, out_ref):
    length, width = out_ref.shape
    for at in range(0, length, BLOCK):
        low = max(0, at - BLOCK)
        allowed = allowed_pairs(at, low, at + BLOCK - low, docs_down_ref, docs_across_ref)
        for h in range(0, width, HEAD):
            query = qkv_ref[at : at + BLOCK, h : h + HEAD]
            key = qkv_ref[low : at + BLOCK, width + h : width + h + HEAD]
            value = qkv_ref[low : at + BLOCK, 2 * width + h : 2 * width + h + HEAD]
            probs = softmax(query, key, allowed)
            out_ref[at : at + BLOCK, h : h + HEAD] = dot(probs.astype(bf16), value).astype(bf16)


def attention_back_kernel(qkv_ref, grad_ref, docs_down_ref, docs_across_ref, out_ref):
    length, width = grad_ref.shape
    scale = 1.0 / math.sqrt(HEAD)
    pending = {}
    for at in range(0, length, BLOCK):
        low = max(0, at - BLOCK)
        allowed = allowed_pairs(at, low, at + BLOCK - low, docs_down_ref, docs_across_ref)
        for h in range(0, width, HEAD):
            query = qkv_ref[at : at + BLOCK, h : h + HEAD]
            key = qkv_ref[low : at + BLOCK, width + h : width + h + HEAD]
            value = qkv_ref[low : at + BLOCK, 2 * width + h : 2 * width + h + HEAD]
            grad = grad_ref[at : at + BLOCK, h : h + HEAD]
            probs = softmax(query, key, allowed)
            grad_probs = dot_nt(grad, value)
            inner = jnp.sum(probs * grad_probs, axis=-1, keepdims=True)
            grad_scores = (probs * (grad_probs - inner)).astype(bf16)
            out_ref[at : at + BLOCK, h : h + HEAD] = (dot(grad_scores, key) * scale).astype(bf16)
            grad_key = dot_tn(grad_scores, query) * scale
            grad_value = dot_tn(probs.astype(bf16), grad)
            if at > 0:
                before_key, before_value = pending[h]
                out_ref[low:at, width + h : width + h + HEAD] = (
                    before_key + grad_key[:BLOCK]
                ).astype(bf16)
                out_ref[low:at, 2 * width + h : 2 * width + h + HEAD] = (
                    before_value + grad_value[:BLOCK]
                ).astype(bf16)
            pending[h] = (grad_key[at - low :], grad_value[at - low :])
    for h, (last_key, last_value) in pending.items():
        out_ref[length - BLOCK :, width + h : width + h + HEAD] = last_key.astype(bf16)
        out_ref[length - BLOCK :, 2 * width + h : 2 * width + h + HEAD] = last_value.astype(bf16)


def local_kernel(kernel, columns, flops, *args):
    length = args[0].shape[0]
    return pl.pallas_call(
        kernel,
        out_shape=jax.ShapeDtypeStruct((length, columns), bf16),
        in_specs=[pl.BlockSpec(memory_space=pltpu.VMEM)] * len(args),
        out_specs=pl.BlockSpec(memory_space=pltpu.VMEM),
        compiler_params=pltpu.CompilerParams(vmem_limit_bytes=40 * 1024 * 1024),
        cost_estimate=pl.CostEstimate(flops=flops, bytes_accessed=length * columns * 8, transcendentals=0),
    )(*args)


def block_map(n, nz):
    return [(j % nz, (j // nz % 2) * n + j // nz // 2) for j in range(2 * n * nz)]


def spread_kernel(places, x_ref, out_ref):
    wide = x_ref.shape[1] // len(places)
    for j, (z, k) in enumerate(places):
        out_ref[z, :, k * wide : (k + 1) * wide] = x_ref[:, j * wide : (j + 1) * wide]


def collect_kernel(places, x_ref, out_ref):
    wide = out_ref.shape[1] // len(places)
    for j, (z, k) in enumerate(places):
        out_ref[:, j * wide : (j + 1) * wide] = x_ref[z, :, k * wide : (k + 1) * wide].astype(f32)


def spread(x, n, nz):
    rows, wide = x.shape
    return pl.pallas_call(
        functools.partial(spread_kernel, block_map(n, nz)),
        out_shape=jax.ShapeDtypeStruct((nz, rows, wide // nz), x.dtype),
        name="spread_units",
    )(x)


def collect(x, n):
    nz, rows, wide = x.shape
    return pl.pallas_call(
        functools.partial(collect_kernel, block_map(n, nz)),
        out_shape=jax.ShapeDtypeStruct((rows, wide * nz), f32),
        name="collect_units",
    )(x)


def rms_parts(values):
    inverse = lax.rsqrt(jnp.mean(values * values, axis=1, keepdims=True) + norm_eps)
    return (values * inverse, inverse)


def norm_back(grad_normed, gain, normed, inverse):
    scaled = grad_normed * gain
    back = inverse * (scaled - normed * jnp.mean(scaled * normed, axis=1, keepdims=True))
    return (back, jnp.sum(grad_normed * normed, axis=0))


def body(
    tokens,
    cotangent,
    lengths,
    norm_attn,
    w_query,
    w_key,
    w_value,
    w_out,
    norm_ffn,
    w_gate,
    w_up,
    w_down,
):
    t, width = tokens.shape
    own_rows, hidden_width = w_gate.shape
    nz = lax.axis_size("z")
    groups = lax.axis_size("p") * 2
    sources = jnp.asarray(ring_sources(nz), jnp.int32)[lax.axis_index("z")]
    feats = width // nz
    block = hidden_width // (groups * nz)
    units = groups * block
    group_rows = nz * own_rows

    n = lax.axis_size("p")
    me, core = lax.axis_index("p"), lax.axis_index("c")
    hops = nz - 1

    inputs = tokens.astype(f32)
    normed_attn, inverse_attn = rms_parts(inputs)
    normed_attn_b = regrouped((normed_attn * norm_attn).astype(bf16), n)

    w_down_here = gather_rows(w_down).reshape(units, width)
    qkv = jnp.concatenate(
        [w.reshape(own_rows, nz, feats) for w in (w_query, w_key, w_value)], axis=2
    ).transpose(1, 0, 2)
    qkv = exchange(qkv)
    w_qkv = gather_rows(qkv).reshape(width, 3 * feats)

    attn_in, out_rows = [after(normed_attn_b, qkv)], [w_out]
    for k in range(hops):
        parts, w_down_here = tick([(hop, attn_in[-1]), (hop, out_rows[-1])], w_down_here)
        attn_in.append(parts[0])
        out_rows.append(parts[1])
    attn_in = placed(attn_in, sources)
    w_out_all = gather_rows(placed(out_rows, sources)).reshape(width, width)

    gate_up = jnp.concatenate([spread(w, n, nz) for w in (w_gate, w_up)], axis=2)
    gate_up = exchange(after(gate_up, attn_in))
    w_gate_up = gather_rows(gate_up).reshape(width, 2 * units)
    cot = [after(cotangent, gate_up)]

    docs = doc_number(jnp.arange(nz * t, dtype=jnp.int32), jnp.cumsum(lengths[0]))
    docs_down, docs_across = docs[:, None], docs[None, :]
    flops = 4 * nz * t * 2 * BLOCK * feats
    def cot_hop():
        return [(hop, cot[-1])] if len(cot) < nz else []

    three = dot(attn_in, w_qkv).astype(bf16)
    attended = local_kernel(attention_kernel, feats, flops, three, docs_down, docs_across)
    part, attended = tick(cot_hop(), attended)
    cot += part
    (attended,), _ = tick([(exchange, attended.reshape(nz, t, feats))])
    attended_b = regrouped(attended.transpose(1, 0, 2).reshape(t, width), n)
    middle = inputs + dot(attended_b, w_out_all)
    normed_ffn, inverse_ffn = rms_parts(middle)
    normed_ffn_b = regrouped((normed_ffn * norm_ffn).astype(bf16), n)
    part, normed_ffn_b = tick(cot_hop(), normed_ffn_b)
    cot += part

    ffn_in = [normed_ffn_b]
    for _ in range(hops):
        (part, *more), _ = tick([(hop, ffn_in[-1])] + cot_hop())
        ffn_in.append(part)
        cot += more

    def next_hop(total, partials, s, jobs=(), also=()):
        first = partials[1 % nz] if s == 0 else total
        (part, *rest), also = tick([(hop, first.astype(bf16)), *jobs], also)
        return part.astype(f32) + partials[(s + 2) % nz], rest, also

    def chunks(x):
        return [x[k * t : (k + 1) * t] for k in range(nz)]

    left, right = jnp.concatenate(ffn_in), jnp.concatenate(cot)
    both = dot(left, w_gate_up)
    gate, up = both[:, :units], both[:, units:]
    sig = jax.nn.sigmoid(gate)
    silu = gate * sig
    hidden = (silu * up).astype(bf16)
    grad_hidden = dot_nt(right, w_down_here)
    grad_gate_up = jnp.concatenate(
        [grad_hidden * up * sig * (1.0 + gate * (1.0 - sig)), grad_hidden * silu], axis=1
    ).astype(bf16)
    grad_parts = chunks(dot_nt(grad_gate_up, w_gate_up))

    gu_other = half_rows(left, grad_gate_up, 1 - core).astype(bf16)
    total, _, gu_other = next_hop(None, grad_parts, 0, (), gu_other)
    down = dot_tn(hidden, right).astype(bf16).reshape(2, n * block, width)
    down_own, down_other = indexed(down, core, 0), indexed(down, 1 - core, 0)
    total, (gu_other,), (down_own, down_other) = next_hop(
        total, grad_parts, 1, [(crossing("c", 1), gu_other)], (down_own, down_other)
    )
    gu = plus(half_rows(left, grad_gate_up, core), gu_other).astype(bf16)
    gate_jobs, gate_kept = plane_open(gu[:, :units])
    up_jobs, up_kept = plane_open(gu[:, units:])
    total, gate_came, up_jobs_sent = next_hop(
        total, grad_parts, 2, gate_jobs, [part for _, part in up_jobs]
    )
    up_jobs = [(job, part) for (job, _), part in zip(up_jobs, up_jobs_sent, strict=True)]
    for s in range(3, hops):
        total, _, _ = next_hop(total, grad_parts, s)
    gate_jobs, gate_kept = plane_turn(gate_came, gate_kept)
    grad_normed_ffn = ungrouped(total, n)
    back_ffn, gain_ffn_part = norm_back(grad_normed_ffn, norm_ffn, normed_ffn, inverse_ffn)
    grad_middle = cotangent.astype(f32) + back_ffn
    grad_branch_b = grad_middle.astype(bf16)
    grad_att = ungrouped(dot_nt(grad_branch_b, w_out_all).astype(bf16), n).reshape(t, nz, feats)
    grad_att = grad_att.transpose(1, 0, 2)
    out_other = half_rows(attended_b, grad_branch_b, 1 - core).astype(bf16)
    (grad_att, *up_came), out_other = tick([(exchange, grad_att), *up_jobs], out_other)
    up_jobs, up_kept = plane_turn(up_came, up_kept)
    out_parts = chunks(dot(hidden, w_down_here))
    grad_three = local_kernel(
        attention_back_kernel,
        3 * feats,
        3 * flops,
        three,
        grad_att.reshape(nz * t, feats),
        docs_down,
        docs_across,
    )
    attn_back = dot_nt(grad_three, w_qkv).reshape(nz, t, width)
    attn_back = [indexed(attn_back, sources[k], 0) for k in range(nz)]
    out_total, came, (grad_three, attn_back) = next_hop(
        None,
        out_parts,
        0,
        [(crossing("c", 1), out_other), (crossing("c", 1), down_other), *gate_jobs, *up_jobs],
        (grad_three, attn_back),
    )
    out_other, down_other, *came = came
    gate_came, up_came = came[: len(gate_jobs)], came[len(gate_jobs) :]
    grad_gate = plane_close(gate_came, gate_kept).astype(bf16).reshape(nz, own_rows, units)
    grad_up = plane_close(up_came, up_kept).astype(bf16).reshape(nz, own_rows, units)

    out_sum = plus(half_rows(attended_b, grad_branch_b, core), out_other).astype(bf16)
    down_sum = plus(down_own, down_other).astype(bf16)
    out_jobs, out_kept = plane_open(out_sum)
    qkv_other = half_rows(attn_in, grad_three, 1 - core).astype(bf16)
    total, _, qkv_other = next_hop(None, attn_back, 0, (), qkv_other)
    total, (qkv_other, *out_came), _ = next_hop(
        total, attn_back, 1, [(crossing("c", 1), qkv_other), *out_jobs]
    )
    qkv_sum = plus(half_rows(attn_in, grad_three, core), qkv_other).astype(bf16)
    out_jobs, out_kept = plane_turn(out_came, out_kept)
    total, out_came, (qkv_sum, down_sum) = next_hop(
        total, attn_back, 2, out_jobs, (qkv_sum, down_sum)
    )
    for s in range(3, hops):
        total, _, _ = next_hop(total, attn_back, s)
    grad_w_out = plane_close(out_came, out_kept).reshape(nz, own_rows, width)
    grad_w_out = [indexed(grad_w_out, sources[k], 0) for k in range(nz)]
    grad_normed_attn = ungrouped(total, n)
    back_attn, gain_attn_part = norm_back(grad_normed_attn, norm_attn, normed_attn, inverse_attn)
    token_grad = grad_middle + back_attn

    qkv_jobs, qkv_kept = plane_open(qkv_sum)
    down_jobs, down_kept = plane_open(down_sum)
    w_out_total, (grad_gate, *qkv_came), _ = next_hop(
        None, grad_w_out, 0, [(exchange, grad_gate), *qkv_jobs]
    )
    qkv_jobs, qkv_kept = plane_turn(qkv_came, qkv_kept)
    gains = butterfly(jnp.stack([gain_attn_part, gain_ffn_part]))
    w_out_total, (grad_up, *qkv_came), gains = next_hop(
        w_out_total, grad_w_out, 1, [(exchange, grad_up), *qkv_jobs], gains
    )
    grad_qkv = plane_close(qkv_came, qkv_kept).astype(bf16).reshape(nz, own_rows, 3 * feats)
    grad_w_gate = collect(grad_gate, n)
    w_out_total, (grad_qkv, *down_came), grad_w_gate = next_hop(
        w_out_total, grad_w_out, 2, [(exchange, grad_qkv), *down_jobs], grad_w_gate
    )
    down_jobs, down_kept = plane_turn(down_came, down_kept)
    grad_w_up = collect(grad_up, n)
    out_total, _, _ = next_hop(out_total, out_parts, 1, (), grad_w_up)
    out_total, down_came, _ = next_hop(out_total, out_parts, 2, down_jobs)
    for s in range(3, hops):
        w_out_total, _, _ = next_hop(w_out_total, grad_w_out, s)
        out_total, _, _ = next_hop(out_total, out_parts, s)
    grad_w_down = plane_close(down_came, down_kept)
    grad_w_out = w_out_total
    activations = (middle + out_total).astype(bf16)
    grad_w_query, grad_w_key, grad_w_value = (
        grad_qkv[:, :, i * feats : (i + 1) * feats]
        .transpose(1, 0, 2)
        .reshape(own_rows, width)
        .astype(f32)
        for i in range(3)
    )
    return (
        activations,
        token_grad,
        gains[0],
        grad_w_query,
        grad_w_key,
        grad_w_value,
        grad_w_out,
        gains[1],
        grad_w_gate,
        grad_w_up,
        grad_w_down,
    )


def solution(mesh):
    dp, seq = mesh.shape["dp"], mesh.shape["seq"]
    grid = Mesh(mesh.devices.reshape(dp // 2, 2, seq), ALL)
    split = P(ALL, None)
    return jax.shard_map(
        body,
        mesh=grid,
        in_specs=(split, split, P(("p", "c"), None), P())
        + (split,) * 4
        + (P(),)
        + (split,) * 3,
        out_specs=(split, split, P(), split, split, split, split, P(), split, split, split),
        check_vma=False,
    )
```

time: 786 us -> 593 us (0.75)
  waiting for transfers between devices: 296 us -> 197 us
  local copies, waits for them, and re-layouts: 117 us -> 60.5 us
  matrix products: 118 us -> 77.9 us
  Pallas kernels: 0 us -> 19.2 us
  other arithmetic: 77.5 us -> 59.2 us
  starting transfers between devices: 74.6 us -> 84.1 us
    all_gather x4, waiting for transfers between devices: 65.1 us -> 0.03 us  [gather_rows(): return lax.all_gather(x, ('c', 'p'), axis=0, tiled=False)]
    ppermute x74 -> x53, waiting for transfers between devices: 224 us -> 184 us  [the longest x24 133 us: hop(): lax.ppermute(x, 'z', [(order[i], order[(i + 1) % n]) for i in range(n)])]
    slice x44 -> x11, local copies, waits for them, and re-layouts: 33.4 us -> 7.4 us  [the longest x7 5.38 us: plane_open(): left, right = (x[..., :half], x[..., half:])]
    another operation x31 -> x7, other arithmetic: 26 us -> 3.55 us  [the longest x14 18.4 us: both_cores(): return jnp.stack([x, swap(x, 'c')])]
    dot_general x12 -> x0, matrix products: 21.7 us -> none  [the longest x2 8.85 us: attention_back(): jnp.einsum('bhqk,bqhd->bkhd', probs_b, grad_blocks, preferred_element_typ...]
    convert_element_type x34 -> x4, local copies, waits for them, and re-layouts: 23.2 us -> 3.24 us  [the longest x3 2.51 us: body(): grad_w_query, grad_w_key, grad_w_value = (grad_qkv[:, :, i * feats:(i + 1...]
    pallas_call x0 -> x6, Pallas kernels: none -> 19.2 us  [the longest x2 9.56 us: local_kernel(): pl.pallas_call(kernel, out_shape=jax.ShapeDtypeStruct((length, columns),...]
    another operation x24 -> x0, local copies, waits for them, and re-layouts: 18.9 us -> none  [the longest x4 7.23 us: body(): jnp.stack([w_gate, w_up]).reshape(2, own_rows, plane, 2, nz, block)]
  transfers between devices with their start and end apart: 82 -> 62, of which waited for: 34 -> 33; matrix products, arithmetic and copies ran while one was open for 38% -> 22% of each run, Pallas kernels for 0% -> 3%
where the time goes in v2:
time: 593 us; the launch traced here: 584 us
  waiting for transfers between devices  197 us (33%)
  starting transfers between devices  84.1 us (14%)
  matrix products  77.9 us (13%)
  blocking collectives  62.3 us (11%)
  local copies, waits for them, and re-layouts  60.5 us (10%)
  other arithmetic  59.2 us (10%)
  between operations  23.8 us (4%)
  Pallas kernels  19.2 us (3%)
    ppermute x24, waiting for transfers between devices, hop(): lax.ppermute(x, 'z', [(order[i], order[(i + 1) % n]) for i in range(n)])  133 us
    dot_general x15, matrix products, dot(): lax.dot_general(left, right, (dims, ((), ())), preferred_element_type=f32)  77.9 us
    all_to_all x2, blocking collectives, exchange(): return lax.all_to_all(x, 'z', 0, 0, tiled=True)  62.3 us
    ppermute x29, waiting for transfers between devices, cross(): return lax.ppermute(x, axis, [(i, i ^ by) for i in range(n)])  50.7 us
    ppermute x29, starting transfers between devices, cross(): return lax.ppermute(x, axis, [(i, i ^ by) for i in range(n)])  32.1 us
    ppermute x24, starting transfers between devices, hop(): lax.ppermute(x, 'z', [(order[i], order[(i + 1) % n]) for i in range(n)])  31.5 us
    all_to_all x5, starting transfers between devices, exchange(): return lax.all_to_all(x, 'z', 0, 0, tiled=True)  20.3 us
    unnamed x219, local copies, waits for them, and re-layouts  20.1 us
  transfers between devices with their start and end apart: 62, of which 33 were waited for; matrix products, arithmetic and copies ran while one was open for 22% of the time, Pallas kernels for 3%

profile of v2, /device:TPU:0, one launch (start us, length us, event | category | flops | bytes accessed | tf_op | source)
XLA Modules:
  0.0 583.9 jit_solution(4091932142329646111)
XLA Ops:
  11.9 26.5 %all_to_all.35 = bf16[4,64,1536]{2,1,0:T(8,128)(2,1)} all-to-all(bf16[4,64,1536]{2,1,0:T(8,128)(2,1)S(1)} %copy.69), channel_id=1, replica_groups=mesh['p'=4,'c'=2,'z'=4] {'z'}, dimensions={0} | all-to-all | bytes 1572864 | tf_op jit(solution)/shard_map/all_to_all | solution.py:100
  41.8 16.4 %collective-permute-done.1 = bf16[64,2048]{1,0:T(8,128)(2,1)} collective-permute-done((bf16[64,2048]{1,0:T(8,128)(2,1)S(1)}, bf16[64,2048]{1,0:T(8,128)(2,1)}, u32[]{:S(2)}, u32[]{:S(2)}) %collective-permute-start.1) | collective-permute-done | bytes 262176 | tf_op jit(solution)/shard_map/ppermute | solution.py:48
  69.5 7.1 %collective-permute-done.3 = bf16[64,2048]{1,0:T(8,128)(2,1)S(1)} collective-permute-done((bf16[64,2048]{1,0:T(8,128)(2,1)}, bf16[64,2048]{1,0:T(8,128)(2,1)S(1)}, u32[]{:S(2)}, u32[]{:S(2)}) %collective-permute-start.3) | collective-permute-done | bytes 262176 | tf_op jit(solution)/shard_map/ppermute | solution.py:48
  81.5 14.2 %collective-permute-done.5 = bf16[64,2048]{1,0:T(8,128)(2,1)S(1)} collective-permute-done((bf16[64,2048]{1,0:T(8,128)(2,1)S(1)}, bf16[64,2048]{1,0:T(8,128)(2,1)S(1)}, u32[]{:S(2)}, u32[]{:S(2)}) %collective-permute-start.5) | collective-permute-done | bytes 262176 | tf_op jit(solution)/shard_map/ppermute | solution.py:48
  108.5 35.8 %all_to_all.36 = bf16[4,64,2816]{2,1,0:T(8,128)(2,1)} all-to-all(bf16[4,64,2816]{2,1,0:T(8,128)(2,1)S(1)} %pad_maximum_fusion.3), channel_id=1, replica_groups=mesh['p'=4,'c'=2,'z'=4] {'z'}, dimensions={0} | all-to-all | bytes 2883584 | tf_op jit(solution)/shard_map/all_to_all | solution.py:100
  145.1 6.8 %convolution_convert_fusion.4.qkv_ref = bf16[512,1536]{1,0:T(8,128)(2,1)S(1)} fusion(bf16[512,2048]{1,0:T(8,128)(2,1)} %bitcast.9, bf16[2048,1536]{1,0:T(8,128)(2,1)} %bitcast.279), kind=kOutput, calls=%fused_computation.8 | convolution fusion | flops 3222011904 | bytes 9961472 | tf_op jit(solution)/shard_map/dot_general | solution.py:25
  164.1 12.5 %all-to-all-done.2 = bf16[4,128,512]{1,2,0:T(8,128)(2,1)S(1)} async-done(((bf16[4,128,512]{1,2,0:T(8,128)(2,1)}), bf16[4,128,512]{1,2,0:T(8,128)(2,1)S(1)}, u32[]{:S(2)}, u32[]{:S(2)}) %all-to-all-start.2) | async-done | bytes 524320 | tf_op jit(solution)/shard_map/all_to_all | solution.py:100
  177.5 4.9 multiply_reduce_fusion.2
  187.8 13.8 %collective-permute-done.8 = bf16[128,2048]{1,0:T(8,128)(2,1)} collective-permute-done((bf16[128,2048]{1,0:T(8,128)(2,1)S(1)}, bf16[128,2048]{1,0:T(8,128)(2,1)}, u32[]{:S(2)}, u32[]{:S(2)}) %collective-permute-start.8) | collective-permute-done | bytes 524320 | tf_op jit(solution)/shard_map/ppermute | solution.py:48
  201.7 8.1 %collective-permute-done.9 = bf16[128,2048]{1,0:T(8,128)(2,1)} collective-permute-done((bf16[128,2048]{1,0:T(8,128)(2,1)}, bf16[128,2048]{1,0:T(8,128)(2,1)}, u32[]{:S(2)}, u32[]{:S(2)}) %collective-permute-start.9) | collective-permute-done | bytes 524320 | tf_op jit(solution)/shard_map/ppermute | solution.py:48
  210.6 11.2 %collective-permute-done.10 = bf16[128,2048]{1,0:T(8,128)(2,1)} collective-permute-done((bf16[128,2048]{1,0:T(8,128)(2,1)}, bf16[128,2048]{1,0:T(8,128)(2,1)}, u32[]{:S(2)}, u32[]{:S(2)}) %collective-permute-start.10) | collective-permute-done | bytes 524320 | tf_op jit(solution)/shard_map/ppermute | solution.py:48
  227.8 5.4 collective-permute-done.11
  233.2 10.2 %fusion.58 = f32[512,2816]{1,0:T(8,128)S(1)} fusion(bf16[2048,2816]{1,0:T(8,128)(2,1)} %bitcast.275, bf16[128,2048]{1,0:T(8,128)(2,1)} %collective-permute-done.11, bf16[128,2048]{1,0:T(8,128)(2,1)} %collective-permute-done.10, bf16[128,2048]{1,0:T(8,128)(2,1)} %collective-permute-done.8, bf16[128,2048]{1,0:T(8,128)(2,1)} %copy-done.44), kind=kOutput, calls=%fused_computation.222 | convolution fusion | flops 5913968640 | bytes 19398656 | tf_op jit(solution)/shard_map/dot_general | solution.py:25
  243.4 9.4 %multiply_convert_fusion.1 = (bf16[512,1408]{1,0:T(8,128)(2,1)S(1)}, bf16[512,1408]{1,0:T(8,128)(2,1)}, bf16[512,1408]{1,0:T(8,128)(2,1)}) fusion(f32[512,2816]{1,0:T(8,128)S(1)} %fusion.58, bf16[512,2048]{1,0:T(8,128)(2,1)} %constant_dynamic-update-slice_fusion.24, bf16[1408,2048]{1,0:T(8,128)(2,1)} %all-gather.10.cloned.1.call-done), kind=kOutput, calls=%fused_computation.13 | convolution fusion | flops 2963603456 | bytes 17956864 | tf_op jit(solution)/shard_map/dot_general | solution.py:25
  252.9 8.0 %fusion.32 = f32[512,2048]{1,0:T(8,128)S(1)} fusion(bf16[2048,2816]{1,0:T(8,128)(2,1)S(1)} %bitcast.278, bf16[512,1408]{1,0:T(8,128)(2,1)} %get-tuple-element.254, bf16[512,1408]{1,0:T(8,128)(2,1)S(1)} %get-tuple-element.253), kind=kOutput, calls=%fused_computation.90 | convolution fusion | flops 5911347200 | bytes 18612224 | tf_op jit(solution)/shard_map/dot_general | solution.py:25
  264.5 5.2 convolution_convert_fusion.1
  274.5 5.2 convolution_convert_fusion
  283.2 6.1 %collective-permute-done.13 = bf16[128,2048]{1,0:T(8,128)(2,1)S(1)} collective-permute-done((bf16[128,2048]{1,0:T(8,128)(2,1)}, bf16[128,2048]{1,0:T(8,128)(2,1)S(1)}, u32[]{:S(2)}, u32[]{:S(2)}) %collective-permute-start.13) | collective-permute-done | bytes 524320 | tf_op jit(solution)/shard_map/ppermute | solution.py:48
  289.4 5.5 add_convert_fusion
  325.0 4.7 all-to-all-start.3
  359.6 7.0 %shard_map.213 = bf16[512,1536]{1,0:T(8,128)(2,1)S(1)} custom-call(bf16[512,1536]{1,0:T(8,128)(2,1)S(1)} %convolution_convert_fusion.4.qkv_ref, bf16[512,512]{1,0:T(8,128)(2,1)S(1)} %bitcast.224, s32[512,1]{1,0:T(8,128)S(1)} %copy.70.docs_down_ref, s32[1,512]{1,0:T(1,128)S(1)} %bitcast.229), custom_call_target="tpu_custom_call" | custom-call | flops 805306368 | bytes 6291456 | tf_op jit(solution)/shard_map/pallas_call | solution.py:220
  366.6 5.6 fusion.66
  377.1 7.3 %collective-permute-done.24 = bf16[256,768]{1,0:T(8,128)(2,1)S(1)} collective-permute-done((bf16[256,768]{1,0:T(8,128)(2,1)S(1)}, bf16[256,768]{1,0:T(8,128)(2,1)S(1)}, u32[]{:S(2)}, u32[]{:S(2)}) %collective-permute-start.24) | collective-permute-done | bytes 393248 | tf_op jit(solution)/shard_map/ppermute | solution.py:38
  384.3 6.6 %collective-permute-done.26 = bf16[256,768]{1,0:T(8,128)(2,1)S(1)} collective-permute-done((bf16[256,768]{1,0:T(8,128)(2,1)S(1)}, bf16[256,768]{1,0:T(8,128)(2,1)S(1)}, u32[]{:S(2)}, u32[]{:S(2)}) %collective-permute-start.26) | collective-permute-done | bytes 393248 | tf_op jit(solution)/shard_map/ppermute | solution.py:38
  393.5 5.9 %add_convert_fusion.1 = bf16[1024,2048]{1,0:T(8,128)(2,1)} fusion(f32[1024,2048]{1,0:T(8,128)S(1)} %fusion.42, bf16[1024,2048]{1,0:T(8,128)(2,1)} %collective-permute-done.21), kind=kLoop, calls=%fused_computation.1 | loop fusion | flops 6291456 | bytes 16777216 | tf_op jit(solution)/shard_map/convert_element_type | solution.py:421
  415.2 4.6 add_convert_fusion.3
  419.8 15.8 %collective-permute-done.29 = bf16[128,2048]{1,0:T(8,128)(2,1)S(1)} collective-permute-done((bf16[128,2048]{1,0:T(8,128)(2,1)S(1)}, bf16[128,2048]{1,0:T(8,128)(2,1)S(1)}, u32[]{:S(2)}, u32[]{:S(2)}) %collective-permute-start.29) | collective-permute-done | bytes 524320 | tf_op jit(solution)/shard_map/ppermute | solution.py:48
  444.0 7.1 %collective-permute-done.33 = bf16[128,2048]{1,0:T(8,128)(2,1)S(1)} collective-permute-done((bf16[128,2048]{1,0:T(8,128)(2,1)S(1)}, bf16[128,2048]{1,0:T(8,128)(2,1)S(1)}, u32[]{:S(2)}, u32[]{:S(2)}) %collective-permute-start.33) | collective-permute-done | bytes 524320 | tf_op jit(solution)/shard_map/ppermute | solution.py:48
  471.9 9.0 %collective-permute-done.42 = f32[2,2048]{1,0:T(2,128)S(1)} collective-permute-done((f32[2,2048]{1,0:T(2,128)S(1)}, f32[2,2048]{1,0:T(2,128)S(1)}, u32[]{:S(2)}, u32[]{:S(2)}) %collective-permute-start.42) | collective-permute-done | bytes 16416 | tf_op jit(solution)/shard_map/ppermute | solution.py:38
  506.1 7.7 %collective-permute-done.45 = f32[2,2048]{1,0:T(2,128)S(1)} collective-permute-done((f32[2,2048]{1,0:T(2,128)S(1)}, f32[2,2048]{1,0:T(2,128)S(1)}, u32[]{:S(2)}, u32[]{:S(2)}) %collective-permute-start.45) | collective-permute-done | bytes 16416 | tf_op jit(solution)/shard_map/ppermute | solution.py:38
  513.8 4.6 collective-permute-start.46
  544.0 10.7 %collective-permute-done.47 = bf16[64,2048]{1,0:T(8,128)(2,1)S(1)} collective-permute-done((bf16[64,2048]{1,0:T(8,128)(2,1)}, bf16[64,2048]{1,0:T(8,128)(2,1)S(1)}, u32[]{:S(2)}, u32[]{:S(2)}) %collective-permute-start.47) | collective-permute-done | bytes 262176 | tf_op jit(solution)/shard_map/ppermute | solution.py:48
  (465 shorter events, 250.8 us)
Async XLA Ops:
  7.2 51.0 %all-gather.10.cloned.1.call-start = ((), (), s32[]{:S(2)}) async-start(), calls=%async_computation.8 | async-start | bytes 6488064 | tf_op jit(solution)/shard_map/all_gather | solution.py:65
  7.9 137.1 %all-gather.12.cloned.1.call-start = ((), (), s32[]{:S(2)}) async-start(), calls=%async_computation.9 | async-start | bytes 7077888 | tf_op jit(solution)/shard_map/all_gather | solution.py:65
  38.4 138.4 %all-gather.8.cloned.1.call-start = ((), (), s32[]{:S(2)}) async-start(), calls=%async_computation.7 | async-start | bytes 9437184 | tf_op jit(solution)/shard_map/all_gather | solution.py:65
  39.0 19.2 %collective-permute-start = (bf16[128,2048]{1,0:T(8,128)(2,1)S(1)}, bf16[128,2048]{1,0:T(8,128)(2,1)S(1)}, u32[]{:S(2)}, u32[]{:S(2)}) collective-permute-start(bf16[128,2048]{1,0:T(8,128)(2,1)S(1)} %constant_dynamic-update-slice_fusion), channel_id=1, source_target_pairs={{1,3},{3,2},{2,0},{0,1},{5,7},{7,6},{6,4},{4,5},{9,11},{11,10},{10... | collective-permute-start | bytes 1572872 | tf_op jit(solution)/shard_map/ppermute | solution.py:48
  39.3 18.9 %collective-permute-start.1 = (bf16[64,2048]{1,0:T(8,128)(2,1)S(1)}, bf16[64,2048]{1,0:T(8,128)(2,1)}, u32[]{:S(2)}, u32[]{:S(2)}) collective-permute-start(bf16[64,2048]{1,0:T(8,128)(2,1)S(1)} %copy-done.62), channel_id=1, source_target_pairs={{1,3},{3,2},{2,0},{0,1},{5,7},{7,6},{6,4},{4,5},{9,11},{11,10},{10... | collective-permute-start | bytes 786440 | tf_op jit(solution)/shard_map/ppermute | solution.py:48
  58.2 18.3 %collective-permute-start.2 = (bf16[128,2048]{1,0:T(8,128)(2,1)S(1)}, bf16[128,2048]{1,0:T(8,128)(2,1)S(1)}, u32[]{:S(2)}, u32[]{:S(2)}) collective-permute-start(bf16[128,2048]{1,0:T(8,128)(2,1)S(1)} %collective-permute-done), channel_id=1, source_target_pairs={{1,3},{3,2},{2,0},{0,1},{5,7},{7,6},{6,4},{4,5},{9,11},{11,10},{10... | collective-permute-start | bytes 1572872 | tf_op jit(solution)/shard_map/ppermute | solution.py:48
  76.6 19.1 %collective-permute-start.4 = (bf16[128,2048]{1,0:T(8,128)(2,1)S(1)}, bf16[128,2048]{1,0:T(8,128)(2,1)S(1)}, u32[]{:S(2)}, u32[]{:S(2)}) collective-permute-start(bf16[128,2048]{1,0:T(8,128)(2,1)S(1)} %collective-permute-done.2), channel_id=1, source_target_pairs={{1,3},{3,2},{2,0},{0,1},{5,7},{7,6},{6,4},{4,5},{9,11},{11,10},{10... | collective-permute-start | bytes 1572872 | tf_op jit(solution)/shard_map/ppermute | solution.py:48
  78.1 17.5 %collective-permute-start.5 = (bf16[64,2048]{1,0:T(8,128)(2,1)S(1)}, bf16[64,2048]{1,0:T(8,128)(2,1)S(1)}, u32[]{:S(2)}, u32[]{:S(2)}) collective-permute-start(bf16[64,2048]{1,0:T(8,128)(2,1)S(1)} %collective-permute-done.3), channel_id=1, source_target_pairs={{1,3},{3,2},{2,0},{0,1},{5,7},{7,6},{6,4},{4,5},{9,11},{11,10},{10... | collective-permute-start | bytes 786440 | tf_op jit(solution)/shard_map/ppermute | solution.py:48
  97.5 135.7 %all-gather.14.cloned.1.call-start = ((), (), s32[]{:S(2)}) async-start(), calls=%async_computation.10 | async-start | bytes 12976128 | tf_op jit(solution)/shard_map/all_gather | solution.py:65
  158.6 18.0 %all-to-all-start.2 = ((bf16[4,128,512]{1,2,0:T(8,128)(2,1)}), bf16[4,128,512]{1,2,0:T(8,128)(2,1)S(1)}, u32[]{:S(2)}, u32[]{:S(2)}) async-start(bf16[4,128,512]{1,2,0:T(8,128)(2,1)} %copy.71), calls=%async_computation.2 | async-start | bytes 1048576 | tf_op jit(solution)/shard_map/all_to_all | solution.py:100
  162.1 23.7 %collective-permute-start.7 = (bf16[128,2048]{1,0:T(8,128)(2,1)}, bf16[128,2048]{1,0:T(8,128)(2,1)}, u32[]{:S(2)}, u32[]{:S(2)}) collective-permute-start(bf16[128,2048]{1,0:T(8,128)(2,1)} %collective-permute-done.6), channel_id=1, source_target_pairs={{1,3},{3,2},{2,0},{0,1},{5,7},{7,6},{6,4},{4,5},{9,11},{11,10},{10... | collective-permute-start | bytes 1572872 | tf_op jit(solution)/shard_map/ppermute | solution.py:48
  185.8 24.0 %collective-permute-start.9 = (bf16[128,2048]{1,0:T(8,128)(2,1)}, bf16[128,2048]{1,0:T(8,128)(2,1)}, u32[]{:S(2)}, u32[]{:S(2)}) collective-permute-start(bf16[128,2048]{1,0:T(8,128)(2,1)} %collective-permute-done.7), channel_id=1, source_target_pairs={{1,3},{3,2},{2,0},{0,1},{5,7},{7,6},{6,4},{4,5},{9,11},{11,10},{10... | collective-permute-start | bytes 1572872 | tf_op jit(solution)/shard_map/ppermute | solution.py:48
  300.8 18.6 %collective-permute-start.17 = (bf16[2,256,768]{2,1,0:T(8,128)(2,1)S(1)}, bf16[2,256,768]{2,1,0:T(8,128)(2,1)S(1)}, u32[]{:S(2)}, u32[]{:S(2)}) collective-permute-start(bf16[2,256,768]{2,1,0:T(8,128)(2,1)S(1)} %dynamic-slice_bitcast_fusion.11), channel_id=1, source_target_pairs={{0,8},{8,0},{16,24},{24,16},{1,9},{9,1},{17,25},{25,17},{2,10},{10... | collective-permute-start | bytes 2359304 | tf_op jit(solution)/shard_map/ppermute | solution.py:38
  325.0 19.6 %all-to-all-start.3 = ((bf16[4,128,512]{2,1,0:T(8,128)(2,1)}), bf16[4,128,512]{2,1,0:T(8,128)(2,1)S(1)}, u32[]{:S(2)}, u32[]{:S(2)}) async-start(bf16[4,128,512]{2,1,0:T(8,128)(2,1)} %bitcast.255), calls=%async_computation.3 | async-start | bytes 1048576 | tf_op jit(solution)/shard_map/all_to_all | solution.py:100
  330.7 17.4 %collective-permute-start.19 = (bf16[2,256,768]{2,1,0:T(8,128)(2,1)}, bf16[2,256,768]{2,1,0:T(8,128)(2,1)}, u32[]{:S(2)}, u32[]{:S(2)}) collective-permute-start(bf16[2,256,768]{2,1,0:T(8,128)(2,1)} %dynamic-slice_bitcast_fusion.10), channel_id=1, source_target_pairs={{0,8},{8,0},{16,24},{24,16},{1,9},{9,1},{17,25},{25,17},{2,10},{10... | collective-permute-start | bytes 2359304 | tf_op jit(solution)/shard_map/ppermute | solution.py:38
  353.1 38.7 %collective-permute-start.21 = (bf16[1024,2048]{1,0:T(8,128)(2,1)}, bf16[1024,2048]{1,0:T(8,128)(2,1)}, u32[]{:S(2)}, u32[]{:S(2)}) collective-permute-start(bf16[1024,2048]{1,0:T(8,128)(2,1)} %convolution_convert_fusion.3), channel_id=1, source_target_pairs={{0,4},{4,0},{1,5},{5,1},{2,6},{6,2},{3,7},{7,3},{8,12},{12,8},{9,1... | collective-permute-start | bytes 12582920 | tf_op jit(solution)/shard_map/ppermute | solution.py:38
  353.2 37.7 %collective-permute-start.22 = (bf16[704,2048]{1,0:T(8,128)(2,1)S(1)}, bf16[704,2048]{1,0:T(8,128)(2,1)}, u32[]{:S(2)}, u32[]{:S(2)}) collective-permute-start(bf16[704,2048]{1,0:T(8,128)(2,1)S(1)} %copy-done.33), channel_id=1, source_target_pairs={{0,4},{4,0},{1,5},{5,1},{2,6},{6,2},{3,7},{7,3},{8,12},{12,8},{9,1... | collective-permute-start | bytes 8650760 | tf_op jit(solution)/shard_map/ppermute | solution.py:38
  355.0 36.0 %collective-permute-start.20 = (bf16[128,2048]{1,0:T(8,128)(2,1)S(1)}, bf16[128,2048]{1,0:T(8,128)(2,1)S(1)}, u32[]{:S(2)}, u32[]{:S(2)}) collective-permute-start(bf16[128,2048]{1,0:T(8,128)(2,1)S(1)} %copy-done.48), channel_id=1, source_target_pairs={{1,3},{3,2},{2,0},{0,1},{5,7},{7,6},{6,4},{4,5},{9,11},{11,10},{10... | collective-permute-start | bytes 1572872 | tf_op jit(solution)/shard_map/ppermute | solution.py:48
  406.8 29.2 %collective-permute-start.30 = (bf16[1024,1536]{1,0:T(8,128)(2,1)S(1)}, bf16[1024,1536]{1,0:T(8,128)(2,1)S(1)}, u32[]{:S(2)}, u32[]{:S(2)}) collective-permute-start(bf16[1024,1536]{1,0:T(8,128)(2,1)S(1)} %convolution_convert_fusion.2), channel_id=1, source_target_pairs={{0,4},{4,0},{1,5},{5,1},{2,6},{6,2},{3,7},{7,3},{8,12},{12,8},{9,1... | collective-permute-start | bytes 9437192 | tf_op jit(solution)/shard_map/ppermute | solution.py:38
  409.1 128.3 %collective-permute-start.27 = (bf16[128,2048]{1,0:T(8,128)(2,1)}, bf16[128,2048]{1,0:T(8,128)(2,1)}, u32[]{:S(2)}, u32[]{:S(2)}) collective-permute-start(bf16[128,2048]{1,0:T(8,128)(2,1)} %fusion.25), channel_id=1, source_target_pairs={{1,3},{3,2},{2,0},{0,1},{5,7},{7,6},{6,4},{4,5},{9,11},{11,10},{10... | collective-permute-start | bytes 1572872 | tf_op jit(solution)/shard_map/ppermute | solution.py:48
  410.0 25.7 %collective-permute-start.31 = (bf16[2,256,1024]{2,1,0:T(8,128)(2,1)S(1)}, bf16[2,256,1024]{2,1,0:T(8,128)(2,1)S(1)}, u32[]{:S(2)}, u32[]{:S(2)}) collective-permute-start(bf16[2,256,1024]{2,1,0:T(8,128)(2,1)S(1)} %dynamic-slice_bitcast_fusion.3), channel_id=1, source_target_pairs={{0,16},{8,24},{16,0},{24,8},{1,17},{9,25},{17,1},{25,9},{2,18},{10... | collective-permute-start | bytes 3145736 | tf_op jit(solution)/shard_map/ppermute | solution.py:38
  411.0 24.9 %collective-permute-start.32 = (bf16[2,256,1024]{2,1,0:T(8,128)(2,1)S(1)}, bf16[2,256,1024]{2,1,0:T(8,128)(2,1)S(1)}, u32[]{:S(2)}, u32[]{:S(2)}) collective-permute-start(bf16[2,256,1024]{2,1,0:T(8,128)(2,1)S(1)} %dynamic-slice_bitcast_fusion.2), channel_id=1, source_target_pairs={{0,8},{8,0},{16,24},{24,16},{1,9},{9,1},{17,25},{25,17},{2,10},{10... | collective-permute-start | bytes 3145736 | tf_op jit(solution)/shard_map/ppermute | solution.py:38
  413.9 21.8 %collective-permute-start.29 = (bf16[128,2048]{1,0:T(8,128)(2,1)S(1)}, bf16[128,2048]{1,0:T(8,128)(2,1)S(1)}, u32[]{:S(2)}, u32[]{:S(2)}) collective-permute-start(bf16[128,2048]{1,0:T(8,128)(2,1)S(1)} %add_convert_fusion.5), channel_id=1, source_target_pairs={{1,3},{3,2},{2,0},{0,1},{5,7},{7,6},{6,4},{4,5},{9,11},{11,10},{10... | collective-permute-start | bytes 1572872 | tf_op jit(solution)/shard_map/ppermute | solution.py:48
  457.7 27.2 %all-to-all-start.4 = ((bf16[4,64,1408]{2,1,0:T(8,128)(2,1)}), bf16[4,64,1408]{2,1,0:T(8,128)(2,1)}, u32[]{:S(2)}, u32[]{:S(2)}) async-start(bf16[4,64,1408]{2,1,0:T(8,128)(2,1)} %pad_maximum_fusion.9), calls=%async_computation.4 | async-start | bytes 1441792 | tf_op jit(solution)/shard_map/all_to_all | solution.py:100
  462.0 22.9 %collective-permute-start.37 = (bf16[2,256,768]{2,1,0:T(8,128)(2,1)}, bf16[2,256,768]{2,1,0:T(8,128)(2,1)}, u32[]{:S(2)}, u32[]{:S(2)}) collective-permute-start(bf16[2,256,768]{2,1,0:T(8,128)(2,1)} %dynamic-slice_bitcast_fusion.9), channel_id=1, source_target_pairs={{0,16},{8,24},{16,0},{24,8},{1,17},{9,25},{17,1},{25,9},{2,18},{10... | collective-permute-start | bytes 2359304 | tf_op jit(solution)/shard_map/ppermute | solution.py:38
  463.4 21.4 %collective-permute-start.38 = (bf16[2,256,768]{2,1,0:T(8,128)(2,1)}, bf16[2,256,768]{2,1,0:T(8,128)(2,1)}, u32[]{:S(2)}, u32[]{:S(2)}) collective-permute-start(bf16[2,256,768]{2,1,0:T(8,128)(2,1)} %dynamic-slice_bitcast_fusion.8), channel_id=1, source_target_pairs={{0,8},{8,0},{16,24},{24,16},{1,9},{9,1},{17,25},{25,17},{2,10},{10... | collective-permute-start | bytes 2359304 | tf_op jit(solution)/shard_map/ppermute | solution.py:38
  480.9 17.8 %collective-permute-start.43 = (f32[2,2048]{1,0:T(2,128)S(1)}, f32[2,2048]{1,0:T(2,128)S(1)}, u32[]{:S(2)}, u32[]{:S(2)}) collective-permute-start(f32[2,2048]{1,0:T(2,128)S(1)} %fusion.57), channel_id=1, source_target_pairs={{0,16},{8,24},{16,0},{24,8},{1,17},{9,25},{17,1},{25,9},{2,18},{10... | collective-permute-start | bytes 49160 | tf_op jit(solution)/shard_map/ppermute | solution.py:38
  492.1 29.0 %all-to-all-start.5 = ((bf16[4,64,1408]{2,1,0:T(8,128)(2,1)}), bf16[4,64,1408]{2,1,0:T(8,128)(2,1)}, u32[]{:S(2)}, u32[]{:S(2)}) async-start(bf16[4,64,1408]{2,1,0:T(8,128)(2,1)} %pad_maximum_fusion.10), calls=%async_computation.5 | async-start | bytes 1441792 | tf_op jit(solution)/shard_map/all_to_all | solution.py:100
  498.8 22.2 %collective-permute-start.39 = (bf16[64,2048]{1,0:T(8,128)(2,1)}, bf16[64,2048]{1,0:T(8,128)(2,1)S(1)}, u32[]{:S(2)}, u32[]{:S(2)}) collective-permute-start(bf16[64,2048]{1,0:T(8,128)(2,1)} %fusion.40), channel_id=1, source_target_pairs={{1,3},{3,2},{2,0},{0,1},{5,7},{7,6},{6,4},{4,5},{9,11},{11,10},{10... | collective-permute-start | bytes 786440 | tf_op jit(solution)/shard_map/ppermute | solution.py:48
  500.9 20.2 %collective-permute-start.40 = (bf16[256,768]{1,0:T(8,128)(2,1)}, bf16[256,768]{1,0:T(8,128)(2,1)}, u32[]{:S(2)}, u32[]{:S(2)}) collective-permute-start(bf16[256,768]{1,0:T(8,128)(2,1)} %dynamic-slice_bitcast_fusion.19), channel_id=1, source_target_pairs={{0,8},{8,0},{16,24},{24,16},{1,9},{9,1},{17,25},{25,17},{2,10},{10... | collective-permute-start | bytes 1179656 | tf_op jit(solution)/shard_map/ppermute | solution.py:38
  502.6 18.4 %collective-permute-start.41 = (bf16[256,768]{1,0:T(8,128)(2,1)}, bf16[256,768]{1,0:T(8,128)(2,1)}, u32[]{:S(2)}, u32[]{:S(2)}) collective-permute-start(bf16[256,768]{1,0:T(8,128)(2,1)} %dynamic-slice_bitcast_fusion.18), channel_id=1, source_target_pairs={{0,16},{8,24},{16,0},{24,8},{1,17},{9,25},{17,1},{25,9},{2,18},{10... | collective-permute-start | bytes 1179656 | tf_op jit(solution)/shard_map/ppermute | solution.py:38
  526.2 30.6 %all-to-all-start.6 = ((bf16[4,64,1536]{2,1,0:T(8,128)(2,1)}), bf16[4,64,1536]{2,1,0:T(8,128)(2,1)S(1)}, u32[]{:S(2)}, u32[]{:S(2)}) async-start(bf16[4,64,1536]{2,1,0:T(8,128)(2,1)} %pad_maximum_fusion.8), calls=%async_computation.6 | async-start | bytes 1572864 | tf_op jit(solution)/shard_map/all_to_all | solution.py:100
  (117 other events, 1002.1 us)
Sparse Core Ops, SparseCore 0:
  9.9 46.0 all-gather.9
  57.8 45.5 all-gather.11
  105.8 54.3 all-gather.7
  162.0 67.6 all-gather.13

commit v3 on v2

v3 whole, which is shorter than its diff:
```python
import functools
import math

import jax
import jax.numpy as jnp
from jax import lax
from jax.experimental import pallas as pl
from jax.experimental.pallas import tpu as pltpu
from jax.sharding import Mesh
from jax.sharding import PartitionSpec as P

HEADS = 16
HEAD = 128
WINDOW = 64
BLOCK = 128
PARTS = 1

ALL = ("p", "c", "z")
norm_eps = 1e-05
masked_score = -1e30
f32 = jnp.float32
bf16 = jnp.bfloat16


def dot(left, right, dims=((1,), (0,))):
    return lax.dot_general(left, right, (dims, ((), ())), preferred_element_type=f32)


def dot_nt(left, right):
    return dot(left, right, ((1,), (1,)))


def dot_tn(left, right):
    return dot(left, right, ((0,), (0,)))


def cross(x, axis, by):
    n = lax.axis_size(axis)
    return lax.ppermute(x, axis, [(i, i ^ by) for i in range(n)])


def ring_order(n):
    return list(range(1, n, 2)) + list(range(n - 2, -1, -2)) if n > 1 else [0]


def hop(x):
    n = lax.axis_size("z")
    order = ring_order(n)
    return lax.ppermute(x, "z", [(order[i], order[(i + 1) % n]) for i in range(n)])


def ring_sources(n):
    order = ring_order(n)
    spot = {place: at for at, place in enumerate(order)}
    return [[order[(spot[z] - k) % n] for k in range(n)] for z in range(n)]


def placed(parts, sources):
    out = jnp.zeros((len(parts),) + parts[0].shape, parts[0].dtype)
    for k, part in enumerate(parts):
        out = lax.dynamic_update_slice(out, part[None], (sources[k],) + (0,) * part.ndim)
    return out.reshape((-1,) + parts[0].shape[1:])


def gather_rows(x):
    return lax.all_gather(x, ("c", "p"), axis=0, tiled=False)


def indexed(x, at, axis):
    return lax.dynamic_index_in_dim(x, at, axis, keepdims=False)


def after(x, *others):
    return lax.optimization_barrier((x, others))[0]


def blocks_in_order(x, order):
    wide = x.shape[1] // len(order)
    return jnp.concatenate([x[:, i * wide : (i + 1) * wide] for i in order], axis=1)


def regrouped(x, n):
    return blocks_in_order(x, [2 * i + c for c in range(2) for i in range(n)])


def ungrouped(x, n):
    return blocks_in_order(x, [c * n + i for i in range(n) for c in range(2)])


def tick(jobs, also=()):
    operands = lax.optimization_barrier([operand for _, operand in jobs])
    results = [job(operand) for (job, _), operand in zip(jobs, operands, strict=True)]
    return lax.optimization_barrier((results, also))


def crossing(axis, by):
    return lambda x: cross(x, axis, by)


def exchange(x):
    return lax.all_to_all(x, "z", 0, 0, tiled=True)


def plus(kept, came):
    return kept.astype(f32) + came.astype(f32)


class Line:
    def __init__(self):
        self.token = lax.optimization_barrier(jnp.zeros((8, 128), f32))

    def hold(self, *values):
        values, self.token = lax.optimization_barrier((values, self.token))
        return values[0] if len(values) == 1 else values

    def __call__(self, piece, *values):
        values, self.token = lax.optimization_barrier((values, self.token))
        return self.hold(piece(*values))


def plane_sent(parts, first, last):
    return [cross(parts[by - 1], "p", by) for by in range(first, last)]


def summed(*parts):
    return sum(part.astype(f32) for part in parts)


def spread_sums(x, axis):
    return [cross(x, axis, by) for by in range(1, lax.axis_size(axis))]


def paired_sum(parts):
    while len(parts) > 1:
        parts = [parts[i] + parts[i + 1] for i in range(0, len(parts), 2)]
    return parts[0]


def doc_number(positions, doc_ends):
    return jnp.sum((positions[:, None] >= doc_ends[None, :]).astype(jnp.int32), axis=1)


def allowed_pairs(at, low, count, docs_down_ref, docs_across_ref):
    query_at = at + lax.broadcasted_iota(jnp.int32, (BLOCK, count), 0)
    key_at = low + lax.broadcasted_iota(jnp.int32, (BLOCK, count), 1)
    same = docs_down_ref[at : at + BLOCK, :] == docs_across_ref[:, low : low + count]
    return (key_at <= query_at) & (key_at > query_at - WINDOW) & same


def softmax(query, key, allowed):
    scores = jnp.where(allowed, dot_nt(query, key) * (1.0 / math.sqrt(HEAD)), masked_score)
    exped = jnp.exp(scores - jnp.max(scores, axis=-1, keepdims=True))
    return exped / jnp.sum(exped, axis=-1, keepdims=True)


def attention_kernel(qkv_ref, docs_down_ref, docs_across_ref, out_ref):
    length, width = out_ref.shape
    for at in range(0, length, BLOCK):
        low = max(0, at - BLOCK)
        allowed = allowed_pairs(at, low, at + BLOCK - low, docs_down_ref, docs_across_ref)
        for h in range(0, width, HEAD):
            query = qkv_ref[at : at + BLOCK, h : h + HEAD]
            key = qkv_ref[low : at + BLOCK, width + h : width + h + HEAD]
            value = qkv_ref[low : at + BLOCK, 2 * width + h : 2 * width + h + HEAD]
            probs = softmax(query, key, allowed)
            out_ref[at : at + BLOCK, h : h + HEAD] = dot(probs.astype(bf16), value).astype(bf16)


def attention_back_kernel(qkv_ref, grad_ref, docs_down_ref, docs_across_ref, out_ref):
    length, width = grad_ref.shape
    scale = 1.0 / math.sqrt(HEAD)
    pending = {}
    for at in range(0, length, BLOCK):
        low = max(0, at - BLOCK)
        allowed = allowed_pairs(at, low, at + BLOCK - low, docs_down_ref, docs_across_ref)
        for h in range(0, width, HEAD):
            query = qkv_ref[at : at + BLOCK, h : h + HEAD]
            key = qkv_ref[low : at + BLOCK, width + h : width + h + HEAD]
            value = qkv_ref[low : at + BLOCK, 2 * width + h : 2 * width + h + HEAD]
            grad = grad_ref[at : at + BLOCK, h : h + HEAD]
            probs = softmax(query, key, allowed)
            grad_probs = dot_nt(grad, value)
            inner = jnp.sum(probs * grad_probs, axis=-1, keepdims=True)
            grad_scores = (probs * (grad_probs - inner)).astype(bf16)
            out_ref[at : at + BLOCK, h : h + HEAD] = (dot(grad_scores, key) * scale).astype(bf16)
            grad_key = dot_tn(grad_scores, query) * scale
            grad_value = dot_tn(probs.astype(bf16), grad)
            if at > 0:
                before_key, before_value = pending[h]
                out_ref[low:at, width + h : width + h + HEAD] = (
                    before_key + grad_key[:BLOCK]
                ).astype(bf16)
                out_ref[low:at, 2 * width + h : 2 * width + h + HEAD] = (
                    before_value + grad_value[:BLOCK]
                ).astype(bf16)
            pending[h] = (grad_key[at - low :], grad_value[at - low :])
    for h, (last_key, last_value) in pending.items():
        out_ref[length - BLOCK :, width + h : width + h + HEAD] = last_key.astype(bf16)
        out_ref[length - BLOCK :, 2 * width + h : 2 * width + h + HEAD] = last_value.astype(bf16)


def local_kernel(kernel, columns, *args):
    length = args[0].shape[0]
    return pl.pallas_call(
        kernel,
        out_shape=jax.ShapeDtypeStruct((length, columns), bf16),
        in_specs=[pl.BlockSpec(memory_space=pltpu.VMEM)] * len(args),
        out_specs=pl.BlockSpec(memory_space=pltpu.VMEM),
        compiler_params=kernel_params(10),
        cost_estimate=kernel_cost(5),
    )(*args)


def unit_pieces(n, nz, block, tile):
    pieces = []
    for j in range(2 * n * nz):
        start = ((j // nz % 2) * n + j // nz // 2) * block
        at = start
        while at < start + block:
            end = min(start + block, (at // tile + 1) * tile)
            column = at // tile * 2 * tile + at % tile
            pieces.append((j * block + at - start, j % nz, column, column + tile, end - at))
            at = end
    return pieces


def spread_kernel(pieces, gate_ref, up_ref, out_ref):
    for stored, z, gate_at, up_at, size in pieces:
        out_ref[z, :, gate_at : gate_at + size] = gate_ref[:, stored : stored + size]
        out_ref[z, :, up_at : up_at + size] = up_ref[:, stored : stored + size]


def collect_kernel(pieces, cut, first_ref, second_ref, gate_ref, up_ref):
    for stored, z, gate_at, up_at, size in pieces:
        for at, ref in ((gate_at, gate_ref), (up_at, up_ref)):
            inside = min(max(cut - at, 0), size)
            for source, low, start, count in (
                (first_ref, at, stored, inside),
                (second_ref, at + inside - cut, stored + inside, size - inside),
            ):
                if count:
                    ref[:, start : start + count] = source[z, :, low : low + count].astype(f32)


def spread(gate, up, nz, pieces):
    rows, wide = gate.shape
    return pl.pallas_call(
        functools.partial(spread_kernel, pieces),
        out_shape=jax.ShapeDtypeStruct((nz, rows, 2 * wide // nz), gate.dtype),
        name="spread_units",
    )(gate, up)


def collect(first, second, pieces):
    nz, rows, cut = first.shape
    wide = nz * (cut + second.shape[2]) // 2
    return pl.pallas_call(
        functools.partial(collect_kernel, pieces, cut),
        out_shape=[jax.ShapeDtypeStruct((rows, wide), f32)] * 2,
        name="collect_units",
    )(first, second)


def units_back(gate, up, grad_hidden):
    sig = jax.nn.sigmoid(gate)
    silu = gate * sig
    return (
        (silu * up).astype(bf16),
        (grad_hidden * up * sig * (1.0 + gate * (1.0 - sig))).astype(bf16),
        (grad_hidden * silu).astype(bf16),
    )


def feed_kernel(nz, places_ref, *refs):
    lefts, rights = refs[:nz], refs[nz : 2 * nz]
    gate_up_ref, down_ref, hidden_ref, grad_ref, left_ref, right_ref = refs[2 * nz :]
    t, tile = lefts[0].shape[0], down_ref.shape[0]

    @pl.when(pl.program_id(0) == 0)
    def _():
        for k in range(nz):
            start = pl.multiple_of(places_ref[k] * t, t)
            left_ref[pl.ds(start, t), :] = lefts[k][...]
            right_ref[pl.ds(start, t), :] = rights[k][...]

    both = dot(left_ref[...], gate_up_ref[...])
    grad_hidden = dot_nt(right_ref[...], down_ref[...])
    hidden, grad_gate, grad_up = units_back(both[:, :tile], both[:, tile:], grad_hidden)
    hidden_ref[...] = hidden
    grad_ref[:, :tile] = grad_gate
    grad_ref[:, tile:] = grad_up


def feed(lefts, rights, places, w_gate_up, w_down, tile):
    nz, (t, width) = len(lefts), lefts[0].shape
    units = w_down.shape[0]
    if tile != 128:
        left, right = placed(lefts, places), placed(rights, places)
        both = dot(left, w_gate_up)
        grad_hidden = dot_nt(right, w_down)
        hidden, grad_gate, grad_up = units_back(both[:, :units], both[:, units:], grad_hidden)
        return hidden, jnp.concatenate([grad_gate, grad_up], axis=1), left, right
    rows = nz * t
    whole = pl.BlockSpec((t, width), lambda i, at: (0, 0))
    every = pl.BlockSpec((rows, width), lambda i, at: (0, 0))
    return pl.pallas_call(
        functools.partial(feed_kernel, nz),
        grid_spec=pltpu.PrefetchScalarGridSpec(
            num_scalar_prefetch=1,
            grid=(units // tile,),
            in_specs=[whole] * (2 * nz)
            + [
                pl.BlockSpec((width, 2 * tile), lambda i, at: (0, i)),
                pl.BlockSpec((tile, width), lambda i, at: (i, 0)),
            ],
            out_specs=[
                pl.BlockSpec((rows, tile), lambda i, at: (0, i)),
                pl.BlockSpec((rows, 2 * tile), lambda i, at: (0, i)),
                every,
                every,
            ],
        ),
        out_shape=[
            jax.ShapeDtypeStruct((rows, units), bf16),
            jax.ShapeDtypeStruct((rows, 2 * units), bf16),
            jax.ShapeDtypeStruct((rows, width), bf16),
            jax.ShapeDtypeStruct((rows, width), bf16),
        ],
        compiler_params=kernel_params(60),
        cost_estimate=kernel_cost(18),
        name="feed_units",
    )(places, *lefts, *rights, w_gate_up, w_down)


def kernel_cost(us):
    return pl.CostEstimate(flops=int(us * 1.15e9 * 0.5), bytes_accessed=0, transcendentals=0)


def kernel_params(mib):
    return pltpu.CompilerParams(vmem_limit_bytes=mib * 1024 * 1024)


def tile_of(columns, most=1408):
    return max(tile for tile in range(128, most + 1, 128) if columns % tile == 0)


def rows_kernel(n, mode, at_ref, left_ref, right_ref, *refs):
    flip_ref, total_ref = refs[-2:]
    came, outs = (refs[:0], refs[:-2]) if mode == "other" else (refs[:PARTS], refs[PARTS:-2])

    @pl.when(pl.program_id(0) == 0)
    def _():
        flip_ref[...] = left_ref[...].T

    total = dot(flip_ref[...], right_ref[...])
    size = total.shape[0] // PARTS
    for k in range(PARTS):
        part = total[k * size : (k + 1) * size]
        if mode == "other":
            outs[k][...] = part.astype(bf16)
        else:
            part = (part + came[k][...].astype(f32)).astype(bf16)
            into = outs[0] if mode == "whole" else total_ref
            into[k * size : (k + 1) * size, :] = part
    if mode == "cut":
        rest = total.shape[0] // n
        for by in range(n):
            start = pl.multiple_of((at_ref[1] ^ by) * rest, rest)
            outs[by][...] = total_ref[pl.ds(start, rest), :]


def rows_product(left, right, half, me, n, mode, came=(), first=0, last=None):
    t, rows = left.shape[0], left.shape[1] // 2
    last = right.shape[1] if last is None else last
    tile = tile_of(math.gcd(last - first, first) if first else last)
    rest, columns, off = rows // n, last - first, first // tile
    at = jnp.stack([half, me]).astype(jnp.int32)
    outs, height = {"whole": (1, rows), "cut": (n, rest), "other": (PARTS, rows // PARTS)}[mode]
    return pl.pallas_call(
        functools.partial(rows_kernel, n, mode),
        grid_spec=pltpu.PrefetchScalarGridSpec(
            num_scalar_prefetch=1,
            grid=(columns // tile,),
            in_specs=[
                pl.BlockSpec((t, rows), lambda i, at: (0, at[0])),
                pl.BlockSpec((t, tile), lambda i, at: (0, i + off)),
            ]
            + [pl.BlockSpec((rows // PARTS, tile), lambda i, at: (0, i + off))] * len(came),
            out_specs=[pl.BlockSpec((height, tile), lambda i, at: (0, i))] * outs,
            scratch_shapes=[pltpu.VMEM((rows, t), bf16), pltpu.VMEM((rows, tile), bf16)],
        ),
        out_shape=[jax.ShapeDtypeStruct((height, columns), bf16)] * outs,
        compiler_params=kernel_params(60),
        cost_estimate=kernel_cost(6.5),
        name="rows_product",
    )(at, left, right, *came)


def down_kernel(n, at_ref, left_ref, right_ref, *refs):
    outs, flip_ref, total_ref = refs[:-2], refs[-2], refs[-1]
    rest = outs[0].shape[0]

    @pl.when(pl.program_id(0) == 0)
    def _():
        flip_ref[...] = left_ref[...].T

    total_ref[...] = dot(flip_ref[...], right_ref[...]).astype(bf16)
    for k, out_ref in enumerate(outs):
        half = at_ref[0] if k < n else 1 - at_ref[0]
        start = (half * n + (at_ref[1] ^ (k % n))) * rest
        out_ref[...] = total_ref[pl.ds(pl.multiple_of(start, math.gcd(rest, 16)), rest), :]


def down_product(left, right, core, me, n):
    t, rows = left.shape
    columns = right.shape[1]
    tile = tile_of(columns)
    rest = rows // (2 * n)
    if rest % 16:
        full = dot_tn(left, right).astype(bf16).reshape(2, n, rest, columns)
        parts = [indexed(indexed(full, at, 0), me ^ by, 0) for at in (core, 1 - core) for by in range(n)]
        return parts[:n], parts[n:]
    parts = pl.pallas_call(
        functools.partial(down_kernel, n),
        grid_spec=pltpu.PrefetchScalarGridSpec(
            num_scalar_prefetch=1,
            grid=(columns // tile,),
            in_specs=[
                pl.BlockSpec((t, rows), lambda i, at: (0, 0)),
                pl.BlockSpec((t, tile), lambda i, at: (0, i)),
            ],
            out_specs=[pl.BlockSpec((rest, tile), lambda i, at: (0, i))] * (2 * n),
            scratch_shapes=[pltpu.VMEM((rows, t), bf16), pltpu.VMEM((rows, tile), bf16)],
        ),
        out_shape=[jax.ShapeDtypeStruct((rest, columns), bf16)] * (2 * n),
        compiler_params=kernel_params(60),
        cost_estimate=kernel_cost(7),
        name="down_product",
    )(jnp.stack([core, me]).astype(jnp.int32), left, right)
    return parts[:n], parts[n:]


def chunks_kernel(transposed, at_ref, x_ref, w_ref, *refs):
    outs, total_ref = refs[:-1], refs[-1]
    t = outs[0].shape[0]
    total_ref[...] = (dot_nt if transposed else dot)(x_ref[...], w_ref[...])
    for k, out_ref in enumerate(outs):
        start = pl.multiple_of(at_ref[k] * t, t)
        out_ref[...] = total_ref[pl.ds(start, t), :].astype(out_ref.dtype)


def chunks_product(x, w, places, transposed):
    rows, depth = x.shape
    n, columns = places.shape[0], w.shape[0 if transposed else 1]
    tile = tile_of(columns)
    w_spec = (
        pl.BlockSpec((tile, depth), lambda i, at: (i, 0))
        if transposed
        else pl.BlockSpec((depth, tile), lambda i, at: (0, i))
    )
    return pl.pallas_call(
        functools.partial(chunks_kernel, transposed),
        grid_spec=pltpu.PrefetchScalarGridSpec(
            num_scalar_prefetch=1,
            grid=(columns // tile,),
            in_specs=[pl.BlockSpec((rows, depth), lambda i, at: (0, 0)), w_spec],
            out_specs=[pl.BlockSpec((rows // n, tile), lambda i, at: (0, i))] * n,
            scratch_shapes=[pltpu.VMEM((rows, tile), f32)],
        ),
        out_shape=[
            jax.ShapeDtypeStruct((rows // n, columns), bf16 if k == 1 % n else f32) for k in range(n)
        ],
        compiler_params=kernel_params(60),
        cost_estimate=kernel_cost(8),
        name="chunks_product",
    )(places, x, w)


def heads_kernel(x_ref, w_ref, out_ref):
    out_ref[0] = dot_nt(x_ref[...], w_ref[...]).astype(bf16)


def heads_product(x, w, n, nz):
    rows, depth = x.shape
    rest, feats = w.shape[0] // (2 * n), w.shape[0] // nz
    per = feats // rest

    def place(i):
        block = i % n * 2 + i // n
        return (block // per, 0, block % per)

    return pl.pallas_call(
        heads_kernel,
        grid=(2 * n,),
        in_specs=[
            pl.BlockSpec((rows, depth), lambda i: (0, 0)),
            pl.BlockSpec((rest, depth), lambda i: (i, 0)),
        ],
        out_specs=pl.BlockSpec((1, rows, rest), place),
        out_shape=jax.ShapeDtypeStruct((nz, rows, feats), bf16),
        compiler_params=kernel_params(60),
        cost_estimate=kernel_cost(4),
        name="heads_product",
    )(x, w)


def rms_parts(values):
    inverse = lax.rsqrt(jnp.mean(values * values, axis=1, keepdims=True) + norm_eps)
    return (values * inverse, inverse)


def norm_back(grad_normed, gain, normed, inverse):
    scaled = grad_normed * gain
    back = inverse * (scaled - normed * jnp.mean(scaled * normed, axis=1, keepdims=True))
    return (back, jnp.sum(grad_normed * normed, axis=0))


def body(
    tokens,
    cotangent,
    lengths,
    norm_attn,
    w_query,
    w_key,
    w_value,
    w_out,
    norm_ffn,
    w_gate,
    w_up,
    w_down,
):
    t, width = tokens.shape
    own_rows, hidden_width = w_gate.shape
    nz = lax.axis_size("z")
    groups = lax.axis_size("p") * 2
    sources = jnp.asarray(ring_sources(nz), jnp.int32)[lax.axis_index("z")]
    feats = width // nz
    block = hidden_width // (groups * nz)
    units = groups * block
    group_rows = nz * own_rows

    n = lax.axis_size("p")
    me, core = lax.axis_index("p"), lax.axis_index("c")
    hops = nz - 1

    inputs = tokens.astype(f32)
    normed_attn, inverse_attn = rms_parts(inputs)
    normed_attn_b = regrouped((normed_attn * norm_attn).astype(bf16), n)

    w_down_here = gather_rows(w_down).reshape(units, width)
    qkv = jnp.concatenate(
        [w.reshape(own_rows, nz, feats) for w in (w_query, w_key, w_value)], axis=2
    ).transpose(1, 0, 2)
    qkv = exchange(qkv)
    w_qkv = gather_rows(qkv).reshape(width, 3 * feats)

    tile = 128 if units % 128 == 0 else units
    cut = -(-units // 256) * 256
    pieces = unit_pieces(n, nz, block, tile)
    gate_up = spread(w_gate, w_up, nz, pieces)
    attn_in, out_rows = [after(normed_attn_b, qkv)], [w_out]
    for k in range(hops):
        parts, (w_down_here, gate_up) = tick(
            [(hop, attn_in[-1]), (hop, out_rows[-1])], (w_down_here, gate_up)
        )
        attn_in.append(parts[0])
        out_rows.append(parts[1])
    attn_in = placed(attn_in, sources)
    w_out_all = gather_rows(placed(out_rows, sources)).reshape(width, width)

    gate_up = exchange(gate_up)
    w_gate_up = gather_rows(gate_up).reshape(width, 2 * units)
    cot = [after(cotangent, gate_up)]

    docs = doc_number(jnp.arange(nz * t, dtype=jnp.int32), jnp.cumsum(lengths[0]))
    docs_down, docs_across = docs[:, None], docs[None, :]
    def cot_hop():
        return [(hop, cot[-1])] if len(cot) < nz else []

    three = dot(attn_in, w_qkv).astype(bf16)
    attended = local_kernel(attention_kernel, feats, three, docs_down, docs_across)
    part, attended = tick(cot_hop(), attended)
    cot += part
    (attended_b,), _ = tick([(exchange, attended.reshape(nz, t, feats))])
    attended_b = regrouped(attended_b.transpose(1, 0, 2).reshape(t, width), n)
    middle = inputs + dot(attended_b, w_out_all)
    normed_ffn, inverse_ffn = rms_parts(middle)
    normed_ffn_b = regrouped((normed_ffn * norm_ffn).astype(bf16), n)
    part, normed_ffn_b = tick(cot_hop(), normed_ffn_b)
    cot += part

    ffn_in = [normed_ffn_b]
    for _ in range(hops):
        (part, *more), _ = tick([(hop, ffn_in[-1])] + cot_hop())
        ffn_in.append(part)
        cot += more

    def ring_first(partials):
        return hop(partials[1 % nz].astype(bf16))

    hidden, grad_gate_up, left, right = feed(ffn_in, cot, sources, w_gate_up, w_down_here, tile)
    line = Line()

    def other_half(x, y):
        return rows_product(x, y, 1 - core, me, n, "other")

    def core_swap(parts):
        return [cross(part, "c", 1) for part in parts]

    def gu_piece(first, last):
        return lambda x, came: rows_product(
            x, grad_gate_up, core, me, n, "cut", came, first, last
        )

    def summed_piece(own, came):
        return line(lambda own, came: summed(own, *came).astype(bf16), own, came)

    def to_line_sum(x):
        return lax.psum_scatter(x, "z", scatter_dimension=0, tiled=True)

    grad_normed_ffn = to_line_sum(line(lambda x: dot_nt(x, w_gate_up).astype(bf16), grad_gate_up))
    gu_other = core_swap(line(other_half, left, grad_gate_up))
    down_own, down_other = line(lambda x, y: down_product(x, y, core, me, n), hidden, right)
    down_other = core_swap(down_other)
    first_own, *first_parts = line(gu_piece(0, cut), left, gu_other)
    first_came = plane_sent(first_parts, 1, n - 1)
    second_own, *second_parts = line(gu_piece(cut, 2 * units), left, gu_other)
    out_parts = line(lambda x: dot(x, w_down_here).astype(bf16), hidden)

    def ffn_back_piece(total):
        total = ungrouped(total.astype(f32), n)
        back, gain_part = norm_back(total, norm_ffn, normed_ffn, inverse_ffn)
        grad_middle = cotangent.astype(f32) + back
        return grad_middle, grad_middle.astype(bf16), gain_part

    grad_normed_ffn, first_came, first_parts = line.hold(grad_normed_ffn, first_came, first_parts)
    first_came = first_came + plane_sent(first_parts, n - 1, n)
    grad_middle, grad_branch_b, gain_ffn_part = line(ffn_back_piece, grad_normed_ffn)
    grad_att = exchange(line(lambda x: heads_product(x, w_out_all, n, nz), grad_branch_b))
    branch = lax.all_gather(grad_branch_b, "z", axis=0, tiled=True)
    down_sums = line(
        lambda own, came: [plus(x, y).astype(bf16) for x, y in zip(own, came, strict=True)][1:],
        down_own,
        down_other,
    )
    first_came, second_parts = line.hold(first_came, second_parts)
    second_came = plane_sent(second_parts, 1, n - 1)
    grad_first = summed_piece(first_own, first_came)
    second_came, second_parts = line.hold(second_came, second_parts)
    second_came = second_came + plane_sent(second_parts, n - 1, n)
    grad_three = line(
        lambda x: local_kernel(
            attention_back_kernel,
            3 * feats,
            three,
            x.reshape(nz * t, feats),
            docs_down,
            docs_across,
        ),
        grad_att,
    )
    grad_first = exchange(grad_first.reshape(nz, own_rows, cut))
    grad_normed_attn = to_line_sum(line(lambda x: dot_nt(x, w_qkv).astype(bf16), grad_three))
    qkv_other = core_swap(line(other_half, attn_in, grad_three))
    second_came, grad_first, out_parts = line.hold(second_came, grad_first, out_parts)
    out_total = to_line_sum(out_parts)
    qkv_own, *qkv_parts = line(
        lambda x, came: rows_product(x, grad_three, core, me, n, "cut", came), attn_in, qkv_other
    )
    qkv_came = plane_sent(qkv_parts, 1, n - 1)
    grad_second = summed_piece(second_own, second_came)
    grad_second = exchange(grad_second.reshape(nz, own_rows, 2 * units - cut))
    out_other = core_swap(line(other_half, attended, branch))
    qkv_came, qkv_parts, down_sums = line.hold(qkv_came, qkv_parts, down_sums)
    qkv_came = qkv_came + plane_sent(qkv_parts, n - 1, n)
    out_own, *out_sums = line(
        lambda x, y, came: rows_product(x, y, core, me, n, "cut", came), attended, branch, out_other
    )
    down_came = plane_sent(down_sums, 1, n - 1)

    def attn_norm_piece(total):
        total = ungrouped(total.astype(f32), n)
        back, gain_part = norm_back(total, norm_attn, normed_attn, inverse_attn)
        return grad_middle + back, jnp.stack([gain_part, gain_ffn_part])

    token_grad, gains = line(attn_norm_piece, grad_normed_attn)
    grad_second, qkv_came, out_sums = line.hold(grad_second, qkv_came, out_sums)
    grad_qkv = summed_piece(qkv_own, qkv_came)
    grad_qkv = exchange(grad_qkv.reshape(nz, own_rows, 3 * feats))
    out_sums = plane_sent(out_sums, 1, n)
    down_came, down_sums = line.hold(down_came, down_sums)
    down_came = down_came + plane_sent(down_sums, n - 1, n)
    grad_w_out = summed_piece(out_own, out_sums)
    grad_w_out = lax.ppermute(
        grad_w_out, ("p", "z"), [(i * nz + j, j * nz + i) for i in range(n) for j in range(nz)]
    )
    grad_w_gate, grad_w_up = line(lambda x, y: collect(x, y, pieces), grad_first, grad_second)
    grad_w_down = line(
        lambda own, other, came: summed(plus(own[0], other[0]), *came),
        down_own,
        down_other,
        down_came,
    )
    activations = (middle + out_total.astype(f32)).astype(bf16)
    for axis in ("c", "p", "z"):
        gains = paired_sum([gains, *spread_sums(gains, axis)])

    def three_piece(x):
        return [
            x[:, :, i * feats : (i + 1) * feats]
            .transpose(1, 0, 2)
            .reshape(own_rows, width)
            .astype(f32)
            for i in range(3)
        ]

    grad_w_query, grad_w_key, grad_w_value = line(three_piece, grad_qkv)
    grad_w_out = line(lambda x: x.astype(f32), grad_w_out)
    gains = gains + jnp.sum(line.token)
    grad_w_down = grad_w_down.astype(f32)
    return (
        activations,
        token_grad,
        gains[0],
        grad_w_query,
        grad_w_key,
        grad_w_value,
        grad_w_out,
        gains[1],
        grad_w_gate,
        grad_w_up,
        grad_w_down,
    )


def solution(mesh):
    dp, seq = mesh.shape["dp"], mesh.shape["seq"]
    grid = Mesh(mesh.devices.reshape(dp // 2, 2, seq), ALL)
    split = P(ALL, None)
    return jax.shard_map(
        body,
        mesh=grid,
        in_specs=(split, split, P(("p", "c"), None), P())
        + (split,) * 4
        + (P(),)
        + (split,) * 3,
        out_specs=(split, split, P(), split, split, split, split, P(), split, split, split),
        check_vma=False,
    )
```

time: 593 us -> 549 us (0.926)
  the two profiles are of different devices: /device:TPU:0 before, /device:TPU:2 now
where the time goes in v3:
time: 549 us; the launch traced here: 539 us
  waiting for transfers between devices  198 us (36%)
  Pallas kernels  94.7 us (17%)
  starting transfers between devices  63.6 us (12%)
  blocking collectives  62.9 us (11%)
  matrix products  38.2 us (7%)
  other arithmetic  32.1 us (6%)
  local copies, waits for them, and re-layouts  26.6 us (5%)
  between operations  23.1 us (4%)
    ppermute x12, waiting for transfers between devices, hop(): lax.ppermute(x, 'z', [(order[i], order[(i + 1) % n]) for i in range(n)])  81.8 us
    all_to_all x2, blocking collectives, exchange(): return lax.all_to_all(x, 'z', 0, 0, tiled=True)  62.9 us
    ppermute x29, waiting for transfers between devices, cross(): return lax.ppermute(x, axis, [(i, i ^ by) for i in range(n)])  59.2 us
    pallas_call x7, Pallas kernels, rows_product(): pl.pallas_call(functools.partial(rows_kernel, n, mode), grid_spec=pltpu.P...  41.3 us
    dot_general x5, matrix products, dot(): lax.dot_general(left, right, (dims, ((), ())), preferred_element_type=f32)  38.2 us
    all_to_all x5, waiting for transfers between devices, exchange(): return lax.all_to_all(x, 'z', 0, 0, tiled=True)  37.8 us
    ppermute x29, starting transfers between devices, cross(): return lax.ppermute(x, axis, [(i, i ^ by) for i in range(n)])  28.9 us
    pallas_call x1, Pallas kernels, feed(): pl.pallas_call(functools.partial(feed_kernel, nz), grid_spec=pltpu.Prefet...  20.1 us
  transfers between devices with their start and end apart: 55, of which 25 were waited for; matrix products, arithmetic and copies ran while one was open for 15% of the time, Pallas kernels for 12%

profile of v3, /device:TPU:2, one launch (start us, length us, event | category | flops | bytes accessed | tf_op | source)
XLA Modules:
  0.0 539.3 jit_solution(18135509980479648301)
XLA Ops:
  11.0 25.0 %all_to_all.35 = bf16[4,64,1536]{2,1,0:T(8,128)(2,1)} all-to-all(bf16[4,64,1536]{2,1,0:T(8,128)(2,1)S(1)} %copy.47), channel_id=1, replica_groups=mesh['p'=4,'c'=2,'z'=4] {'z'}, dimensions={0} | all-to-all | bytes 1572864 | tf_op jit(solution)/shard_map/all_to_all | solution.py:101
  43.3 12.5 %collective-permute-done.1 = bf16[64,2048]{1,0:T(8,128)(2,1)} collective-permute-done((bf16[64,2048]{1,0:T(8,128)(2,1)S(1)}, bf16[64,2048]{1,0:T(8,128)(2,1)}, u32[]{:S(2)}, u32[]{:S(2)}) %collective-permute-start.1) | collective-permute-done | bytes 262176 | tf_op jit(solution)/shard_map/ppermute | solution.py:49
  67.1 8.2 %collective-permute-done.3 = bf16[64,2048]{1,0:T(8,128)(2,1)S(1)} collective-permute-done((bf16[64,2048]{1,0:T(8,128)(2,1)}, bf16[64,2048]{1,0:T(8,128)(2,1)S(1)}, u32[]{:S(2)}, u32[]{:S(2)}) %collective-permute-start.3) | collective-permute-done | bytes 262176 | tf_op jit(solution)/shard_map/ppermute | solution.py:49
  80.2 14.2 %collective-permute-done.5 = bf16[64,2048]{1,0:T(8,128)(2,1)S(1)} collective-permute-done((bf16[64,2048]{1,0:T(8,128)(2,1)S(1)}, bf16[64,2048]{1,0:T(8,128)(2,1)S(1)}, u32[]{:S(2)}, u32[]{:S(2)}) %collective-permute-start.5) | collective-permute-done | bytes 262176 | tf_op jit(solution)/shard_map/ppermute | solution.py:49
  96.3 37.9 %all_to_all.36 = bf16[4,64,2816]{2,1,0:T(8,128)(2,1)} all-to-all(bf16[4,64,2816]{2,1,0:T(8,128)(2,1)S(1)} %copy-done.4), channel_id=1, replica_groups=mesh['p'=4,'c'=2,'z'=4] {'z'}, dimensions={0} | all-to-all | bytes 2883584 | tf_op jit(solution)/shard_map/all_to_all | solution.py:101
  142.0 6.9 %convolution_convert_fusion.2.qkv_ref = bf16[512,1536]{1,0:T(8,128)(2,1)S(1)} fusion(bf16[512,2048]{1,0:T(8,128)(2,1)} %bitcast.9.left_ref, bf16[2048,1536]{1,0:T(8,128)(2,1)} %bitcast.96), kind=kOutput, calls=%fused_computation.2 | convolution fusion | flops 3222011904 | bytes 9961472 | tf_op jit(solution)/shard_map/dot_general | solution.py:26
  161.5 12.5 %all-to-all-done.2 = bf16[4,128,512]{1,2,0:T(8,128)(2,1)S(1)} async-done(((bf16[4,128,512]{1,2,0:T(8,128)(2,1)}), bf16[4,128,512]{1,2,0:T(8,128)(2,1)S(1)}, u32[]{:S(2)}, u32[]{:S(2)}) %all-to-all-start.2) | async-done | bytes 524320 | tf_op jit(solution)/shard_map/all_to_all | solution.py:101
  179.1 4.9 multiply_reduce_fusion.2
  185.8 14.3 %collective-permute-done.8.refs_1_ = bf16[128,2048]{1,0:T(8,128)(2,1)S(1)} collective-permute-done((bf16[128,2048]{1,0:T(8,128)(2,1)S(1)}, bf16[128,2048]{1,0:T(8,128)(2,1)S(1)}, u32[]{:S(2)}, u32[]{:S(2)}) %collective-permute-start.8) | collective-permute-done | bytes 524320 | tf_op jit(solution)/shard_map/ppermute | solution.py:49
  200.2 7.6 %collective-permute-done.9.refs_7_ = bf16[128,2048]{1,0:T(8,128)(2,1)S(1)} collective-permute-done((bf16[128,2048]{1,0:T(8,128)(2,1)}, bf16[128,2048]{1,0:T(8,128)(2,1)S(1)}, u32[]{:S(2)}, u32[]{:S(2)}) %collective-permute-start.9) | collective-permute-done | bytes 524320 | tf_op jit(solution)/shard_map/ppermute | solution.py:49
  207.8 11.7 %collective-permute-done.10.refs_2_ = bf16[128,2048]{1,0:T(8,128)(2,1)} collective-permute-done((bf16[128,2048]{1,0:T(8,128)(2,1)S(1)}, bf16[128,2048]{1,0:T(8,128)(2,1)}, u32[]{:S(2)}, u32[]{:S(2)}) %collective-permute-start.10) | collective-permute-done | bytes 524320 | tf_op jit(solution)/shard_map/ppermute | solution.py:49
  220.3 9.7 %collective-permute-done.11.refs_3_ = bf16[128,2048]{1,0:T(8,128)(2,1)} collective-permute-done((bf16[128,2048]{1,0:T(8,128)(2,1)}, bf16[128,2048]{1,0:T(8,128)(2,1)}, u32[]{:S(2)}, u32[]{:S(2)}) %collective-permute-start.11) | collective-permute-done | bytes 524320 | tf_op jit(solution)/shard_map/ppermute | solution.py:49
  230.0 20.1 %feed_units.1 = (bf16[512,1408]{1,0:T(8,128)(2,1)}, bf16[512,2816]{1,0:T(8,128)(2,1)}, bf16[512,2048]{1,0:T(8,128)(2,1)}, bf16[512,2048]{1,0:T(8,128)(2,1)}) custom-call(s32[4]{0:T(128)} %get-tuple-element.526.places_ref, bf16[128,2048]{1,0:T(8,128)(2,1)} %copy-done.27, bf16[128,2048]{1,0:T(8,128)(2,1)} %copy-done.28, ...), custom_call_target="tpu_custom_call" | custom-call | flops 10350000128 | tf_op jit(solution)/shard_map/feed_units/pallas_call | solution.py:306
  250.1 10.9 %convolution_convert_fusion.1 = bf16[512,2048]{1,0:T(8,128)(2,1)} fusion(bf16[512,2816]{1,0:T(8,128)(2,1)} %get-tuple-element.298.right_ref, bf16[2048,2816]{1,0:T(8,128)(2,1)} %bitcast.95), kind=kOutput, calls=%fused_computation.1 | convolution fusion | flops 5906628608 | bytes 16515072 | tf_op jit(solution)/shard_map/dot_general | solution.py:26
  261.0 7.9 %rows_product.7 = bf16[1024,2816]{1,0:T(8,128)(2,1)} custom-call(s32[2]{0:T(128)} %get-tuple-element.535.at_ref, bf16[512,2048]{1,0:T(8,128)(2,1)} %get-tuple-element.327.left_ref, bf16[512,2816]{1,0:T(8,128)(2,1)} %get-tuple-element.298.right_ref), custom_call_target="tpu_custom_call" | custom-call | flops 3737499904 | tf_op jit(solution)/shard_map/rows_product/pallas_call | solution.py:379
  268.9 8.1 %down_product.1 = (bf16[176,2048]{1,0:T(8,128)(2,1)}, bf16[176,2048]{1,0:T(8,128)(2,1)}, bf16[176,2048]{1,0:T(8,128)(2,1)}, bf16[176,2048]{1,0:T(8,128)(2,1)}, b...) custom-call(s32[2]{0:T(128)} %get-tuple-element.534.at_ref, ...), custom_call_target="tpu_custom_call" | custom-call | flops 4024999936 | tf_op jit(solution)/shard_map/down_product/pallas_call | solution.py:423
  278.6 6.3 %rows_product.8 = (bf16[256,1536]{1,0:T(8,128)(2,1)}, bf16[256,1536]{1,0:T(8,128)(2,1)}, bf16[256,1536]{1,0:T(8,128)(2,1)}, bf16[256,1536]{1,0:T(8,128)(2,1)}) custom-call(s32[2]{0:T(128)} %get-tuple-element.534.at_ref, bf16[512,2048]{1,0:T(8,128)(2,1)} %get-tuple-element.327.left_ref, bf16[512,2816]{1,0:T(8,128)(2,1)} %get-tuple-element.298.right_ref, ...), custom_call_target="tpu_custom_call" | custom-call | flops 3737499904 | tf_op jit(solution)/shard_map/rows_product/pallas_call | solution.py:379
  284.9 7.4 %rows_product.9 = (bf16[256,1280]{1,0:T(8,128)(2,1)}, bf16[256,1280]{1,0:T(8,128)(2,1)}, bf16[256,1280]{1,0:T(8,128)(2,1)}, bf16[256,1280]{1,0:T(8,128)(2,1)}) custom-call(s32[2]{0:T(128)} %get-tuple-element.534.at_ref, bf16[512,2048]{1,0:T(8,128)(2,1)} %get-tuple-element.327.left_ref, bf16[512,2816]{1,0:T(8,128)(2,1)} %get-tuple-element.298.right_ref, ...), custom_call_target="tpu_custom_call" | custom-call | flops 3737499904 | tf_op jit(solution)/shard_map/rows_product/pallas_call | solution.py:379
  293.5 8.0 %convolution_convert_fusion.3 = bf16[512,2048]{1,0:T(8,128)(2,1)} fusion(bf16[512,1408]{1,0:T(8,128)(2,1)} %get-tuple-element.335.left_ref, bf16[1408,2048]{1,0:T(8,128)(2,1)} %all-gather.13.cloned.1.call-done.refs_9_), kind=kOutput, calls=%fused_computation.3 | convolution fusion | flops 2953838592 | bytes 9306112 | tf_op jit(solution)/shard_map/dot_general | solution.py:26
  301.5 10.8 %collective-permute-done.13 = bf16[256,1536]{1,0:T(8,128)(2,1)} collective-permute-done((bf16[256,1536]{1,0:T(8,128)(2,1)}, bf16[256,1536]{1,0:T(8,128)(2,1)}, u32[]{:S(2)}, u32[]{:S(2)}) %collective-permute-start.13) | collective-permute-done | bytes 786464 | tf_op jit(solution)/shard_map/ppermute | solution.py:39
  317.7 8.8 %heads_product.1 = bf16[4,128,512]{2,1,0:T(8,128)(2,1)} custom-call(bf16[128,2048]{1,0:T(8,128)(2,1)} %get-tuple-element.358.x_ref, bf16[2048,2048]{1,0:T(8,128)(2,1)} %bitcast.76), custom_call_target="tpu_custom_call" | custom-call | flops 2300000000 | tf_op jit(solution)/shard_map/heads_product/pallas_call | solution.py:492
  342.8 10.6 %collective-permute-done.20 = bf16[256,1280]{1,0:T(8,128)(2,1)} collective-permute-done((bf16[256,1280]{1,0:T(8,128)(2,1)}, bf16[256,1280]{1,0:T(8,128)(2,1)}, u32[]{:S(2)}, u32[]{:S(2)}) %collective-permute-start.20) | collective-permute-done | bytes 655392 | tf_op jit(solution)/shard_map/ppermute | solution.py:39
  354.5 7.0 %shard_map.213.right_ref = bf16[512,1536]{1,0:T(8,128)(2,1)S(1)} custom-call(bf16[512,1536]{1,0:T(8,128)(2,1)S(1)} %convolution_convert_fusion.2.qkv_ref, bf16[512,512]{1,0:T(8,128)(2,1)S(1)} %bitcast.71, s32[512,1]{1,0:T(8,128)S(1)} %copy.48.docs_down_ref, s32[1,512]{1,0:T(1,128)S(1)} %bitcast.74), custom_call_target="tpu_custom_call" | custom-call | flops 2875000064 | tf_op jit(solution)/shard_map/pallas_call | solution.py:204
  362.7 7.5 %convolution_convert_fusion = bf16[512,2048]{1,0:T(8,128)(2,1)} fusion(bf16[512,1536]{1,0:T(8,128)(2,1)S(1)} %shard_map.213.right_ref, bf16[2048,1536]{1,0:T(8,128)(2,1)} %bitcast.97), kind=kOutput, calls=%fused_computation | convolution fusion | flops 3222274048 | bytes 9961472 | tf_op jit(solution)/shard_map/dot_general | solution.py:26
  370.2 5.7 %rows_product.10 = bf16[1024,1536]{1,0:T(8,128)(2,1)} custom-call(s32[2]{0:T(128)} %get-tuple-element.535.at_ref, bf16[512,2048]{1,0:T(8,128)(2,1)} %bitcast.9.left_ref, bf16[512,1536]{1,0:T(8,128)(2,1)} %copy-done.1), custom_call_target="tpu_custom_call" | custom-call | flops 3737499904 | tf_op jit(solution)/shard_map/rows_product/pallas_call | solution.py:379
  382.2 25.2 %all-to-all-done.3.first_ref = bf16[4,64,1536]{2,1,0:T(8,128)(2,1)S(1)} async-done(((bf16[4,64,1536]{2,1,0:T(8,128)(2,1)}), bf16[4,64,1536]{2,1,0:T(8,128)(2,1)S(1)}, u32[]{:S(2)}, u32[]{:S(2)}) %all-to-all-start.3) | async-done | bytes 786464 | tf_op jit(solution)/shard_map/all_to_all | solution.py:101
  407.4 6.3 %rows_product.11 = (bf16[256,1536]{1,0:T(8,128)(2,1)}, bf16[256,1536]{1,0:T(8,128)(2,1)}, bf16[256,1536]{1,0:T(8,128)(2,1)}, bf16[256,1536]{1,0:T(8,128)(2,1)}) custom-call(s32[2]{0:T(128)} %get-tuple-element.534.at_ref, bf16[512,2048]{1,0:T(8,128)(2,1)} %bitcast.9.left_ref, bf16[512,1536]{1,0:T(8,128)(2,1)} %copy-done.1, ...), custom_call_target="tpu_custom_call" | custom-call | flops 3737499904 | tf_op jit(solution)/shard_map/rows_product/pallas_call | solution.py:379
  425.8 14.3 %collective-permute-done.25 = bf16[256,1536]{1,0:T(8,128)(2,1)S(1)} collective-permute-done((bf16[256,1536]{1,0:T(8,128)(2,1)}, bf16[256,1536]{1,0:T(8,128)(2,1)S(1)}, u32[]{:S(2)}, u32[]{:S(2)}) %collective-permute-start.25) | collective-permute-done | bytes 786464 | tf_op jit(solution)/shard_map/ppermute | solution.py:39
  456.1 6.3 %collective-permute-done.30 = f32[2,2048]{1,0:T(2,128)S(1)} collective-permute-done((f32[2,2048]{1,0:T(2,128)S(1)}, f32[2,2048]{1,0:T(2,128)S(1)}, u32[]{:S(2)}, u32[]{:S(2)}) %collective-permute-start.30) | collective-permute-done | bytes 16416 | tf_op jit(solution)/shard_map/ppermute | solution.py:39
  468.1 8.7 %collective-permute-done.38 = bf16[176,2048]{1,0:T(8,128)(2,1)S(1)} collective-permute-done((bf16[176,2048]{1,0:T(8,128)(2,1)}, bf16[176,2048]{1,0:T(8,128)(2,1)S(1)}, u32[]{:S(2)}, u32[]{:S(2)}) %collective-permute-start.38) | collective-permute-done | bytes 720928 | tf_op jit(solution)/shard_map/ppermute | solution.py:39
  487.5 13.7 %reduce-scatter.6.cloned.1.call-done = bf16[128,2048]{1,0:T(8,128)(2,1)} async-done(((bf16[512,2048]{1,0:T(8,128)(2,1)}), bf16[128,2048]{1,0:T(8,128)(2,1)}) %reduce-scatter.6.cloned.1.call-update) | async-done | bytes 524304 | tf_op jit(solution)/shard_map/reduce_scatter | solution.py:619
  524.4 4.9 collective-permute-done.40
  (265 shorter events, 152.4 us)
Async XLA Ops:
  7.2 48.6 %all-gather.13.cloned.1.call-start = ((), (), s32[]{:S(2)}) async-start(), calls=%async_computation.15 | async-start | bytes 6488064 | tf_op jit(solution)/shard_map/all_gather | solution.py:66
  7.9 134.0 %all-gather.15.cloned.1.call-start = ((), (), s32[]{:S(2)}) async-start(), calls=%async_computation.16 | async-start | bytes 7077888 | tf_op jit(solution)/shard_map/all_gather | solution.py:66
  36.0 143.1 %all-gather.9.cloned.1.call-start = ((), (), s32[]{:S(2)}) async-start(), calls=%async_computation.10 | async-start | bytes 9437184 | tf_op jit(solution)/shard_map/all_gather | solution.py:66
  96.2 133.8 %all-gather.17.cloned.1.call-start = ((), (), s32[]{:S(2)}) async-start(), calls=%async_computation.17 | async-start | bytes 12976128 | tf_op jit(solution)/shard_map/all_gather | solution.py:66
  159.5 152.9 %reduce-scatter.4.cloned.1.call-start = ((), (), s32[]{:S(2)}) async-start(), calls=%async_computation.11 | async-start | bytes 2621440 | tf_op jit(solution)/shard_map/reduce_scatter | solution.py:619
  159.5 24.8 %collective-permute-start.7 = (bf16[128,2048]{1,0:T(8,128)(2,1)}, bf16[128,2048]{1,0:T(8,128)(2,1)}, u32[]{:S(2)}, u32[]{:S(2)}) collective-permute-start(bf16[128,2048]{1,0:T(8,128)(2,1)} %collective-permute-done.6.refs_5_), channel_id=1, source_target_pairs={{1,3},{3,2},{2,0},{0,1},{5,7},{7,6},{6,4},{4,5},{9,11},{11,10},{10... | collective-permute-start | bytes 1572872 | tf_op jit(solution)/shard_map/ppermute | solution.py:49
  184.5 23.2 %collective-permute-start.9 = (bf16[128,2048]{1,0:T(8,128)(2,1)}, bf16[128,2048]{1,0:T(8,128)(2,1)S(1)}, u32[]{:S(2)}, u32[]{:S(2)}) collective-permute-start(bf16[128,2048]{1,0:T(8,128)(2,1)} %collective-permute-done.7.refs_6_), channel_id=1, source_target_pairs={{1,3},{3,2},{2,0},{0,1},{5,7},{7,6},{6,4},{4,5},{9,11},{11,10},{10... | collective-permute-start | bytes 1572872 | tf_op jit(solution)/shard_map/ppermute | solution.py:49
  276.9 49.5 %collective-permute-start.16 = (bf16[176,2048]{1,0:T(8,128)(2,1)}, bf16[176,2048]{1,0:T(8,128)(2,1)}, u32[]{:S(2)}, u32[]{:S(2)}) collective-permute-start(bf16[176,2048]{1,0:T(8,128)(2,1)} %get-tuple-element.348), channel_id=1, source_target_pairs={{0,4},{4,0},{1,5},{5,1},{2,6},{6,2},{3,7},{7,3},{8,12},{12,8},{9,1... | collective-permute-start | bytes 2162696 | tf_op jit(solution)/shard_map/ppermute | solution.py:39
  277.5 49.0 %collective-permute-start.17 = (bf16[176,2048]{1,0:T(8,128)(2,1)}, bf16[176,2048]{1,0:T(8,128)(2,1)}, u32[]{:S(2)}, u32[]{:S(2)}) collective-permute-start(bf16[176,2048]{1,0:T(8,128)(2,1)} %get-tuple-element.349), channel_id=1, source_target_pairs={{0,4},{4,0},{1,5},{5,1},{2,6},{6,2},{3,7},{7,3},{8,12},{12,8},{9,1... | collective-permute-start | bytes 2162696 | tf_op jit(solution)/shard_map/ppermute | solution.py:39
  277.5 48.9 %collective-permute-start.18 = (bf16[176,2048]{1,0:T(8,128)(2,1)}, bf16[176,2048]{1,0:T(8,128)(2,1)}, u32[]{:S(2)}, u32[]{:S(2)}) collective-permute-start(bf16[176,2048]{1,0:T(8,128)(2,1)} %get-tuple-element.350), channel_id=1, source_target_pairs={{0,4},{4,0},{1,5},{5,1},{2,6},{6,2},{3,7},{7,3},{8,12},{12,8},{9,1... | collective-permute-start | bytes 2162696 | tf_op jit(solution)/shard_map/ppermute | solution.py:39
  292.3 19.9 %collective-permute-start.13 = (bf16[256,1536]{1,0:T(8,128)(2,1)}, bf16[256,1536]{1,0:T(8,128)(2,1)}, u32[]{:S(2)}, u32[]{:S(2)}) collective-permute-start(bf16[256,1536]{1,0:T(8,128)(2,1)} %get-tuple-element.323), channel_id=1, source_target_pairs={{0,8},{8,0},{16,24},{24,16},{1,9},{9,1},{17,25},{25,17},{2,10},{10... | collective-permute-start | bytes 2359304 | tf_op jit(solution)/shard_map/ppermute | solution.py:39
  313.7 23.5 %collective-permute-start.15 = (bf16[256,1536]{1,0:T(8,128)(2,1)}, bf16[256,1536]{1,0:T(8,128)(2,1)}, u32[]{:S(2)}, u32[]{:S(2)}) collective-permute-start(bf16[256,1536]{1,0:T(8,128)(2,1)} %get-tuple-element.340), channel_id=1, source_target_pairs={{0,24},{8,16},{16,8},{24,0},{1,25},{9,17},{17,9},{25,1},{2,26},{10... | collective-permute-start | bytes 2359304 | tf_op jit(solution)/shard_map/ppermute | solution.py:39
  326.4 28.1 %all-to-all-start.4 = ((bf16[4,128,512]{2,1,0:T(8,128)(2,1)}), bf16[4,128,512]{2,1,0:T(8,128)(2,1)S(1)}, u32[]{:S(2)}, u32[]{:S(2)}) async-start(bf16[4,128,512]{2,1,0:T(8,128)(2,1)} %heads_product.1), calls=%async_computation.5 | async-start | bytes 1048576 | tf_op jit(solution)/shard_map/all_to_all | solution.py:101
  330.2 86.0 %all-gather.11.cloned.1.call-start = ((), (), s32[]{:S(2)}) async-start(), calls=%async_computation.14 | async-start | bytes 2621440 | tf_op jit(solution)/shard_map/all_gather | solution.py:640
  339.6 107.2 %reduce-scatter.8.cloned.1.call-start = ((), (), s32[]{:S(2)}) async-start(), calls=%async_computation.13 | async-start | bytes 2621440 | tf_op jit(solution)/shard_map/reduce_scatter | solution.py:619
  375.9 31.5 %collective-permute-start.23 = (bf16[1024,1536]{1,0:T(8,128)(2,1)}, bf16[1024,1536]{1,0:T(8,128)(2,1)}, u32[]{:S(2)}, u32[]{:S(2)}) collective-permute-start(bf16[1024,1536]{1,0:T(8,128)(2,1)} %rows_product.10), channel_id=1, source_target_pairs={{0,4},{4,0},{1,5},{5,1},{2,6},{6,2},{3,7},{7,3},{8,12},{12,8},{9,1... | collective-permute-start | bytes 9437192 | tf_op jit(solution)/shard_map/ppermute | solution.py:39
  375.9 31.5 %all-to-all-start.3 = ((bf16[4,64,1536]{2,1,0:T(8,128)(2,1)}), bf16[4,64,1536]{2,1,0:T(8,128)(2,1)S(1)}, u32[]{:S(2)}, u32[]{:S(2)}) async-start(bf16[4,64,1536]{2,1,0:T(8,128)(2,1)} %bitcast.30), calls=%async_computation.4 | async-start | bytes 1572864 | tf_op jit(solution)/shard_map/all_to_all | solution.py:101
  380.7 120.4 %reduce-scatter.6.cloned.1.call-start = ((), (), s32[]{:S(2)}) async-start(), calls=%async_computation.12 | async-start | bytes 2621440 | tf_op jit(solution)/shard_map/reduce_scatter | solution.py:619
  380.7 26.7 %collective-permute-start.22 = (bf16[256,1280]{1,0:T(8,128)(2,1)}, bf16[256,1280]{1,0:T(8,128)(2,1)S(1)}, u32[]{:S(2)}, u32[]{:S(2)}) collective-permute-start(bf16[256,1280]{1,0:T(8,128)(2,1)} %get-tuple-element.385), channel_id=1, source_target_pairs={{0,24},{8,16},{16,8},{24,0},{1,25},{9,17},{17,9},{25,1},{2,26},{10... | collective-permute-start | bytes 1966088 | tf_op jit(solution)/shard_map/ppermute | solution.py:39
  420.0 22.8 %collective-permute-start.24 = (bf16[256,2048]{1,0:T(8,128)(2,1)}, bf16[256,2048]{1,0:T(8,128)(2,1)}, u32[]{:S(2)}, u32[]{:S(2)}) collective-permute-start(bf16[256,2048]{1,0:T(8,128)(2,1)} %rows_product.12), channel_id=1, source_target_pairs={{0,4},{4,0},{1,5},{5,1},{2,6},{6,2},{3,7},{7,3},{8,12},{12,8},{9,1... | collective-permute-start | bytes 3145736 | tf_op jit(solution)/shard_map/ppermute | solution.py:39
  420.0 20.2 %collective-permute-start.25 = (bf16[256,1536]{1,0:T(8,128)(2,1)}, bf16[256,1536]{1,0:T(8,128)(2,1)S(1)}, u32[]{:S(2)}, u32[]{:S(2)}) collective-permute-start(bf16[256,1536]{1,0:T(8,128)(2,1)} %get-tuple-element.427), channel_id=1, source_target_pairs={{0,8},{8,0},{16,24},{24,16},{1,9},{9,1},{17,25},{25,17},{2,10},{10... | collective-permute-start | bytes 2359304 | tf_op jit(solution)/shard_map/ppermute | solution.py:39
  422.1 42.9 %all-to-all-start.5 = ((bf16[4,64,1280]{2,1,0:T(8,128)(2,1)}), bf16[4,64,1280]{2,1,0:T(8,128)(2,1)S(1)}, u32[]{:S(2)}, u32[]{:S(2)}) async-start(bf16[4,64,1280]{2,1,0:T(8,128)(2,1)} %bitcast.34), calls=%async_computation.8 | async-start | bytes 1310720 | tf_op jit(solution)/shard_map/all_to_all | solution.py:101
  440.5 24.5 %collective-permute-start.34 = (bf16[256,1536]{1,0:T(8,128)(2,1)}, bf16[256,1536]{1,0:T(8,128)(2,1)}, u32[]{:S(2)}, u32[]{:S(2)}) collective-permute-start(bf16[256,1536]{1,0:T(8,128)(2,1)} %get-tuple-element.453), channel_id=1, source_target_pairs={{0,24},{8,16},{16,8},{24,0},{1,25},{9,17},{17,9},{25,1},{2,26},{10... | collective-permute-start | bytes 2359304 | tf_op jit(solution)/shard_map/ppermute | solution.py:39
  455.5 21.3 %collective-permute-start.38 = (bf16[176,2048]{1,0:T(8,128)(2,1)}, bf16[176,2048]{1,0:T(8,128)(2,1)S(1)}, u32[]{:S(2)}, u32[]{:S(2)}) collective-permute-start(bf16[176,2048]{1,0:T(8,128)(2,1)} %add_convert_fusion.4), channel_id=1, source_target_pairs={{0,8},{8,0},{16,24},{24,16},{1,9},{9,1},{17,25},{25,17},{2,10},{10... | collective-permute-start | bytes 2162696 | tf_op jit(solution)/shard_map/ppermute | solution.py:39
  463.9 66.8 %collective-permute-start.33 = (f32[2,2048]{1,0:T(2,128)S(1)}, f32[2,2048]{1,0:T(2,128)S(1)}, u32[]{:S(2)}, u32[]{:S(2)}) collective-permute-start(f32[2,2048]{1,0:T(2,128)S(1)} %add_add_fusion.1), channel_id=1, source_target_pairs={{0,3},{1,2},{2,1},{3,0},{4,7},{5,6},{6,5},{7,4},{8,11},{9,10},{10,... | collective-permute-start | bytes 49160 | tf_op jit(solution)/shard_map/ppermute | solution.py:39
  478.1 43.5 %all-to-all-start.6 = ((bf16[4,64,1536]{2,1,0:T(8,128)(2,1)}), bf16[4,64,1536]{2,1,0:T(8,128)(2,1)S(1)}, u32[]{:S(2)}, u32[]{:S(2)}) async-start(bf16[4,64,1536]{2,1,0:T(8,128)(2,1)} %bitcast.35), calls=%async_computation.9 | async-start | bytes 1572864 | tf_op jit(solution)/shard_map/all_to_all | solution.py:101
  481.8 21.3 %collective-permute-start.35 = (bf16[64,2048]{1,0:T(8,128)(2,1)}, bf16[64,2048]{1,0:T(8,128)(2,1)S(1)}, u32[]{:S(2)}, u32[]{:S(2)}) collective-permute-start(bf16[64,2048]{1,0:T(8,128)(2,1)} %get-tuple-element.458), channel_id=1, source_target_pairs={{0,8},{8,0},{16,24},{24,16},{1,9},{9,1},{17,25},{25,17},{2,10},{10... | collective-permute-start | bytes 786440 | tf_op jit(solution)/shard_map/ppermute | solution.py:39
  483.1 26.6 %collective-permute-start.36 = (bf16[64,2048]{1,0:T(8,128)(2,1)}, bf16[64,2048]{1,0:T(8,128)(2,1)S(1)}, u32[]{:S(2)}, u32[]{:S(2)}) collective-permute-start(bf16[64,2048]{1,0:T(8,128)(2,1)} %get-tuple-element.459), channel_id=1, source_target_pairs={{0,16},{8,24},{16,0},{24,8},{1,17},{9,25},{17,1},{25,9},{2,18},{10... | collective-permute-start | bytes 786440 | tf_op jit(solution)/shard_map/ppermute | solution.py:39
  484.6 26.8 %collective-permute-start.37 = (bf16[64,2048]{1,0:T(8,128)(2,1)}, bf16[64,2048]{1,0:T(8,128)(2,1)}, u32[]{:S(2)}, u32[]{:S(2)}) collective-permute-start(bf16[64,2048]{1,0:T(8,128)(2,1)} %get-tuple-element.460), channel_id=1, source_target_pairs={{0,24},{8,16},{16,8},{24,0},{1,25},{9,17},{17,9},{25,1},{2,26},{10... | collective-permute-start | bytes 786440 | tf_op jit(solution)/shard_map/ppermute | solution.py:39
  485.3 33.1 %collective-permute-start.41 = (bf16[176,2048]{1,0:T(8,128)(2,1)}, bf16[176,2048]{1,0:T(8,128)(2,1)}, u32[]{:S(2)}, u32[]{:S(2)}) collective-permute-start(bf16[176,2048]{1,0:T(8,128)(2,1)} %add_convert_fusion.2), channel_id=1, source_target_pairs={{0,24},{8,16},{16,8},{24,0},{1,25},{9,17},{17,9},{25,1},{2,26},{10... | collective-permute-start | bytes 2162696 | tf_op jit(solution)/shard_map/ppermute | solution.py:39
  503.1 27.6 %collective-permute-start.32 = (f32[2,2048]{1,0:T(2,128)S(1)}, f32[2,2048]{1,0:T(2,128)S(1)}, u32[]{:S(2)}, u32[]{:S(2)}) collective-permute-start(f32[2,2048]{1,0:T(2,128)S(1)} %add_add_fusion.1), channel_id=1, source_target_pairs={{0,2},{1,3},{2,0},{3,1},{4,6},{5,7},{6,4},{7,5},{8,10},{9,11},{10,... | collective-permute-start | bytes 49160 | tf_op jit(solution)/shard_map/ppermute | solution.py:39
  509.7 20.9 %collective-permute-start.31 = (f32[2,2048]{1,0:T(2,128)S(1)}, f32[2,2048]{1,0:T(2,128)S(1)}, u32[]{:S(2)}, u32[]{:S(2)}) collective-permute-start(f32[2,2048]{1,0:T(2,128)S(1)} %add_add_fusion.1), channel_id=1, source_target_pairs={{0,1},{1,0},{2,3},{3,2},{4,5},{5,4},{6,7},{7,6},{8,9},{9,8},{10,11... | collective-permute-start | bytes 49160 | tf_op jit(solution)/shard_map/ppermute | solution.py:39
  (54 other events, 727.7 us)
Sparse Core Ops, SparseCore 0:
  9.9 44.5 all-gather.12
  56.4 45.5 all-gather.14
  104.4 54.3 all-gather.8
  160.5 67.6 all-gather.16
  269.0 43.3 reduce-scatter.3
  339.7 51.9 all-gather.10
  394.1 50.7 reduce-scatter.7
  447.2 53.9 reduce-scatter.5

commit v4 on v3

--- a/solution.py
+++ b/solution.py
@@ -207,7 +207,7 @@
         in_specs=[pl.BlockSpec(memory_space=pltpu.VMEM)] * len(args),
         out_specs=pl.BlockSpec(memory_space=pltpu.VMEM),
         compiler_params=kernel_params(10),
-        cost_estimate=kernel_cost(5),
+        cost_estimate=kernel_cost(0),
     )(*args)
 
 
@@ -499,7 +499,7 @@
         out_specs=pl.BlockSpec((1, rows, rest), place),
         out_shape=jax.ShapeDtypeStruct((nz, rows, feats), bf16),
         compiler_params=kernel_params(60),
-        cost_estimate=kernel_cost(4),
+        cost_estimate=kernel_cost(0),
         name="heads_product",
     )(x, w)
 
@@ -558,15 +558,18 @@
     cut = -(-units // 256) * 256
     pieces = unit_pieces(n, nz, block, tile)
     gate_up = spread(w_gate, w_up, nz, pieces)
-    attn_in, out_rows = [after(normed_attn_b, qkv)], [w_out]
+    def laid(whole, part, k):
+        return lax.dynamic_update_slice(whole, part, (sources[k] * part.shape[0], 0))
+
+    came, out_came = normed_attn_b, w_out
+    attn_in = laid(jnp.zeros((nz * t, width), bf16), came, 0)
+    out_rows = laid(jnp.zeros((nz * own_rows, width), bf16), out_came, 0)
     for k in range(hops):
-        parts, (w_down_here, gate_up) = tick(
-            [(hop, attn_in[-1]), (hop, out_rows[-1])], (w_down_here, gate_up)
+        (came, out_came), (w_down_here, gate_up, attn_in, out_rows) = tick(
+            [(hop, came), (hop, out_came)], (w_down_here, gate_up, attn_in, out_rows)
         )
-        attn_in.append(parts[0])
-        out_rows.append(parts[1])
-    attn_in = placed(attn_in, sources)
-    w_out_all = gather_rows(placed(out_rows, sources)).reshape(width, width)
+        attn_in, out_rows = laid(attn_in, came, k + 1), laid(out_rows, out_came, k + 1)
+    w_out_all = gather_rows(out_rows.reshape(nz, own_rows, width)).reshape(width, width)
 
     gate_up = exchange(gate_up)
     w_gate_up = gather_rows(gate_up).reshape(width, 2 * units)
@@ -662,21 +665,26 @@
     grad_first = exchange(grad_first.reshape(nz, own_rows, cut))
     grad_normed_attn = to_line_sum(line(lambda x: dot_nt(x, w_qkv).astype(bf16), grad_three))
     qkv_other = core_swap(line(other_half, attn_in, grad_three))
-    second_came, grad_first, out_parts = line.hold(second_came, grad_first, out_parts)
-    out_total = to_line_sum(out_parts)
+    second_came = line.hold(second_came)
     qkv_own, *qkv_parts = line(
         lambda x, came: rows_product(x, grad_three, core, me, n, "cut", came), attn_in, qkv_other
     )
     qkv_came = plane_sent(qkv_parts, 1, n - 1)
+    qkv_came, qkv_parts = line.hold(qkv_came, qkv_parts)
+    qkv_came = qkv_came + plane_sent(qkv_parts, n - 1, n)
+    grad_first, out_parts = line.hold(grad_first, out_parts)
+    out_total = to_line_sum(out_parts)
     grad_second = summed_piece(second_own, second_came)
     grad_second = exchange(grad_second.reshape(nz, own_rows, 2 * units - cut))
     out_other = core_swap(line(other_half, attended, branch))
-    qkv_came, qkv_parts, down_sums = line.hold(qkv_came, qkv_parts, down_sums)
-    qkv_came = qkv_came + plane_sent(qkv_parts, n - 1, n)
+    qkv_came, down_sums = line.hold(qkv_came, down_sums)
     out_own, *out_sums = line(
         lambda x, y, came: rows_product(x, y, core, me, n, "cut", came), attended, branch, out_other
     )
     down_came = plane_sent(down_sums, 1, n - 1)
+    grad_qkv = summed_piece(qkv_own, qkv_came)
+    grad_second = line.hold(grad_second)
+    grad_qkv = exchange(grad_qkv.reshape(nz, own_rows, 3 * feats))
 
     def attn_norm_piece(total):
         total = ungrouped(total.astype(f32), n)
@@ -684,9 +692,7 @@
         return grad_middle + back, jnp.stack([gain_part, gain_ffn_part])
 
     token_grad, gains = line(attn_norm_piece, grad_normed_attn)
-    grad_second, qkv_came, out_sums = line.hold(grad_second, qkv_came, out_sums)
-    grad_qkv = summed_piece(qkv_own, qkv_came)
-    grad_qkv = exchange(grad_qkv.reshape(nz, own_rows, 3 * feats))
+    out_sums = line.hold(out_sums)
     out_sums = plane_sent(out_sums, 1, n)
     down_came, down_sums = line.hold(down_came, down_sums)
     down_came = down_came + plane_sent(down_sums, n - 1, n)
@@ -694,17 +700,6 @@
     grad_w_out = lax.ppermute(
         grad_w_out, ("p", "z"), [(i * nz + j, j * nz + i) for i in range(n) for j in range(nz)]
     )
-    grad_w_gate, grad_w_up = line(lambda x, y: collect(x, y, pieces), grad_first, grad_second)
-    grad_w_down = line(
-        lambda own, other, came: summed(plus(own[0], other[0]), *came),
-        down_own,
-        down_other,
-        down_came,
-    )
-    activations = (middle + out_total.astype(f32)).astype(bf16)
-    for axis in ("c", "p", "z"):
-        gains = paired_sum([gains, *spread_sums(gains, axis)])
-
     def three_piece(x):
         return [
             x[:, :, i * feats : (i + 1) * feats]
@@ -715,6 +710,17 @@
         ]
 
     grad_w_query, grad_w_key, grad_w_value = line(three_piece, grad_qkv)
+
+    grad_w_gate, grad_w_up = line(lambda x, y: collect(x, y, pieces), grad_first, grad_second)
+    grad_w_down = line(
+        lambda own, other, came: summed(plus(own[0], other[0]), *came),
+        down_own,
+        down_other,
+        down_came,
+    )
+    activations = (middle + out_total.astype(f32)).astype(bf16)
+    for axis in ("c", "p", "z"):
+        gains = paired_sum([gains, *spread_sums(gains, axis)])
     grad_w_out = line(lambda x: x.astype(f32), grad_w_out)
     gains = gains + jnp.sum(line.token)
     grad_w_down = grad_w_down.astype(f32)

time: 549 us -> 540 us (0.984)
  the two profiles are of different devices: /device:TPU:2 before, /device:TPU:0 now
where the time goes in v4:
time: 540 us; the launch traced here: 530 us
  waiting for transfers between devices  189 us (35%)
  Pallas kernels  94.8 us (18%)
  starting transfers between devices  65.6 us (12%)
  blocking collectives  64.2 us (12%)
  matrix products  38.1 us (7%)
  other arithmetic  31.4 us (6%)
  local copies, waits for them, and re-layouts  26.5 us (5%)
  between operations  20.7 us (4%)
    ppermute x12, waiting for transfers between devices, hop(): lax.ppermute(x, 'z', [(order[i], order[(i + 1) % n]) for i in range(n)])  79.3 us
    ppermute x29, waiting for transfers between devices, cross(): return lax.ppermute(x, axis, [(i, i ^ by) for i in range(n)])  71.1 us
    all_to_all x2, blocking collectives, exchange(): return lax.all_to_all(x, 'z', 0, 0, tiled=True)  64.2 us
    pallas_call x7, Pallas kernels, rows_product(): pl.pallas_call(functools.partial(rows_kernel, n, mode), grid_spec=pltpu.P...  41.5 us
    dot_general x5, matrix products, dot(): lax.dot_general(left, right, (dims, ((), ())), preferred_element_type=f32)  38.1 us
    all_to_all x5, waiting for transfers between devices, exchange(): return lax.all_to_all(x, 'z', 0, 0, tiled=True)  32.5 us
    ppermute x29, starting transfers between devices, cross(): return lax.ppermute(x, axis, [(i, i ^ by) for i in range(n)])  29.5 us
    all_to_all x5, starting transfers between devices, exchange(): return lax.all_to_all(x, 'z', 0, 0, tiled=True)  21.6 us
  transfers between devices with their start and end apart: 55, of which 25 were waited for; matrix products, arithmetic and copies ran while one was open for 15% of the time, Pallas kernels for 13%

profile of v4, /device:TPU:0, one launch (start us, length us, event | category | flops | bytes accessed | tf_op | source)
XLA Modules:
  0.0 530.3 jit_solution(3069652456341843785)
XLA Ops:
  11.0 26.5 %all_to_all.35 = bf16[4,64,1536]{2,1,0:T(8,128)(2,1)} all-to-all(bf16[4,64,1536]{2,1,0:T(8,128)(2,1)S(1)} %copy.47), channel_id=1, replica_groups=mesh['p'=4,'c'=2,'z'=4] {'z'}, dimensions={0} | all-to-all | bytes 1572864 | tf_op jit(solution)/shard_map/all_to_all | solution.py:101
  49.5 8.0 %collective-permute-done = bf16[128,2048]{1,0:T(8,128)(2,1)S(1)} collective-permute-done((bf16[128,2048]{1,0:T(8,128)(2,1)S(1)}, bf16[128,2048]{1,0:T(8,128)(2,1)S(1)}, u32[]{:S(2)}, u32[]{:S(2)}) %collective-permute-start) | collective-permute-done | bytes 524320 | tf_op jit(solution)/shard_map/ppermute | solution.py:49
  62.3 14.2 %collective-permute-done.3 = bf16[64,2048]{1,0:T(8,128)(2,1)S(1)} collective-permute-done((bf16[64,2048]{1,0:T(8,128)(2,1)S(1)}, bf16[64,2048]{1,0:T(8,128)(2,1)S(1)}, u32[]{:S(2)}, u32[]{:S(2)}) %collective-permute-start.3) | collective-permute-done | bytes 262176 | tf_op jit(solution)/shard_map/ppermute | solution.py:49
  85.4 10.1 %collective-permute-done.5 = bf16[64,2048]{1,0:T(8,128)(2,1)S(1)} collective-permute-done((bf16[64,2048]{1,0:T(8,128)(2,1)}, bf16[64,2048]{1,0:T(8,128)(2,1)S(1)}, u32[]{:S(2)}, u32[]{:S(2)}) %collective-permute-start.5) | collective-permute-done | bytes 262176 | tf_op jit(solution)/shard_map/ppermute | solution.py:49
  96.7 37.8 %all_to_all.36 = bf16[4,64,2816]{2,1,0:T(8,128)(2,1)} all-to-all(bf16[4,64,2816]{2,1,0:T(8,128)(2,1)S(1)} %copy-done.5), channel_id=1, replica_groups=mesh['p'=4,'c'=2,'z'=4] {'z'}, dimensions={0} | all-to-all | bytes 2883584 | tf_op jit(solution)/shard_map/all_to_all | solution.py:101
  136.8 6.8 %convolution_convert_fusion.2.qkv_ref = bf16[512,1536]{1,0:T(8,128)(2,1)S(1)} fusion(bf16[512,2048]{1,0:T(8,128)(2,1)} %constant_dynamic-update-slice_fusion.25.left_ref, bf16[2048,1536]{1,0:T(8,128)(2,1)} %bitcast.83), kind=kOutput, calls=%fused_computation.2 | convolution fusion | flops 3222011904 | bytes 9961472 | tf_op jit(solution)/shard_map/dot_general | solution.py:26
  156.3 12.5 %all-to-all-done.2 = bf16[4,128,512]{1,2,0:T(8,128)(2,1)S(1)} async-done(((bf16[4,128,512]{1,2,0:T(8,128)(2,1)}), bf16[4,128,512]{1,2,0:T(8,128)(2,1)S(1)}, u32[]{:S(2)}, u32[]{:S(2)}) %all-to-all-start.2) | async-done | bytes 524320 | tf_op jit(solution)/shard_map/all_to_all | solution.py:101
  173.9 4.9 multiply_reduce_fusion.2
  181.8 14.0 %collective-permute-done.8.refs_1_ = bf16[128,2048]{1,0:T(8,128)(2,1)S(1)} collective-permute-done((bf16[128,2048]{1,0:T(8,128)(2,1)S(1)}, bf16[128,2048]{1,0:T(8,128)(2,1)S(1)}, u32[]{:S(2)}, u32[]{:S(2)}) %collective-permute-start.8) | collective-permute-done | bytes 524320 | tf_op jit(solution)/shard_map/ppermute | solution.py:49
  195.7 7.6 %collective-permute-done.9.refs_7_ = bf16[128,2048]{1,0:T(8,128)(2,1)S(1)} collective-permute-done((bf16[128,2048]{1,0:T(8,128)(2,1)}, bf16[128,2048]{1,0:T(8,128)(2,1)S(1)}, u32[]{:S(2)}, u32[]{:S(2)}) %collective-permute-start.9) | collective-permute-done | bytes 524320 | tf_op jit(solution)/shard_map/ppermute | solution.py:49
  203.3 12.1 %collective-permute-done.10.refs_2_ = bf16[128,2048]{1,0:T(8,128)(2,1)} collective-permute-done((bf16[128,2048]{1,0:T(8,128)(2,1)S(1)}, bf16[128,2048]{1,0:T(8,128)(2,1)}, u32[]{:S(2)}, u32[]{:S(2)}) %collective-permute-start.10) | collective-permute-done | bytes 524320 | tf_op jit(solution)/shard_map/ppermute | solution.py:49
  216.2 9.7 %collective-permute-done.11.refs_3_ = bf16[128,2048]{1,0:T(8,128)(2,1)} collective-permute-done((bf16[128,2048]{1,0:T(8,128)(2,1)}, bf16[128,2048]{1,0:T(8,128)(2,1)}, u32[]{:S(2)}, u32[]{:S(2)}) %collective-permute-start.11) | collective-permute-done | bytes 524320 | tf_op jit(solution)/shard_map/ppermute | solution.py:49
  229.7 20.1 %feed_units.1 = (bf16[512,1408]{1,0:T(8,128)(2,1)}, bf16[512,2816]{1,0:T(8,128)(2,1)}, bf16[512,2048]{1,0:T(8,128)(2,1)}, bf16[512,2048]{1,0:T(8,128)(2,1)}) custom-call(s32[4]{0:T(128)} %get-tuple-element.542.places_ref, bf16[128,2048]{1,0:T(8,128)(2,1)} %copy-done.29, bf16[128,2048]{1,0:T(8,128)(2,1)} %copy-done.31, ...), custom_call_target="tpu_custom_call" | custom-call | flops 10350000128 | tf_op jit(solution)/shard_map/feed_units/pallas_call | solution.py:306
  249.8 10.9 %convolution_convert_fusion.1 = bf16[512,2048]{1,0:T(8,128)(2,1)} fusion(bf16[512,2816]{1,0:T(8,128)(2,1)} %get-tuple-element.310.right_ref, bf16[2048,2816]{1,0:T(8,128)(2,1)} %bitcast.82), kind=kOutput, calls=%fused_computation.1 | convolution fusion | flops 5906628608 | bytes 16515072 | tf_op jit(solution)/shard_map/dot_general | solution.py:26
  260.7 7.9 %rows_product.7 = bf16[1024,2816]{1,0:T(8,128)(2,1)} custom-call(s32[2]{0:T(128)} %get-tuple-element.551.at_ref, bf16[512,2048]{1,0:T(8,128)(2,1)} %get-tuple-element.341.left_ref, bf16[512,2816]{1,0:T(8,128)(2,1)} %get-tuple-element.310.right_ref), custom_call_target="tpu_custom_call" | custom-call | flops 3737499904 | tf_op jit(solution)/shard_map/rows_product/pallas_call | solution.py:379
  268.9 8.1 %down_product.1 = (bf16[176,2048]{1,0:T(8,128)(2,1)}, bf16[176,2048]{1,0:T(8,128)(2,1)}, bf16[176,2048]{1,0:T(8,128)(2,1)}, bf16[176,2048]{1,0:T(8,128)(2,1)}, b...) custom-call(s32[2]{0:T(128)} %get-tuple-element.550.at_ref, ...), custom_call_target="tpu_custom_call" | custom-call | flops 4024999936 | tf_op jit(solution)/shard_map/down_product/pallas_call | solution.py:423
  278.3 6.3 %rows_product.8 = (bf16[256,1536]{1,0:T(8,128)(2,1)}, bf16[256,1536]{1,0:T(8,128)(2,1)}, bf16[256,1536]{1,0:T(8,128)(2,1)}, bf16[256,1536]{1,0:T(8,128)(2,1)}) custom-call(s32[2]{0:T(128)} %get-tuple-element.550.at_ref, bf16[512,2048]{1,0:T(8,128)(2,1)} %get-tuple-element.341.left_ref, bf16[512,2816]{1,0:T(8,128)(2,1)} %get-tuple-element.310.right_ref, ...), custom_call_target="tpu_custom_call" | custom-call | flops 3737499904 | tf_op jit(solution)/shard_map/rows_product/pallas_call | solution.py:379
  284.6 7.4 %rows_product.9 = (bf16[256,1280]{1,0:T(8,128)(2,1)}, bf16[256,1280]{1,0:T(8,128)(2,1)}, bf16[256,1280]{1,0:T(8,128)(2,1)}, bf16[256,1280]{1,0:T(8,128)(2,1)}) custom-call(s32[2]{0:T(128)} %get-tuple-element.550.at_ref, bf16[512,2048]{1,0:T(8,128)(2,1)} %get-tuple-element.341.left_ref, bf16[512,2816]{1,0:T(8,128)(2,1)} %get-tuple-element.310.right_ref, ...), custom_call_target="tpu_custom_call" | custom-call | flops 3737499904 | tf_op jit(solution)/shard_map/rows_product/pallas_call | solution.py:379
  294.0 7.9 %convolution_convert_fusion.3 = bf16[512,2048]{1,0:T(8,128)(2,1)} fusion(bf16[512,1408]{1,0:T(8,128)(2,1)} %get-tuple-element.349.left_ref, bf16[1408,2048]{1,0:T(8,128)(2,1)} %all-gather.13.cloned.1.call-done.refs_9_), kind=kOutput, calls=%fused_computation.3 | convolution fusion | flops 2953838592 | bytes 9306112 | tf_op jit(solution)/shard_map/dot_general | solution.py:26
  301.9 10.1 %collective-permute-done.13 = bf16[256,1536]{1,0:T(8,128)(2,1)} collective-permute-done((bf16[256,1536]{1,0:T(8,128)(2,1)}, bf16[256,1536]{1,0:T(8,128)(2,1)}, u32[]{:S(2)}, u32[]{:S(2)}) %collective-permute-start.13) | collective-permute-done | bytes 786464 | tf_op jit(solution)/shard_map/ppermute | solution.py:39
  319.1 8.8 %heads_product.1 = bf16[4,128,512]{2,1,0:T(8,128)(2,1)} custom-call(bf16[128,2048]{1,0:T(8,128)(2,1)} %get-tuple-element.372.x_ref, bf16[2048,2048]{1,0:T(8,128)(2,1)} %bitcast.63), custom_call_target="tpu_custom_call" | custom-call | tf_op jit(solution)/shard_map/heads_product/pallas_call | solution.py:492
  344.2 10.5 %collective-permute-done.20 = bf16[256,1280]{1,0:T(8,128)(2,1)S(1)} collective-permute-done((bf16[256,1280]{1,0:T(8,128)(2,1)}, bf16[256,1280]{1,0:T(8,128)(2,1)S(1)}, u32[]{:S(2)}, u32[]{:S(2)}) %collective-permute-start.20) | collective-permute-done | bytes 655392 | tf_op jit(solution)/shard_map/ppermute | solution.py:39
  355.4 7.0 %shard_map.213.right_ref = bf16[512,1536]{1,0:T(8,128)(2,1)S(1)} custom-call(bf16[512,1536]{1,0:T(8,128)(2,1)S(1)} %convolution_convert_fusion.2.qkv_ref, bf16[512,512]{1,0:T(8,128)(2,1)S(1)} %bitcast.57, s32[512,1]{1,0:T(8,128)S(1)} %copy.48.docs_down_ref, s32[1,512]{1,0:T(1,128)S(1)} %bitcast.61), custom_call_target="tpu_custom_call" | custom-call | tf_op jit(solution)/shard_map/pallas_call | solution.py:204
  363.6 7.5 %convolution_convert_fusion = bf16[512,2048]{1,0:T(8,128)(2,1)} fusion(bf16[512,1536]{1,0:T(8,128)(2,1)S(1)} %shard_map.213.right_ref, bf16[2048,1536]{1,0:T(8,128)(2,1)} %bitcast.84), kind=kOutput, calls=%fused_computation | convolution fusion | flops 3222274048 | bytes 9961472 | tf_op jit(solution)/shard_map/dot_general | solution.py:26
  371.1 5.7 %rows_product.10 = bf16[1024,1536]{1,0:T(8,128)(2,1)} custom-call(s32[2]{0:T(128)} %get-tuple-element.551.at_ref, bf16[512,2048]{1,0:T(8,128)(2,1)} %constant_dynamic-update-slice_fusion.25.left_ref, bf16[512,1536]{1,0:T(8,128)(2,1)} %copy-done.1), custom_call_target="tpu_custom_call" | custom-call | flops 3737499904 | tf_op jit(solution)/shard_map/rows_product/pallas_call | solution.py:379
  384.6 10.3 %collective-permute-done.23 = bf16[256,1280]{1,0:T(8,128)(2,1)S(1)} collective-permute-done((bf16[256,1280]{1,0:T(8,128)(2,1)S(1)}, bf16[256,1280]{1,0:T(8,128)(2,1)S(1)}, u32[]{:S(2)}, u32[]{:S(2)}) %collective-permute-start.23) | collective-permute-done | bytes 655392 | tf_op jit(solution)/shard_map/ppermute | solution.py:39
  395.0 6.2 %rows_product.11 = (bf16[256,1536]{1,0:T(8,128)(2,1)}, bf16[256,1536]{1,0:T(8,128)(2,1)}, bf16[256,1536]{1,0:T(8,128)(2,1)}, bf16[256,1536]{1,0:T(8,128)(2,1)}) custom-call(s32[2]{0:T(128)} %get-tuple-element.550.at_ref, bf16[512,2048]{1,0:T(8,128)(2,1)} %constant_dynamic-update-slice_fusion.25.left_ref, bf16[512,1536]{1,0:T(8,128)(2,1)} %copy-done.1, ...), custom_call_target="tpu_custom_call" | custom-call | flops 3737499904 | tf_op jit(solution)/shard_map/rows_product/pallas_call | solution.py:379
  403.8 16.0 %collective-permute-done.24 = bf16[256,1536]{1,0:T(8,128)(2,1)S(1)} collective-permute-done((bf16[256,1536]{1,0:T(8,128)(2,1)}, bf16[256,1536]{1,0:T(8,128)(2,1)S(1)}, u32[]{:S(2)}, u32[]{:S(2)}) %collective-permute-start.24) | collective-permute-done | bytes 786464 | tf_op jit(solution)/shard_map/ppermute | solution.py:39
  428.8 4.8 all-to-all-start.5
  434.4 14.3 %collective-permute-done.26 = bf16[256,1536]{1,0:T(8,128)(2,1)} collective-permute-done((bf16[256,1536]{1,0:T(8,128)(2,1)}, bf16[256,1536]{1,0:T(8,128)(2,1)}, u32[]{:S(2)}, u32[]{:S(2)}) %collective-permute-start.26) | collective-permute-done | bytes 786464 | tf_op jit(solution)/shard_map/ppermute | solution.py:39
  457.2 5.0 all-to-all-start.6
  488.0 19.9 %all-to-all-done.6 = bf16[4,64,1536]{2,1,0:T(8,128)(2,1)S(1)} async-done(((bf16[4,64,1536]{2,1,0:T(8,128)(2,1)}), bf16[4,64,1536]{2,1,0:T(8,128)(2,1)S(1)}, u32[]{:S(2)}, u32[]{:S(2)}) %all-to-all-start.6) | async-done | bytes 786464 | tf_op jit(solution)/shard_map/all_to_all | solution.py:101
  (277 shorter events, 150.9 us)
Async XLA Ops:
  7.2 50.3 %all-gather.13.cloned.1.call-start = ((), (), s32[]{:S(2)}) async-start(), calls=%async_computation.15 | async-start | bytes 6488064 | tf_op jit(solution)/shard_map/all_gather | solution.py:66
  7.9 128.8 %all-gather.15.cloned.1.call-start = ((), (), s32[]{:S(2)}) async-start(), calls=%async_computation.16 | async-start | bytes 7077888 | tf_op jit(solution)/shard_map/all_gather | solution.py:66
  37.4 136.4 %all-gather.9.cloned.1.call-start = ((), (), s32[]{:S(2)}) async-start(), calls=%async_computation.10 | async-start | bytes 9437184 | tf_op jit(solution)/shard_map/all_gather | solution.py:66
  38.6 18.9 %collective-permute-start = (bf16[128,2048]{1,0:T(8,128)(2,1)S(1)}, bf16[128,2048]{1,0:T(8,128)(2,1)S(1)}, u32[]{:S(2)}, u32[]{:S(2)}) collective-permute-start(bf16[128,2048]{1,0:T(8,128)(2,1)S(1)} %constant_dynamic-update-slice_fusion), channel_id=1, source_target_pairs={{1,3},{3,2},{2,0},{0,1},{5,7},{7,6},{6,4},{4,5},{9,11},{11,10},{10... | collective-permute-start | bytes 1572872 | tf_op jit(solution)/shard_map/ppermute | solution.py:49
  57.5 19.1 %collective-permute-start.2 = (bf16[128,2048]{1,0:T(8,128)(2,1)S(1)}, bf16[128,2048]{1,0:T(8,128)(2,1)}, u32[]{:S(2)}, u32[]{:S(2)}) collective-permute-start(bf16[128,2048]{1,0:T(8,128)(2,1)S(1)} %collective-permute-done), channel_id=1, source_target_pairs={{1,3},{3,2},{2,0},{0,1},{5,7},{7,6},{6,4},{4,5},{9,11},{11,10},{10... | collective-permute-start | bytes 1572872 | tf_op jit(solution)/shard_map/ppermute | solution.py:49
  76.6 19.0 %collective-permute-start.4 = (bf16[128,2048]{1,0:T(8,128)(2,1)}, bf16[128,2048]{1,0:T(8,128)(2,1)S(1)}, u32[]{:S(2)}, u32[]{:S(2)}) collective-permute-start(bf16[128,2048]{1,0:T(8,128)(2,1)} %collective-permute-done.2), channel_id=1, source_target_pairs={{1,3},{3,2},{2,0},{0,1},{5,7},{7,6},{6,4},{4,5},{9,11},{11,10},{10... | collective-permute-start | bytes 1572872 | tf_op jit(solution)/shard_map/ppermute | solution.py:49
  96.6 133.1 %all-gather.17.cloned.1.call-start = ((), (), s32[]{:S(2)}) async-start(), calls=%async_computation.17 | async-start | bytes 12976128 | tf_op jit(solution)/shard_map/all_gather | solution.py:66
  154.3 158.6 %reduce-scatter.4.cloned.1.call-start = ((), (), s32[]{:S(2)}) async-start(), calls=%async_computation.11 | async-start | bytes 2621440 | tf_op jit(solution)/shard_map/reduce_scatter | solution.py:622
  154.3 24.9 %collective-permute-start.7 = (bf16[128,2048]{1,0:T(8,128)(2,1)}, bf16[128,2048]{1,0:T(8,128)(2,1)}, u32[]{:S(2)}, u32[]{:S(2)}) collective-permute-start(bf16[128,2048]{1,0:T(8,128)(2,1)} %collective-permute-done.6.refs_5_), channel_id=1, source_target_pairs={{1,3},{3,2},{2,0},{0,1},{5,7},{7,6},{6,4},{4,5},{9,11},{11,10},{10... | collective-permute-start | bytes 1572872 | tf_op jit(solution)/shard_map/ppermute | solution.py:49
  180.1 23.2 %collective-permute-start.9 = (bf16[128,2048]{1,0:T(8,128)(2,1)}, bf16[128,2048]{1,0:T(8,128)(2,1)S(1)}, u32[]{:S(2)}, u32[]{:S(2)}) collective-permute-start(bf16[128,2048]{1,0:T(8,128)(2,1)} %collective-permute-done.7.refs_6_), channel_id=1, source_target_pairs={{1,3},{3,2},{2,0},{0,1},{5,7},{7,6},{6,4},{4,5},{9,11},{11,10},{10... | collective-permute-start | bytes 1572872 | tf_op jit(solution)/shard_map/ppermute | solution.py:49
  276.9 50.9 %collective-permute-start.16 = (bf16[176,2048]{1,0:T(8,128)(2,1)}, bf16[176,2048]{1,0:T(8,128)(2,1)}, u32[]{:S(2)}, u32[]{:S(2)}) collective-permute-start(bf16[176,2048]{1,0:T(8,128)(2,1)} %get-tuple-element.362), channel_id=1, source_target_pairs={{0,4},{4,0},{1,5},{5,1},{2,6},{6,2},{3,7},{7,3},{8,12},{12,8},{9,1... | collective-permute-start | bytes 2162696 | tf_op jit(solution)/shard_map/ppermute | solution.py:39
  277.2 50.7 %collective-permute-start.17 = (bf16[176,2048]{1,0:T(8,128)(2,1)}, bf16[176,2048]{1,0:T(8,128)(2,1)}, u32[]{:S(2)}, u32[]{:S(2)}) collective-permute-start(bf16[176,2048]{1,0:T(8,128)(2,1)} %get-tuple-element.363), channel_id=1, source_target_pairs={{0,4},{4,0},{1,5},{5,1},{2,6},{6,2},{3,7},{7,3},{8,12},{12,8},{9,1... | collective-permute-start | bytes 2162696 | tf_op jit(solution)/shard_map/ppermute | solution.py:39
  277.4 50.4 %collective-permute-start.18 = (bf16[176,2048]{1,0:T(8,128)(2,1)}, bf16[176,2048]{1,0:T(8,128)(2,1)}, u32[]{:S(2)}, u32[]{:S(2)}) collective-permute-start(bf16[176,2048]{1,0:T(8,128)(2,1)} %get-tuple-element.364), channel_id=1, source_target_pairs={{0,4},{4,0},{1,5},{5,1},{2,6},{6,2},{3,7},{7,3},{8,12},{12,8},{9,1... | collective-permute-start | bytes 2162696 | tf_op jit(solution)/shard_map/ppermute | solution.py:39
  292.0 20.0 %collective-permute-start.13 = (bf16[256,1536]{1,0:T(8,128)(2,1)}, bf16[256,1536]{1,0:T(8,128)(2,1)}, u32[]{:S(2)}, u32[]{:S(2)}) collective-permute-start(bf16[256,1536]{1,0:T(8,128)(2,1)} %get-tuple-element.337), channel_id=1, source_target_pairs={{0,8},{8,0},{16,24},{24,16},{1,9},{9,1},{17,25},{25,17},{2,10},{10... | collective-permute-start | bytes 2359304 | tf_op jit(solution)/shard_map/ppermute | solution.py:39
  293.4 19.7 %collective-permute-start.14 = (bf16[256,1536]{1,0:T(8,128)(2,1)}, bf16[256,1536]{1,0:T(8,128)(2,1)}, u32[]{:S(2)}, u32[]{:S(2)}) collective-permute-start(bf16[256,1536]{1,0:T(8,128)(2,1)} %get-tuple-element.338), channel_id=1, source_target_pairs={{0,16},{8,24},{16,0},{24,8},{1,17},{9,25},{17,1},{25,9},{2,18},{10... | collective-permute-start | bytes 2359304 | tf_op jit(solution)/shard_map/ppermute | solution.py:39
  314.3 24.2 %collective-permute-start.15 = (bf16[256,1536]{1,0:T(8,128)(2,1)}, bf16[256,1536]{1,0:T(8,128)(2,1)}, u32[]{:S(2)}, u32[]{:S(2)}) collective-permute-start(bf16[256,1536]{1,0:T(8,128)(2,1)} %get-tuple-element.354), channel_id=1, source_target_pairs={{0,24},{8,16},{16,8},{24,0},{1,25},{9,17},{17,9},{25,1},{2,26},{10... | collective-permute-start | bytes 2359304 | tf_op jit(solution)/shard_map/ppermute | solution.py:39
  327.9 27.6 %all-to-all-start.4 = ((bf16[4,128,512]{2,1,0:T(8,128)(2,1)}), bf16[4,128,512]{2,1,0:T(8,128)(2,1)S(1)}, u32[]{:S(2)}, u32[]{:S(2)}) async-start(bf16[4,128,512]{2,1,0:T(8,128)(2,1)} %heads_product.1), calls=%async_computation.5 | async-start | bytes 1048576 | tf_op jit(solution)/shard_map/all_to_all | solution.py:101
  331.4 92.3 %all-gather.11.cloned.1.call-start = ((), (), s32[]{:S(2)}) async-start(), calls=%async_computation.14 | async-start | bytes 2621440 | tf_op jit(solution)/shard_map/all_gather | solution.py:643
  341.0 116.2 %reduce-scatter.8.cloned.1.call-start = ((), (), s32[]{:S(2)}) async-start(), calls=%async_computation.13 | async-start | bytes 2621440 | tf_op jit(solution)/shard_map/reduce_scatter | solution.py:622
  379.8 40.9 %all-to-all-start.3 = ((bf16[4,64,1536]{2,1,0:T(8,128)(2,1)}), bf16[4,64,1536]{2,1,0:T(8,128)(2,1)S(1)}, u32[]{:S(2)}, u32[]{:S(2)}) async-start(bf16[4,64,1536]{2,1,0:T(8,128)(2,1)} %bitcast.25), calls=%async_computation.4 | async-start | bytes 1572864 | tf_op jit(solution)/shard_map/all_to_all | solution.py:101
  427.5 23.1 %collective-permute-start.27 = (bf16[256,2048]{1,0:T(8,128)(2,1)}, bf16[256,2048]{1,0:T(8,128)(2,1)}, u32[]{:S(2)}, u32[]{:S(2)}) collective-permute-start(bf16[256,2048]{1,0:T(8,128)(2,1)} %rows_product.12), channel_id=1, source_target_pairs={{0,4},{4,0},{1,5},{5,1},{2,6},{6,2},{3,7},{7,3},{8,12},{12,8},{9,1... | collective-permute-start | bytes 3145736 | tf_op jit(solution)/shard_map/ppermute | solution.py:39
  427.5 21.2 %collective-permute-start.26 = (bf16[256,1536]{1,0:T(8,128)(2,1)}, bf16[256,1536]{1,0:T(8,128)(2,1)}, u32[]{:S(2)}, u32[]{:S(2)}) collective-permute-start(bf16[256,1536]{1,0:T(8,128)(2,1)} %get-tuple-element.444), channel_id=1, source_target_pairs={{0,24},{8,16},{16,8},{24,0},{1,25},{9,17},{17,9},{25,1},{2,26},{10... | collective-permute-start | bytes 2359304 | tf_op jit(solution)/shard_map/ppermute | solution.py:39
  428.8 28.4 %all-to-all-start.5 = ((bf16[4,64,1280]{2,1,0:T(8,128)(2,1)}), bf16[4,64,1280]{2,1,0:T(8,128)(2,1)S(1)}, u32[]{:S(2)}, u32[]{:S(2)}) async-start(bf16[4,64,1280]{2,1,0:T(8,128)(2,1)} %bitcast.27), calls=%async_computation.8 | async-start | bytes 1310720 | tf_op jit(solution)/shard_map/all_to_all | solution.py:101
  433.6 87.5 %reduce-scatter.6.cloned.1.call-start = ((), (), s32[]{:S(2)}) async-start(), calls=%async_computation.12 | async-start | bytes 2621440 | tf_op jit(solution)/shard_map/reduce_scatter | solution.py:622
  448.7 25.8 %collective-permute-start.38 = (bf16[176,2048]{1,0:T(8,128)(2,1)}, bf16[176,2048]{1,0:T(8,128)(2,1)}, u32[]{:S(2)}, u32[]{:S(2)}) collective-permute-start(bf16[176,2048]{1,0:T(8,128)(2,1)} %add_convert_fusion.4), channel_id=1, source_target_pairs={{0,8},{8,0},{16,24},{24,16},{1,9},{9,1},{17,25},{25,17},{2,10},{10... | collective-permute-start | bytes 2162696 | tf_op jit(solution)/shard_map/ppermute | solution.py:39
  449.4 29.0 %collective-permute-start.39 = (bf16[176,2048]{1,0:T(8,128)(2,1)}, bf16[176,2048]{1,0:T(8,128)(2,1)}, u32[]{:S(2)}, u32[]{:S(2)}) collective-permute-start(bf16[176,2048]{1,0:T(8,128)(2,1)} %add_convert_fusion.3), channel_id=1, source_target_pairs={{0,16},{8,24},{16,0},{24,8},{1,17},{9,25},{17,1},{25,9},{2,18},{10... | collective-permute-start | bytes 2162696 | tf_op jit(solution)/shard_map/ppermute | solution.py:39
  457.2 50.7 %all-to-all-start.6 = ((bf16[4,64,1536]{2,1,0:T(8,128)(2,1)}), bf16[4,64,1536]{2,1,0:T(8,128)(2,1)S(1)}, u32[]{:S(2)}, u32[]{:S(2)}) async-start(bf16[4,64,1536]{2,1,0:T(8,128)(2,1)} %bitcast.30), calls=%async_computation.9 | async-start | bytes 1572864 | tf_op jit(solution)/shard_map/all_to_all | solution.py:101
  474.5 45.3 %collective-permute-start.34 = (f32[2,2048]{1,0:T(2,128)S(1)}, f32[2,2048]{1,0:T(2,128)S(1)}, u32[]{:S(2)}, u32[]{:S(2)}) collective-permute-start(f32[2,2048]{1,0:T(2,128)S(1)} %add_add_fusion.1), channel_id=1, source_target_pairs={{0,3},{1,2},{2,1},{3,0},{4,7},{5,6},{6,5},{7,4},{8,11},{9,10},{10,... | collective-permute-start | bytes 49160 | tf_op jit(solution)/shard_map/ppermute | solution.py:39
  478.4 41.4 %collective-permute-start.33 = (f32[2,2048]{1,0:T(2,128)S(1)}, f32[2,2048]{1,0:T(2,128)S(1)}, u32[]{:S(2)}, u32[]{:S(2)}) collective-permute-start(f32[2,2048]{1,0:T(2,128)S(1)} %add_add_fusion.1), channel_id=1, source_target_pairs={{0,2},{1,3},{2,0},{3,1},{4,6},{5,7},{6,4},{7,5},{8,10},{9,11},{10,... | collective-permute-start | bytes 49160 | tf_op jit(solution)/shard_map/ppermute | solution.py:39
  480.2 39.6 %collective-permute-start.32 = (f32[2,2048]{1,0:T(2,128)S(1)}, f32[2,2048]{1,0:T(2,128)S(1)}, u32[]{:S(2)}, u32[]{:S(2)}) collective-permute-start(f32[2,2048]{1,0:T(2,128)S(1)} %add_add_fusion.1), channel_id=1, source_target_pairs={{0,1},{1,0},{2,3},{3,2},{4,5},{5,4},{6,7},{7,6},{8,9},{9,8},{10,11... | collective-permute-start | bytes 49160 | tf_op jit(solution)/shard_map/ppermute | solution.py:39
  485.3 28.8 %collective-permute-start.41 = (bf16[176,2048]{1,0:T(8,128)(2,1)}, bf16[176,2048]{1,0:T(8,128)(2,1)S(1)}, u32[]{:S(2)}, u32[]{:S(2)}) collective-permute-start(bf16[176,2048]{1,0:T(8,128)(2,1)} %add_convert_fusion.2), channel_id=1, source_target_pairs={{0,24},{8,16},{16,8},{24,0},{1,25},{9,17},{17,9},{25,1},{2,26},{10... | collective-permute-start | bytes 2162696 | tf_op jit(solution)/shard_map/ppermute | solution.py:39
  486.6 30.8 %collective-permute-start.40 = (bf16[64,2048]{1,0:T(8,128)(2,1)S(1)}, bf16[64,2048]{1,0:T(8,128)(2,1)}, u32[]{:S(2)}, u32[]{:S(2)}) collective-permute-start(bf16[64,2048]{1,0:T(8,128)(2,1)S(1)} %add_convert_fusion.7), channel_id=1, source_target_pairs={{0,0},{1,8},{2,16},{3,24},{8,1},{9,9},{10,17},{11,25},{16,2},{17,1... | collective-permute-start | bytes 786440 | tf_op jit(solution)/shard_map/ppermute | solution.py:700
  (60 other events, 761.9 us)
Sparse Core Ops, SparseCore 0:
  9.9 46.0 all-gather.12
  57.8 45.5 all-gather.14
  105.9 54.3 all-gather.8
  162.0 67.6 all-gather.16
  269.0 43.8 reduce-scatter.3
  341.1 46.0 all-gather.10
  389.6 46.5 reduce-scatter.7
  438.5 67.8 reduce-scatter.5

commit v5 on v4

--- a/solution.py
+++ b/solution.py
@@ -700,6 +700,8 @@
     grad_w_out = lax.ppermute(
         grad_w_out, ("p", "z"), [(i * nz + j, j * nz + i) for i in range(n) for j in range(nz)]
     )
+    grad_w_gate, grad_w_up = line(lambda x, y: collect(x, y, pieces), grad_first, grad_second)
+
     def three_piece(x):
         return [
             x[:, :, i * feats : (i + 1) * feats]
@@ -711,7 +713,6 @@
 
     grad_w_query, grad_w_key, grad_w_value = line(three_piece, grad_qkv)
 
-    grad_w_gate, grad_w_up = line(lambda x, y: collect(x, y, pieces), grad_first, grad_second)
     grad_w_down = line(
         lambda own, other, came: summed(plus(own[0], other[0]), *came),
         down_own,

time: 540 us -> 536 us (level)
  transfers between devices with their start and end apart: 55 -> 55, of which waited for: 25 -> 26; matrix products, arithmetic and copies ran while one was open for 15% -> 15% of each run, Pallas kernels for 13% -> 13%
where the time goes in v5:
time: 536 us; the launch traced here: 526 us
  waiting for transfers between devices  186 us (35%)
  Pallas kernels  94.8 us (18%)
  starting transfers between devices  64.9 us (12%)
  blocking collectives  64.2 us (12%)
  matrix products  38.1 us (7%)
  other arithmetic  30.4 us (6%)
  local copies, waits for them, and re-layouts  26.5 us (5%)
  between operations  20.7 us (4%)
    ppermute x12, waiting for transfers between devices, hop(): lax.ppermute(x, 'z', [(order[i], order[(i + 1) % n]) for i in range(n)])  79.3 us
    ppermute x29, waiting for transfers between devices, cross(): return lax.ppermute(x, axis, [(i, i ^ by) for i in range(n)])  71.1 us
    all_to_all x2, blocking collectives, exchange(): return lax.all_to_all(x, 'z', 0, 0, tiled=True)  64.2 us
    pallas_call x7, Pallas kernels, rows_product(): pl.pallas_call(functools.partial(rows_kernel, n, mode), grid_spec=pltpu.P...  41.5 us
    dot_general x5, matrix products, dot(): lax.dot_general(left, right, (dims, ((), ())), preferred_element_type=f32)  38.1 us
    all_to_all x5, waiting for transfers between devices, exchange(): return lax.all_to_all(x, 'z', 0, 0, tiled=True)  29.7 us
    ppermute x29, starting transfers between devices, cross(): return lax.ppermute(x, axis, [(i, i ^ by) for i in range(n)])  29.5 us
    all_to_all x5, starting transfers between devices, exchange(): return lax.all_to_all(x, 'z', 0, 0, tiled=True)  21.7 us
  transfers between devices with their start and end apart: 55, of which 26 were waited for; matrix products, arithmetic and copies ran while one was open for 15% of the time, Pallas kernels for 13%

profile of v5, /device:TPU:0, one launch (start us, length us, event | category | flops | bytes accessed | tf_op | source)
XLA Modules:
  0.0 526.0 jit_solution(8715975208654174280)
XLA Ops:
  11.0 26.5 %all_to_all.35 = bf16[4,64,1536]{2,1,0:T(8,128)(2,1)} all-to-all(bf16[4,64,1536]{2,1,0:T(8,128)(2,1)S(1)} %copy.47), channel_id=1, replica_groups=mesh['p'=4,'c'=2,'z'=4] {'z'}, dimensions={0} | all-to-all | bytes 1572864 | tf_op jit(solution)/shard_map/all_to_all | solution.py:101
  49.5 8.0 %collective-permute-done = bf16[128,2048]{1,0:T(8,128)(2,1)S(1)} collective-permute-done((bf16[128,2048]{1,0:T(8,128)(2,1)S(1)}, bf16[128,2048]{1,0:T(8,128)(2,1)S(1)}, u32[]{:S(2)}, u32[]{:S(2)}) %collective-permute-start) | collective-permute-done | bytes 524320 | tf_op jit(solution)/shard_map/ppermute | solution.py:49
  62.3 14.2 %collective-permute-done.3 = bf16[64,2048]{1,0:T(8,128)(2,1)S(1)} collective-permute-done((bf16[64,2048]{1,0:T(8,128)(2,1)S(1)}, bf16[64,2048]{1,0:T(8,128)(2,1)S(1)}, u32[]{:S(2)}, u32[]{:S(2)}) %collective-permute-start.3) | collective-permute-done | bytes 262176 | tf_op jit(solution)/shard_map/ppermute | solution.py:49
  85.4 10.1 %collective-permute-done.5 = bf16[64,2048]{1,0:T(8,128)(2,1)S(1)} collective-permute-done((bf16[64,2048]{1,0:T(8,128)(2,1)}, bf16[64,2048]{1,0:T(8,128)(2,1)S(1)}, u32[]{:S(2)}, u32[]{:S(2)}) %collective-permute-start.5) | collective-permute-done | bytes 262176 | tf_op jit(solution)/shard_map/ppermute | solution.py:49
  96.7 37.8 %all_to_all.36 = bf16[4,64,2816]{2,1,0:T(8,128)(2,1)} all-to-all(bf16[4,64,2816]{2,1,0:T(8,128)(2,1)S(1)} %copy-done.5), channel_id=1, replica_groups=mesh['p'=4,'c'=2,'z'=4] {'z'}, dimensions={0} | all-to-all | bytes 2883584 | tf_op jit(solution)/shard_map/all_to_all | solution.py:101
  136.8 6.8 %convolution_convert_fusion.2.qkv_ref = bf16[512,1536]{1,0:T(8,128)(2,1)S(1)} fusion(bf16[512,2048]{1,0:T(8,128)(2,1)} %constant_dynamic-update-slice_fusion.25.left_ref, bf16[2048,1536]{1,0:T(8,128)(2,1)} %bitcast.83), kind=kOutput, calls=%fused_computation.2 | convolution fusion | flops 3222011904 | bytes 9961472 | tf_op jit(solution)/shard_map/dot_general | solution.py:26
  156.3 12.5 %all-to-all-done.2 = bf16[4,128,512]{1,2,0:T(8,128)(2,1)S(1)} async-done(((bf16[4,128,512]{1,2,0:T(8,128)(2,1)}), bf16[4,128,512]{1,2,0:T(8,128)(2,1)S(1)}, u32[]{:S(2)}, u32[]{:S(2)}) %all-to-all-start.2) | async-done | bytes 524320 | tf_op jit(solution)/shard_map/all_to_all | solution.py:101
  173.9 4.9 multiply_reduce_fusion.2
  181.8 13.9 %collective-permute-done.8.refs_1_ = bf16[128,2048]{1,0:T(8,128)(2,1)S(1)} collective-permute-done((bf16[128,2048]{1,0:T(8,128)(2,1)S(1)}, bf16[128,2048]{1,0:T(8,128)(2,1)S(1)}, u32[]{:S(2)}, u32[]{:S(2)}) %collective-permute-start.8) | collective-permute-done | bytes 524320 | tf_op jit(solution)/shard_map/ppermute | solution.py:49
  195.7 7.6 %collective-permute-done.9.refs_7_ = bf16[128,2048]{1,0:T(8,128)(2,1)S(1)} collective-permute-done((bf16[128,2048]{1,0:T(8,128)(2,1)}, bf16[128,2048]{1,0:T(8,128)(2,1)S(1)}, u32[]{:S(2)}, u32[]{:S(2)}) %collective-permute-start.9) | collective-permute-done | bytes 524320 | tf_op jit(solution)/shard_map/ppermute | solution.py:49
  203.3 12.1 %collective-permute-done.10.refs_2_ = bf16[128,2048]{1,0:T(8,128)(2,1)} collective-permute-done((bf16[128,2048]{1,0:T(8,128)(2,1)S(1)}, bf16[128,2048]{1,0:T(8,128)(2,1)}, u32[]{:S(2)}, u32[]{:S(2)}) %collective-permute-start.10) | collective-permute-done | bytes 524320 | tf_op jit(solution)/shard_map/ppermute | solution.py:49
  216.1 9.8 %collective-permute-done.11.refs_3_ = bf16[128,2048]{1,0:T(8,128)(2,1)} collective-permute-done((bf16[128,2048]{1,0:T(8,128)(2,1)}, bf16[128,2048]{1,0:T(8,128)(2,1)}, u32[]{:S(2)}, u32[]{:S(2)}) %collective-permute-start.11) | collective-permute-done | bytes 524320 | tf_op jit(solution)/shard_map/ppermute | solution.py:49
  229.7 20.0 %feed_units.1 = (bf16[512,1408]{1,0:T(8,128)(2,1)}, bf16[512,2816]{1,0:T(8,128)(2,1)}, bf16[512,2048]{1,0:T(8,128)(2,1)}, bf16[512,2048]{1,0:T(8,128)(2,1)}) custom-call(s32[4]{0:T(128)} %get-tuple-element.542.places_ref, bf16[128,2048]{1,0:T(8,128)(2,1)} %copy-done.30, bf16[128,2048]{1,0:T(8,128)(2,1)} %copy-done.32, ...), custom_call_target="tpu_custom_call" | custom-call | flops 10350000128 | tf_op jit(solution)/shard_map/feed_units/pallas_call | solution.py:306
  249.8 10.9 %convolution_convert_fusion.1 = bf16[512,2048]{1,0:T(8,128)(2,1)} fusion(bf16[512,2816]{1,0:T(8,128)(2,1)} %get-tuple-element.310.right_ref, bf16[2048,2816]{1,0:T(8,128)(2,1)} %bitcast.82), kind=kOutput, calls=%fused_computation.1 | convolution fusion | flops 5906628608 | bytes 16515072 | tf_op jit(solution)/shard_map/dot_general | solution.py:26
  260.6 8.0 %rows_product.7 = bf16[1024,2816]{1,0:T(8,128)(2,1)} custom-call(s32[2]{0:T(128)} %get-tuple-element.551.at_ref, bf16[512,2048]{1,0:T(8,128)(2,1)} %get-tuple-element.341.left_ref, bf16[512,2816]{1,0:T(8,128)(2,1)} %get-tuple-element.310.right_ref), custom_call_target="tpu_custom_call" | custom-call | flops 3737499904 | tf_op jit(solution)/shard_map/rows_product/pallas_call | solution.py:379
  268.9 8.0 %down_product.1 = (bf16[176,2048]{1,0:T(8,128)(2,1)}, bf16[176,2048]{1,0:T(8,128)(2,1)}, bf16[176,2048]{1,0:T(8,128)(2,1)}, bf16[176,2048]{1,0:T(8,128)(2,1)}, b...) custom-call(s32[2]{0:T(128)} %get-tuple-element.550.at_ref, ...), custom_call_target="tpu_custom_call" | custom-call | flops 4024999936 | tf_op jit(solution)/shard_map/down_product/pallas_call | solution.py:423
  278.4 6.3 %rows_product.8 = (bf16[256,1536]{1,0:T(8,128)(2,1)}, bf16[256,1536]{1,0:T(8,128)(2,1)}, bf16[256,1536]{1,0:T(8,128)(2,1)}, bf16[256,1536]{1,0:T(8,128)(2,1)}) custom-call(s32[2]{0:T(128)} %get-tuple-element.550.at_ref, bf16[512,2048]{1,0:T(8,128)(2,1)} %get-tuple-element.341.left_ref, bf16[512,2816]{1,0:T(8,128)(2,1)} %get-tuple-element.310.right_ref, ...), custom_call_target="tpu_custom_call" | custom-call | flops 3737499904 | tf_op jit(solution)/shard_map/rows_product/pallas_call | solution.py:379
  284.6 7.4 %rows_product.9 = (bf16[256,1280]{1,0:T(8,128)(2,1)}, bf16[256,1280]{1,0:T(8,128)(2,1)}, bf16[256,1280]{1,0:T(8,128)(2,1)}, bf16[256,1280]{1,0:T(8,128)(2,1)}) custom-call(s32[2]{0:T(128)} %get-tuple-element.550.at_ref, bf16[512,2048]{1,0:T(8,128)(2,1)} %get-tuple-element.341.left_ref, bf16[512,2816]{1,0:T(8,128)(2,1)} %get-tuple-element.310.right_ref, ...), custom_call_target="tpu_custom_call" | custom-call | flops 3737499904 | tf_op jit(solution)/shard_map/rows_product/pallas_call | solution.py:379
  294.1 7.9 %convolution_convert_fusion.3 = bf16[512,2048]{1,0:T(8,128)(2,1)} fusion(bf16[512,1408]{1,0:T(8,128)(2,1)} %get-tuple-element.349.left_ref, bf16[1408,2048]{1,0:T(8,128)(2,1)} %all-gather.13.cloned.1.call-done.refs_9_), kind=kOutput, calls=%fused_computation.3 | convolution fusion | flops 2953838592 | bytes 9306112 | tf_op jit(solution)/shard_map/dot_general | solution.py:26
  302.0 10.1 %collective-permute-done.13 = bf16[256,1536]{1,0:T(8,128)(2,1)} collective-permute-done((bf16[256,1536]{1,0:T(8,128)(2,1)}, bf16[256,1536]{1,0:T(8,128)(2,1)}, u32[]{:S(2)}, u32[]{:S(2)}) %collective-permute-start.13) | collective-permute-done | bytes 786464 | tf_op jit(solution)/shard_map/ppermute | solution.py:39
  319.1 8.8 %heads_product.1 = bf16[4,128,512]{2,1,0:T(8,128)(2,1)} custom-call(bf16[128,2048]{1,0:T(8,128)(2,1)} %get-tuple-element.372.x_ref, bf16[2048,2048]{1,0:T(8,128)(2,1)} %bitcast.63), custom_call_target="tpu_custom_call" | custom-call | tf_op jit(solution)/shard_map/heads_product/pallas_call | solution.py:492
  344.3 10.5 %collective-permute-done.20 = bf16[256,1280]{1,0:T(8,128)(2,1)S(1)} collective-permute-done((bf16[256,1280]{1,0:T(8,128)(2,1)}, bf16[256,1280]{1,0:T(8,128)(2,1)S(1)}, u32[]{:S(2)}, u32[]{:S(2)}) %collective-permute-start.20) | collective-permute-done | bytes 655392 | tf_op jit(solution)/shard_map/ppermute | solution.py:39
  355.5 7.0 %shard_map.213.right_ref = bf16[512,1536]{1,0:T(8,128)(2,1)S(1)} custom-call(bf16[512,1536]{1,0:T(8,128)(2,1)S(1)} %convolution_convert_fusion.2.qkv_ref, bf16[512,512]{1,0:T(8,128)(2,1)S(1)} %bitcast.57, s32[512,1]{1,0:T(8,128)S(1)} %copy.48.docs_down_ref, s32[1,512]{1,0:T(1,128)S(1)} %bitcast.61), custom_call_target="tpu_custom_call" | custom-call | tf_op jit(solution)/shard_map/pallas_call | solution.py:204
  363.7 7.5 %convolution_convert_fusion = bf16[512,2048]{1,0:T(8,128)(2,1)} fusion(bf16[512,1536]{1,0:T(8,128)(2,1)S(1)} %shard_map.213.right_ref, bf16[2048,1536]{1,0:T(8,128)(2,1)} %bitcast.84), kind=kOutput, calls=%fused_computation | convolution fusion | flops 3222274048 | bytes 9961472 | tf_op jit(solution)/shard_map/dot_general | solution.py:26
  371.2 5.6 %rows_product.10 = bf16[1024,1536]{1,0:T(8,128)(2,1)} custom-call(s32[2]{0:T(128)} %get-tuple-element.551.at_ref, bf16[512,2048]{1,0:T(8,128)(2,1)} %constant_dynamic-update-slice_fusion.25.left_ref, bf16[512,1536]{1,0:T(8,128)(2,1)} %copy-done.1), custom_call_target="tpu_custom_call" | custom-call | flops 3737499904 | tf_op jit(solution)/shard_map/rows_product/pallas_call | solution.py:379
  384.6 10.3 %collective-permute-done.23 = bf16[256,1280]{1,0:T(8,128)(2,1)S(1)} collective-permute-done((bf16[256,1280]{1,0:T(8,128)(2,1)S(1)}, bf16[256,1280]{1,0:T(8,128)(2,1)S(1)}, u32[]{:S(2)}, u32[]{:S(2)}) %collective-permute-start.23) | collective-permute-done | bytes 655392 | tf_op jit(solution)/shard_map/ppermute | solution.py:39
  395.0 6.2 %rows_product.11 = (bf16[256,1536]{1,0:T(8,128)(2,1)}, bf16[256,1536]{1,0:T(8,128)(2,1)}, bf16[256,1536]{1,0:T(8,128)(2,1)}, bf16[256,1536]{1,0:T(8,128)(2,1)}) custom-call(s32[2]{0:T(128)} %get-tuple-element.550.at_ref, bf16[512,2048]{1,0:T(8,128)(2,1)} %constant_dynamic-update-slice_fusion.25.left_ref, bf16[512,1536]{1,0:T(8,128)(2,1)} %copy-done.1, ...), custom_call_target="tpu_custom_call" | custom-call | flops 3737499904 | tf_op jit(solution)/shard_map/rows_product/pallas_call | solution.py:379
  403.8 16.0 %collective-permute-done.24 = bf16[256,1536]{1,0:T(8,128)(2,1)S(1)} collective-permute-done((bf16[256,1536]{1,0:T(8,128)(2,1)}, bf16[256,1536]{1,0:T(8,128)(2,1)S(1)}, u32[]{:S(2)}, u32[]{:S(2)}) %collective-permute-start.24) | collective-permute-done | bytes 786464 | tf_op jit(solution)/shard_map/ppermute | solution.py:39
  428.8 4.8 all-to-all-start.5
  434.4 14.2 %collective-permute-done.26 = bf16[256,1536]{1,0:T(8,128)(2,1)} collective-permute-done((bf16[256,1536]{1,0:T(8,128)(2,1)}, bf16[256,1536]{1,0:T(8,128)(2,1)}, u32[]{:S(2)}, u32[]{:S(2)}) %collective-permute-start.26) | collective-permute-done | bytes 786464 | tf_op jit(solution)/shard_map/ppermute | solution.py:39
  457.2 5.0 all-to-all-start.6
  490.8 17.2 %all-to-all-done.6 = bf16[4,64,1536]{2,1,0:T(8,128)(2,1)S(1)} async-done(((bf16[4,64,1536]{2,1,0:T(8,128)(2,1)}), bf16[4,64,1536]{2,1,0:T(8,128)(2,1)S(1)}, u32[]{:S(2)}, u32[]{:S(2)}) %all-to-all-start.6) | async-done | bytes 786464 | tf_op jit(solution)/shard_map/all_to_all | solution.py:101
  (279 shorter events, 149.3 us)
Async XLA Ops:
  7.2 50.3 %all-gather.13.cloned.1.call-start = ((), (), s32[]{:S(2)}) async-start(), calls=%async_computation.15 | async-start | bytes 6488064 | tf_op jit(solution)/shard_map/all_gather | solution.py:66
  7.9 128.9 %all-gather.15.cloned.1.call-start = ((), (), s32[]{:S(2)}) async-start(), calls=%async_computation.16 | async-start | bytes 7077888 | tf_op jit(solution)/shard_map/all_gather | solution.py:66
  37.4 136.4 %all-gather.9.cloned.1.call-start = ((), (), s32[]{:S(2)}) async-start(), calls=%async_computation.10 | async-start | bytes 9437184 | tf_op jit(solution)/shard_map/all_gather | solution.py:66
  38.6 18.9 %collective-permute-start = (bf16[128,2048]{1,0:T(8,128)(2,1)S(1)}, bf16[128,2048]{1,0:T(8,128)(2,1)S(1)}, u32[]{:S(2)}, u32[]{:S(2)}) collective-permute-start(bf16[128,2048]{1,0:T(8,128)(2,1)S(1)} %constant_dynamic-update-slice_fusion), channel_id=1, source_target_pairs={{1,3},{3,2},{2,0},{0,1},{5,7},{7,6},{6,4},{4,5},{9,11},{11,10},{10... | collective-permute-start | bytes 1572872 | tf_op jit(solution)/shard_map/ppermute | solution.py:49
  57.5 19.1 %collective-permute-start.2 = (bf16[128,2048]{1,0:T(8,128)(2,1)S(1)}, bf16[128,2048]{1,0:T(8,128)(2,1)}, u32[]{:S(2)}, u32[]{:S(2)}) collective-permute-start(bf16[128,2048]{1,0:T(8,128)(2,1)S(1)} %collective-permute-done), channel_id=1, source_target_pairs={{1,3},{3,2},{2,0},{0,1},{5,7},{7,6},{6,4},{4,5},{9,11},{11,10},{10... | collective-permute-start | bytes 1572872 | tf_op jit(solution)/shard_map/ppermute | solution.py:49
  76.6 19.0 %collective-permute-start.4 = (bf16[128,2048]{1,0:T(8,128)(2,1)}, bf16[128,2048]{1,0:T(8,128)(2,1)S(1)}, u32[]{:S(2)}, u32[]{:S(2)}) collective-permute-start(bf16[128,2048]{1,0:T(8,128)(2,1)} %collective-permute-done.2), channel_id=1, source_target_pairs={{1,3},{3,2},{2,0},{0,1},{5,7},{7,6},{6,4},{4,5},{9,11},{11,10},{10... | collective-permute-start | bytes 1572872 | tf_op jit(solution)/shard_map/ppermute | solution.py:49
  96.6 133.1 %all-gather.17.cloned.1.call-start = ((), (), s32[]{:S(2)}) async-start(), calls=%async_computation.17 | async-start | bytes 12976128 | tf_op jit(solution)/shard_map/all_gather | solution.py:66
  154.3 158.6 %reduce-scatter.4.cloned.1.call-start = ((), (), s32[]{:S(2)}) async-start(), calls=%async_computation.11 | async-start | bytes 2621440 | tf_op jit(solution)/shard_map/reduce_scatter | solution.py:622
  154.3 24.9 %collective-permute-start.7 = (bf16[128,2048]{1,0:T(8,128)(2,1)}, bf16[128,2048]{1,0:T(8,128)(2,1)}, u32[]{:S(2)}, u32[]{:S(2)}) collective-permute-start(bf16[128,2048]{1,0:T(8,128)(2,1)} %collective-permute-done.6.refs_5_), channel_id=1, source_target_pairs={{1,3},{3,2},{2,0},{0,1},{5,7},{7,6},{6,4},{4,5},{9,11},{11,10},{10... | collective-permute-start | bytes 1572872 | tf_op jit(solution)/shard_map/ppermute | solution.py:49
  180.1 23.2 %collective-permute-start.9 = (bf16[128,2048]{1,0:T(8,128)(2,1)}, bf16[128,2048]{1,0:T(8,128)(2,1)S(1)}, u32[]{:S(2)}, u32[]{:S(2)}) collective-permute-start(bf16[128,2048]{1,0:T(8,128)(2,1)} %collective-permute-done.7.refs_6_), channel_id=1, source_target_pairs={{1,3},{3,2},{2,0},{0,1},{5,7},{7,6},{6,4},{4,5},{9,11},{11,10},{10... | collective-permute-start | bytes 1572872 | tf_op jit(solution)/shard_map/ppermute | solution.py:49
  276.9 50.9 %collective-permute-start.16 = (bf16[176,2048]{1,0:T(8,128)(2,1)}, bf16[176,2048]{1,0:T(8,128)(2,1)}, u32[]{:S(2)}, u32[]{:S(2)}) collective-permute-start(bf16[176,2048]{1,0:T(8,128)(2,1)} %get-tuple-element.362), channel_id=1, source_target_pairs={{0,4},{4,0},{1,5},{5,1},{2,6},{6,2},{3,7},{7,3},{8,12},{12,8},{9,1... | collective-permute-start | bytes 2162696 | tf_op jit(solution)/shard_map/ppermute | solution.py:39
  277.2 50.7 %collective-permute-start.17 = (bf16[176,2048]{1,0:T(8,128)(2,1)}, bf16[176,2048]{1,0:T(8,128)(2,1)}, u32[]{:S(2)}, u32[]{:S(2)}) collective-permute-start(bf16[176,2048]{1,0:T(8,128)(2,1)} %get-tuple-element.363), channel_id=1, source_target_pairs={{0,4},{4,0},{1,5},{5,1},{2,6},{6,2},{3,7},{7,3},{8,12},{12,8},{9,1... | collective-permute-start | bytes 2162696 | tf_op jit(solution)/shard_map/ppermute | solution.py:39
  277.4 50.4 %collective-permute-start.18 = (bf16[176,2048]{1,0:T(8,128)(2,1)}, bf16[176,2048]{1,0:T(8,128)(2,1)}, u32[]{:S(2)}, u32[]{:S(2)}) collective-permute-start(bf16[176,2048]{1,0:T(8,128)(2,1)} %get-tuple-element.364), channel_id=1, source_target_pairs={{0,4},{4,0},{1,5},{5,1},{2,6},{6,2},{3,7},{7,3},{8,12},{12,8},{9,1... | collective-permute-start | bytes 2162696 | tf_op jit(solution)/shard_map/ppermute | solution.py:39
  292.0 20.0 %collective-permute-start.13 = (bf16[256,1536]{1,0:T(8,128)(2,1)}, bf16[256,1536]{1,0:T(8,128)(2,1)}, u32[]{:S(2)}, u32[]{:S(2)}) collective-permute-start(bf16[256,1536]{1,0:T(8,128)(2,1)} %get-tuple-element.337), channel_id=1, source_target_pairs={{0,8},{8,0},{16,24},{24,16},{1,9},{9,1},{17,25},{25,17},{2,10},{10... | collective-permute-start | bytes 2359304 | tf_op jit(solution)/shard_map/ppermute | solution.py:39
  293.5 19.7 %collective-permute-start.14 = (bf16[256,1536]{1,0:T(8,128)(2,1)}, bf16[256,1536]{1,0:T(8,128)(2,1)}, u32[]{:S(2)}, u32[]{:S(2)}) collective-permute-start(bf16[256,1536]{1,0:T(8,128)(2,1)} %get-tuple-element.338), channel_id=1, source_target_pairs={{0,16},{8,24},{16,0},{24,8},{1,17},{9,25},{17,1},{25,9},{2,18},{10... | collective-permute-start | bytes 2359304 | tf_op jit(solution)/shard_map/ppermute | solution.py:39
  314.4 24.2 %collective-permute-start.15 = (bf16[256,1536]{1,0:T(8,128)(2,1)}, bf16[256,1536]{1,0:T(8,128)(2,1)}, u32[]{:S(2)}, u32[]{:S(2)}) collective-permute-start(bf16[256,1536]{1,0:T(8,128)(2,1)} %get-tuple-element.354), channel_id=1, source_target_pairs={{0,24},{8,16},{16,8},{24,0},{1,25},{9,17},{17,9},{25,1},{2,26},{10... | collective-permute-start | bytes 2359304 | tf_op jit(solution)/shard_map/ppermute | solution.py:39
  327.9 27.6 %all-to-all-start.4 = ((bf16[4,128,512]{2,1,0:T(8,128)(2,1)}), bf16[4,128,512]{2,1,0:T(8,128)(2,1)S(1)}, u32[]{:S(2)}, u32[]{:S(2)}) async-start(bf16[4,128,512]{2,1,0:T(8,128)(2,1)} %heads_product.1), calls=%async_computation.5 | async-start | bytes 1048576 | tf_op jit(solution)/shard_map/all_to_all | solution.py:101
  331.5 92.2 %all-gather.11.cloned.1.call-start = ((), (), s32[]{:S(2)}) async-start(), calls=%async_computation.14 | async-start | bytes 2621440 | tf_op jit(solution)/shard_map/all_gather | solution.py:643
  341.1 116.1 %reduce-scatter.8.cloned.1.call-start = ((), (), s32[]{:S(2)}) async-start(), calls=%async_computation.13 | async-start | bytes 2621440 | tf_op jit(solution)/shard_map/reduce_scatter | solution.py:622
  379.8 40.9 %all-to-all-start.3 = ((bf16[4,64,1536]{2,1,0:T(8,128)(2,1)}), bf16[4,64,1536]{2,1,0:T(8,128)(2,1)S(1)}, u32[]{:S(2)}, u32[]{:S(2)}) async-start(bf16[4,64,1536]{2,1,0:T(8,128)(2,1)} %bitcast.25), calls=%async_computation.4 | async-start | bytes 1572864 | tf_op jit(solution)/shard_map/all_to_all | solution.py:101
  427.5 23.1 %collective-permute-start.27 = (bf16[256,2048]{1,0:T(8,128)(2,1)}, bf16[256,2048]{1,0:T(8,128)(2,1)}, u32[]{:S(2)}, u32[]{:S(2)}) collective-permute-start(bf16[256,2048]{1,0:T(8,128)(2,1)} %rows_product.12), channel_id=1, source_target_pairs={{0,4},{4,0},{1,5},{5,1},{2,6},{6,2},{3,7},{7,3},{8,12},{12,8},{9,1... | collective-permute-start | bytes 3145736 | tf_op jit(solution)/shard_map/ppermute | solution.py:39
  427.5 21.2 %collective-permute-start.26 = (bf16[256,1536]{1,0:T(8,128)(2,1)}, bf16[256,1536]{1,0:T(8,128)(2,1)}, u32[]{:S(2)}, u32[]{:S(2)}) collective-permute-start(bf16[256,1536]{1,0:T(8,128)(2,1)} %get-tuple-element.444), channel_id=1, source_target_pairs={{0,24},{8,16},{16,8},{24,0},{1,25},{9,17},{17,9},{25,1},{2,26},{10... | collective-permute-start | bytes 2359304 | tf_op jit(solution)/shard_map/ppermute | solution.py:39
  428.8 28.4 %all-to-all-start.5 = ((bf16[4,64,1280]{2,1,0:T(8,128)(2,1)}), bf16[4,64,1280]{2,1,0:T(8,128)(2,1)S(1)}, u32[]{:S(2)}, u32[]{:S(2)}) async-start(bf16[4,64,1280]{2,1,0:T(8,128)(2,1)} %bitcast.27), calls=%async_computation.8 | async-start | bytes 1310720 | tf_op jit(solution)/shard_map/all_to_all | solution.py:101
  433.6 83.1 %reduce-scatter.6.cloned.1.call-start = ((), (), s32[]{:S(2)}) async-start(), calls=%async_computation.12 | async-start | bytes 2621440 | tf_op jit(solution)/shard_map/reduce_scatter | solution.py:622
  448.6 25.8 %collective-permute-start.38 = (bf16[176,2048]{1,0:T(8,128)(2,1)}, bf16[176,2048]{1,0:T(8,128)(2,1)}, u32[]{:S(2)}, u32[]{:S(2)}) collective-permute-start(bf16[176,2048]{1,0:T(8,128)(2,1)} %add_convert_fusion.4), channel_id=1, source_target_pairs={{0,8},{8,0},{16,24},{24,16},{1,9},{9,1},{17,25},{25,17},{2,10},{10... | collective-permute-start | bytes 2162696 | tf_op jit(solution)/shard_map/ppermute | solution.py:39
  449.4 29.0 %collective-permute-start.39 = (bf16[176,2048]{1,0:T(8,128)(2,1)}, bf16[176,2048]{1,0:T(8,128)(2,1)}, u32[]{:S(2)}, u32[]{:S(2)}) collective-permute-start(bf16[176,2048]{1,0:T(8,128)(2,1)} %add_convert_fusion.3), channel_id=1, source_target_pairs={{0,16},{8,24},{16,0},{24,8},{1,17},{9,25},{17,1},{25,9},{2,18},{10... | collective-permute-start | bytes 2162696 | tf_op jit(solution)/shard_map/ppermute | solution.py:39
  457.2 50.8 %all-to-all-start.6 = ((bf16[4,64,1536]{2,1,0:T(8,128)(2,1)}), bf16[4,64,1536]{2,1,0:T(8,128)(2,1)S(1)}, u32[]{:S(2)}, u32[]{:S(2)}) async-start(bf16[4,64,1536]{2,1,0:T(8,128)(2,1)} %bitcast.30), calls=%async_computation.9 | async-start | bytes 1572864 | tf_op jit(solution)/shard_map/all_to_all | solution.py:101
  474.5 41.0 %collective-permute-start.34 = (f32[2,2048]{1,0:T(2,128)S(1)}, f32[2,2048]{1,0:T(2,128)S(1)}, u32[]{:S(2)}, u32[]{:S(2)}) collective-permute-start(f32[2,2048]{1,0:T(2,128)S(1)} %add_add_fusion.1), channel_id=1, source_target_pairs={{0,3},{1,2},{2,1},{3,0},{4,7},{5,6},{6,5},{7,4},{8,11},{9,10},{10,... | collective-permute-start | bytes 49160 | tf_op jit(solution)/shard_map/ppermute | solution.py:39
  478.4 37.1 %collective-permute-start.33 = (f32[2,2048]{1,0:T(2,128)S(1)}, f32[2,2048]{1,0:T(2,128)S(1)}, u32[]{:S(2)}, u32[]{:S(2)}) collective-permute-start(f32[2,2048]{1,0:T(2,128)S(1)} %add_add_fusion.1), channel_id=1, source_target_pairs={{0,2},{1,3},{2,0},{3,1},{4,6},{5,7},{6,4},{7,5},{8,10},{9,11},{10,... | collective-permute-start | bytes 49160 | tf_op jit(solution)/shard_map/ppermute | solution.py:39
  480.2 35.2 %collective-permute-start.32 = (f32[2,2048]{1,0:T(2,128)S(1)}, f32[2,2048]{1,0:T(2,128)S(1)}, u32[]{:S(2)}, u32[]{:S(2)}) collective-permute-start(f32[2,2048]{1,0:T(2,128)S(1)} %add_add_fusion.1), channel_id=1, source_target_pairs={{0,1},{1,0},{2,3},{3,2},{4,5},{5,4},{6,7},{7,6},{8,9},{9,8},{10,11... | collective-permute-start | bytes 49160 | tf_op jit(solution)/shard_map/ppermute | solution.py:39
  485.3 25.4 %collective-permute-start.41 = (bf16[176,2048]{1,0:T(8,128)(2,1)S(1)}, bf16[176,2048]{1,0:T(8,128)(2,1)S(1)}, u32[]{:S(2)}, u32[]{:S(2)}) collective-permute-start(bf16[176,2048]{1,0:T(8,128)(2,1)S(1)} %copy-done.12), channel_id=1, source_target_pairs={{0,24},{8,16},{16,8},{24,0},{1,25},{9,17},{17,9},{25,1},{2,26},{10... | collective-permute-start | bytes 2162696 | tf_op jit(solution)/shard_map/ppermute | solution.py:39
  486.6 27.4 %collective-permute-start.40 = (bf16[64,2048]{1,0:T(8,128)(2,1)S(1)}, bf16[64,2048]{1,0:T(8,128)(2,1)S(1)}, u32[]{:S(2)}, u32[]{:S(2)}) collective-permute-start(bf16[64,2048]{1,0:T(8,128)(2,1)S(1)} %add_convert_fusion.7), channel_id=1, source_target_pairs={{0,0},{1,8},{2,16},{3,24},{8,1},{9,9},{10,17},{11,25},{16,2},{17,1... | collective-permute-start | bytes 786440 | tf_op jit(solution)/shard_map/ppermute | solution.py:700
  (61 other events, 780.2 us)
Sparse Core Ops, SparseCore 0:
  9.9 46.0 all-gather.12
  57.8 45.5 all-gather.14
  105.9 54.3 all-gather.8
  162.0 67.6 all-gather.16
  269.0 43.8 reduce-scatter.3
  341.2 45.9 all-gather.10
  389.6 46.5 reduce-scatter.7
  438.5 66.8 reduce-scatter.5

commit v6 on v5

--- a/solution.py
+++ b/solution.py
@@ -259,6 +259,23 @@
         out_shape=[jax.ShapeDtypeStruct((rows, wide), f32)] * 2,
         name="collect_units",
     )(first, second)
+
+
+def three_kernel(x_ref, *outs):
+    feats = x_ref.shape[2] // 3
+    for z in range(x_ref.shape[0]):
+        for i, out_ref in enumerate(outs):
+            part = x_ref[z, :, i * feats : (i + 1) * feats]
+            out_ref[:, z * feats : (z + 1) * feats] = part.astype(f32)
+
+
+def three_apart(x):
+    nz, rows, wide = x.shape
+    return pl.pallas_call(
+        three_kernel,
+        out_shape=[jax.ShapeDtypeStruct((rows, nz * wide // 3), f32)] * 3,
+        name="three_apart",
+    )(x)
 
 
 def units_back(gate, up, grad_hidden):
@@ -702,16 +719,7 @@
     )
     grad_w_gate, grad_w_up = line(lambda x, y: collect(x, y, pieces), grad_first, grad_second)
 
-    def three_piece(x):
-        return [
-            x[:, :, i * feats : (i + 1) * feats]
-            .transpose(1, 0, 2)
-            .reshape(own_rows, width)
-            .astype(f32)
-            for i in range(3)
-        ]
-
-    grad_w_query, grad_w_key, grad_w_value = line(three_piece, grad_qkv)
+    grad_w_query, grad_w_key, grad_w_value = line(three_apart, grad_qkv)
 
     grad_w_down = line(
         lambda own, other, came: summed(plus(own[0], other[0]), *came),
@@ -723,7 +731,7 @@
     for axis in ("c", "p", "z"):
         gains = paired_sum([gains, *spread_sums(gains, axis)])
     grad_w_out = line(lambda x: x.astype(f32), grad_w_out)
-    gains = gains + jnp.sum(line.token)
+    gains = gains + line.token[0, 0]
     grad_w_down = grad_w_down.astype(f32)
     return (
         activations,

time: 536 us -> 539 us (level)
  the two profiles are of different devices: /device:TPU:0 before, /device:TPU:6 now
where the time goes in v6:
time: 539 us; the launch traced here: 529 us
  waiting for transfers between devices  167 us (31%)
  Pallas kernels  97.1 us (18%)
  starting transfers between devices  88.5 us (16%)
  blocking collectives  61.5 us (11%)
  matrix products  39.6 us (7%)
  other arithmetic  29.6 us (5%)
  local copies, waits for them, and re-layouts  25.5 us (5%)
  between operations  20.7 us (4%)
    ppermute x12, waiting for transfers between devices, hop(): lax.ppermute(x, 'z', [(order[i], order[(i + 1) % n]) for i in range(n)])  76.6 us
    ppermute x29, waiting for transfers between devices, cross(): return lax.ppermute(x, axis, [(i, i ^ by) for i in range(n)])  69.2 us
    all_to_all x2, blocking collectives, exchange(): return lax.all_to_all(x, 'z', 0, 0, tiled=True)  61.5 us
    pallas_call x7, Pallas kernels, rows_product(): pl.pallas_call(functools.partial(rows_kernel, n, mode), grid_spec=pltpu.P...  41.5 us
    dot_general x5, matrix products, dot(): lax.dot_general(left, right, (dims, ((), ())), preferred_element_type=f32)  39.6 us
    ppermute x29, starting transfers between devices, cross(): return lax.ppermute(x, axis, [(i, i ^ by) for i in range(n)])  28.9 us
    ppermute x1, starting transfers between devices, body(): lax.ppermute(grad_w_out, ('p', 'z'), [(i * nz + j, j * nz + i) for i in r...  24.1 us
    all_to_all x5, starting transfers between devices, exchange(): return lax.all_to_all(x, 'z', 0, 0, tiled=True)  22.5 us
  transfers between devices with their start and end apart: 55, of which 22 were waited for; matrix products, arithmetic and copies ran while one was open for 14% of the time, Pallas kernels for 13%

profile of v6, /device:TPU:6, one launch (start us, length us, event | category | flops | bytes accessed | tf_op | source)
XLA Modules:
  0.0 529.2 jit_solution(9840589897157972481)
XLA Ops:
  11.0 25.0 %all_to_all.35 = bf16[4,64,1536]{2,1,0:T(8,128)(2,1)} all-to-all(bf16[4,64,1536]{2,1,0:T(8,128)(2,1)S(1)} %copy.35), channel_id=1, replica_groups=mesh['p'=4,'c'=2,'z'=4] {'z'}, dimensions={0} | all-to-all | bytes 1572864 | tf_op jit(solution)/shard_map/all_to_all | solution.py:101
  48.0 7.9 %collective-permute-done = bf16[128,2048]{1,0:T(8,128)(2,1)S(1)} collective-permute-done((bf16[128,2048]{1,0:T(8,128)(2,1)S(1)}, bf16[128,2048]{1,0:T(8,128)(2,1)S(1)}, u32[]{:S(2)}, u32[]{:S(2)}) %collective-permute-start) | collective-permute-done | bytes 524320 | tf_op jit(solution)/shard_map/ppermute | solution.py:49
  60.9 13.3 %collective-permute-done.3 = bf16[64,2048]{1,0:T(8,128)(2,1)S(1)} collective-permute-done((bf16[64,2048]{1,0:T(8,128)(2,1)S(1)}, bf16[64,2048]{1,0:T(8,128)(2,1)S(1)}, u32[]{:S(2)}, u32[]{:S(2)}) %collective-permute-start.3) | collective-permute-done | bytes 262176 | tf_op jit(solution)/shard_map/ppermute | solution.py:49
  83.1 9.2 %collective-permute-done.5 = bf16[64,2048]{1,0:T(8,128)(2,1)S(1)} collective-permute-done((bf16[64,2048]{1,0:T(8,128)(2,1)}, bf16[64,2048]{1,0:T(8,128)(2,1)S(1)}, u32[]{:S(2)}, u32[]{:S(2)}) %collective-permute-start.5) | collective-permute-done | bytes 262176 | tf_op jit(solution)/shard_map/ppermute | solution.py:49
  93.5 36.5 %all_to_all.36 = bf16[4,64,2816]{2,1,0:T(8,128)(2,1)} all-to-all(bf16[4,64,2816]{2,1,0:T(8,128)(2,1)S(1)} %copy-done.5), channel_id=1, replica_groups=mesh['p'=4,'c'=2,'z'=4] {'z'}, dimensions={0} | all-to-all | bytes 2883584 | tf_op jit(solution)/shard_map/all_to_all | solution.py:101
  132.2 7.8 %convolution_convert_fusion.2.qkv_ref = bf16[512,1536]{1,0:T(8,128)(2,1)S(1)} fusion(bf16[512,2048]{1,0:T(8,128)(2,1)} %constant_dynamic-update-slice_fusion.25.left_ref, bf16[2048,1536]{1,0:T(8,128)(2,1)} %bitcast.69), kind=kOutput, calls=%fused_computation.2 | convolution fusion | flops 3222011904 | bytes 9961472 | tf_op jit(solution)/shard_map/dot_general | solution.py:26
  151.2 12.5 %all-to-all-done.2 = bf16[4,128,512]{1,2,0:T(8,128)(2,1)S(1)} async-done(((bf16[4,128,512]{1,2,0:T(8,128)(2,1)}), bf16[4,128,512]{1,2,0:T(8,128)(2,1)S(1)}, u32[]{:S(2)}, u32[]{:S(2)}) %all-to-all-start.2) | async-done | bytes 524320 | tf_op jit(solution)/shard_map/all_to_all | solution.py:101
  168.9 5.6 %multiply_reduce_fusion.2 = (f32[128]{0:T(128)S(1)}, f32[128,2048]{1,0:T(8,128)S(1)}) fusion(bf16[128,2048]{0,1:T(8,128)(2,1)} %constant_dynamic-update-slice_fusion.8, bf16[2048,2048]{1,0:T(8,128)(2,1)} %bitcast.51, bf16[128,2048]{1,0:T(8,128)(2,1)S(1)} %copy-done.4), kind=kOutput, calls=%fused_computation.30 | convolution fusion | flops 1074790272 | bytes 10486272 | tf_op jit(solution)/shard_map/dot_general | solution.py:26
  177.3 14.0 %collective-permute-done.8.refs_1_ = bf16[128,2048]{1,0:T(8,128)(2,1)S(1)} collective-permute-done((bf16[128,2048]{1,0:T(8,128)(2,1)S(1)}, bf16[128,2048]{1,0:T(8,128)(2,1)S(1)}, u32[]{:S(2)}, u32[]{:S(2)}) %collective-permute-start.8) | collective-permute-done | bytes 524320 | tf_op jit(solution)/shard_map/ppermute | solution.py:49
  191.3 7.6 %collective-permute-done.9.refs_7_ = bf16[128,2048]{1,0:T(8,128)(2,1)S(1)} collective-permute-done((bf16[128,2048]{1,0:T(8,128)(2,1)}, bf16[128,2048]{1,0:T(8,128)(2,1)S(1)}, u32[]{:S(2)}, u32[]{:S(2)}) %collective-permute-start.9) | collective-permute-done | bytes 524320 | tf_op jit(solution)/shard_map/ppermute | solution.py:49
  198.9 12.8 %collective-permute-done.10.refs_2_ = bf16[128,2048]{1,0:T(8,128)(2,1)} collective-permute-done((bf16[128,2048]{1,0:T(8,128)(2,1)S(1)}, bf16[128,2048]{1,0:T(8,128)(2,1)}, u32[]{:S(2)}, u32[]{:S(2)}) %collective-permute-start.10) | collective-permute-done | bytes 524320 | tf_op jit(solution)/shard_map/ppermute | solution.py:49
  212.5 9.7 %collective-permute-done.11.refs_3_ = bf16[128,2048]{1,0:T(8,128)(2,1)} collective-permute-done((bf16[128,2048]{1,0:T(8,128)(2,1)}, bf16[128,2048]{1,0:T(8,128)(2,1)}, u32[]{:S(2)}, u32[]{:S(2)}) %collective-permute-start.11) | collective-permute-done | bytes 524320 | tf_op jit(solution)/shard_map/ppermute | solution.py:49
  222.2 5.1 all-gather.17.cloned.1.call-done
  227.3 20.1 %feed_units.1 = (bf16[512,1408]{1,0:T(8,128)(2,1)}, bf16[512,2816]{1,0:T(8,128)(2,1)}, bf16[512,2048]{1,0:T(8,128)(2,1)}, bf16[512,2048]{1,0:T(8,128)(2,1)}) custom-call(s32[4]{0:T(128)} %get-tuple-element.545.places_ref, bf16[128,2048]{1,0:T(8,128)(2,1)} %copy-done.30, bf16[128,2048]{1,0:T(8,128)(2,1)} %copy-done.32, ...), custom_call_target="tpu_custom_call" | custom-call | flops 10350000128 | tf_op jit(solution)/shard_map/feed_units/pallas_call | solution.py:323
  247.4 10.9 %convolution_convert_fusion.1 = bf16[512,2048]{1,0:T(8,128)(2,1)} fusion(bf16[512,2816]{1,0:T(8,128)(2,1)} %get-tuple-element.313.right_ref, bf16[2048,2816]{1,0:T(8,128)(2,1)} %bitcast.68), kind=kOutput, calls=%fused_computation.1 | convolution fusion | flops 5906628608 | bytes 16515072 | tf_op jit(solution)/shard_map/dot_general | solution.py:26
  258.2 7.9 %rows_product.7 = bf16[1024,2816]{1,0:T(8,128)(2,1)} custom-call(s32[2]{0:T(128)} %get-tuple-element.554.at_ref, bf16[512,2048]{1,0:T(8,128)(2,1)} %get-tuple-element.344.left_ref, bf16[512,2816]{1,0:T(8,128)(2,1)} %get-tuple-element.313.right_ref), custom_call_target="tpu_custom_call" | custom-call | flops 3737499904 | tf_op jit(solution)/shard_map/rows_product/pallas_call | solution.py:396
  266.5 8.0 %down_product.1 = (bf16[176,2048]{1,0:T(8,128)(2,1)}, bf16[176,2048]{1,0:T(8,128)(2,1)}, bf16[176,2048]{1,0:T(8,128)(2,1)}, bf16[176,2048]{1,0:T(8,128)(2,1)}, b...) custom-call(s32[2]{0:T(128)} %get-tuple-element.553.at_ref, ...), custom_call_target="tpu_custom_call" | custom-call | flops 4024999936 | tf_op jit(solution)/shard_map/down_product/pallas_call | solution.py:440
  275.9 6.3 %rows_product.8 = (bf16[256,1536]{1,0:T(8,128)(2,1)}, bf16[256,1536]{1,0:T(8,128)(2,1)}, bf16[256,1536]{1,0:T(8,128)(2,1)}, bf16[256,1536]{1,0:T(8,128)(2,1)}) custom-call(s32[2]{0:T(128)} %get-tuple-element.553.at_ref, bf16[512,2048]{1,0:T(8,128)(2,1)} %get-tuple-element.344.left_ref, bf16[512,2816]{1,0:T(8,128)(2,1)} %get-tuple-element.313.right_ref, ...), custom_call_target="tpu_custom_call" | custom-call | flops 3737499904 | tf_op jit(solution)/shard_map/rows_product/pallas_call | solution.py:396
  282.1 7.4 %rows_product.9 = (bf16[256,1280]{1,0:T(8,128)(2,1)}, bf16[256,1280]{1,0:T(8,128)(2,1)}, bf16[256,1280]{1,0:T(8,128)(2,1)}, bf16[256,1280]{1,0:T(8,128)(2,1)}) custom-call(s32[2]{0:T(128)} %get-tuple-element.553.at_ref, bf16[512,2048]{1,0:T(8,128)(2,1)} %get-tuple-element.344.left_ref, bf16[512,2816]{1,0:T(8,128)(2,1)} %get-tuple-element.313.right_ref, ...), custom_call_target="tpu_custom_call" | custom-call | flops 3737499904 | tf_op jit(solution)/shard_map/rows_product/pallas_call | solution.py:396
  291.6 7.9 %convolution_convert_fusion.3 = bf16[512,2048]{1,0:T(8,128)(2,1)} fusion(bf16[512,1408]{1,0:T(8,128)(2,1)} %get-tuple-element.352.left_ref, bf16[1408,2048]{1,0:T(8,128)(2,1)} %all-gather.13.cloned.1.call-done.refs_9_), kind=kOutput, calls=%fused_computation.3 | convolution fusion | flops 2953838592 | bytes 9306112 | tf_op jit(solution)/shard_map/dot_general | solution.py:26
  299.4 10.2 %collective-permute-done.13 = bf16[256,1536]{1,0:T(8,128)(2,1)} collective-permute-done((bf16[256,1536]{1,0:T(8,128)(2,1)}, bf16[256,1536]{1,0:T(8,128)(2,1)}, u32[]{:S(2)}, u32[]{:S(2)}) %collective-permute-start.13) | collective-permute-done | bytes 786464 | tf_op jit(solution)/shard_map/ppermute | solution.py:39
  316.1 8.8 %heads_product.1 = bf16[4,128,512]{2,1,0:T(8,128)(2,1)} custom-call(bf16[128,2048]{1,0:T(8,128)(2,1)} %get-tuple-element.375.x_ref, bf16[2048,2048]{1,0:T(8,128)(2,1)} %bitcast.52), custom_call_target="tpu_custom_call" | custom-call | tf_op jit(solution)/shard_map/heads_product/pallas_call | solution.py:509
  341.4 10.8 %collective-permute-done.20 = bf16[256,1280]{1,0:T(8,128)(2,1)S(1)} collective-permute-done((bf16[256,1280]{1,0:T(8,128)(2,1)}, bf16[256,1280]{1,0:T(8,128)(2,1)S(1)}, u32[]{:S(2)}, u32[]{:S(2)}) %collective-permute-start.20) | collective-permute-done | bytes 655392 | tf_op jit(solution)/shard_map/ppermute | solution.py:39
  353.5 7.0 %shard_map.213.right_ref = bf16[512,1536]{1,0:T(8,128)(2,1)S(1)} custom-call(bf16[512,1536]{1,0:T(8,128)(2,1)S(1)} %convolution_convert_fusion.2.qkv_ref, bf16[512,512]{1,0:T(8,128)(2,1)S(1)} %bitcast.46, s32[512,1]{1,0:T(8,128)S(1)} %copy.36.docs_down_ref, s32[1,512]{1,0:T(1,128)S(1)} %bitcast.50), custom_call_target="tpu_custom_call" | custom-call | tf_op jit(solution)/shard_map/pallas_call | solution.py:204
  361.7 7.5 %convolution_convert_fusion = bf16[512,2048]{1,0:T(8,128)(2,1)} fusion(bf16[512,1536]{1,0:T(8,128)(2,1)S(1)} %shard_map.213.right_ref, bf16[2048,1536]{1,0:T(8,128)(2,1)} %bitcast.70), kind=kOutput, calls=%fused_computation | convolution fusion | flops 3222274048 | bytes 9961472 | tf_op jit(solution)/shard_map/dot_general | solution.py:26
  369.2 5.6 %rows_product.10 = bf16[1024,1536]{1,0:T(8,128)(2,1)} custom-call(s32[2]{0:T(128)} %get-tuple-element.554.at_ref, bf16[512,2048]{1,0:T(8,128)(2,1)} %constant_dynamic-update-slice_fusion.25.left_ref, bf16[512,1536]{1,0:T(8,128)(2,1)} %copy-done.1), custom_call_target="tpu_custom_call" | custom-call | flops 3737499904 | tf_op jit(solution)/shard_map/rows_product/pallas_call | solution.py:396
  381.8 11.2 %collective-permute-done.23 = bf16[256,1280]{1,0:T(8,128)(2,1)S(1)} collective-permute-done((bf16[256,1280]{1,0:T(8,128)(2,1)S(1)}, bf16[256,1280]{1,0:T(8,128)(2,1)S(1)}, u32[]{:S(2)}, u32[]{:S(2)}) %collective-permute-start.23) | collective-permute-done | bytes 655392 | tf_op jit(solution)/shard_map/ppermute | solution.py:39
  393.0 6.3 %rows_product.11 = (bf16[256,1536]{1,0:T(8,128)(2,1)}, bf16[256,1536]{1,0:T(8,128)(2,1)}, bf16[256,1536]{1,0:T(8,128)(2,1)}, bf16[256,1536]{1,0:T(8,128)(2,1)}) custom-call(s32[2]{0:T(128)} %get-tuple-element.553.at_ref, bf16[512,2048]{1,0:T(8,128)(2,1)} %constant_dynamic-update-slice_fusion.25.left_ref, bf16[512,1536]{1,0:T(8,128)(2,1)} %copy-done.1, ...), custom_call_target="tpu_custom_call" | custom-call | flops 3737499904 | tf_op jit(solution)/shard_map/rows_product/pallas_call | solution.py:396
  400.9 17.0 %collective-permute-done.24 = bf16[256,1536]{1,0:T(8,128)(2,1)S(1)} collective-permute-done((bf16[256,1536]{1,0:T(8,128)(2,1)}, bf16[256,1536]{1,0:T(8,128)(2,1)S(1)}, u32[]{:S(2)}, u32[]{:S(2)}) %collective-permute-start.24) | collective-permute-done | bytes 786464 | tf_op jit(solution)/shard_map/ppermute | solution.py:39
  432.0 14.1 %collective-permute-done.26 = bf16[256,1536]{1,0:T(8,128)(2,1)} collective-permute-done((bf16[256,1536]{1,0:T(8,128)(2,1)}, bf16[256,1536]{1,0:T(8,128)(2,1)}, u32[]{:S(2)}, u32[]{:S(2)}) %collective-permute-start.26) | collective-permute-done | bytes 786464 | tf_op jit(solution)/shard_map/ppermute | solution.py:39
  454.9 4.9 all-to-all-start.6
  483.3 24.1 %collective-permute-start.40 = (bf16[64,2048]{1,0:T(8,128)(2,1)S(1)}, bf16[64,2048]{1,0:T(8,128)(2,1)S(1)}, u32[]{:S(2)}, u32[]{:S(2)}) collective-permute-start(bf16[64,2048]{1,0:T(8,128)(2,1)S(1)} %add_convert_fusion.7), channel_id=1, source_target_pairs={{0,0},{1,8},{2,16},{3,24},{8,1},{9,9},{10,17},{11,25},{16,2},{17,1... | collective-permute-start | bytes 786440 | tf_op jit(solution)/shard_map/ppermute | solution.py:717
  (276 shorter events, 145.9 us)
Async XLA Ops:
  7.2 48.8 %all-gather.13.cloned.1.call-start = ((), (), s32[]{:S(2)}) async-start(), calls=%async_computation.15 | async-start | bytes 6488064 | tf_op jit(solution)/shard_map/all_gather | solution.py:66
  7.9 124.3 %all-gather.15.cloned.1.call-start = ((), (), s32[]{:S(2)}) async-start(), calls=%async_computation.16 | async-start | bytes 7077888 | tf_op jit(solution)/shard_map/all_gather | solution.py:66
  36.0 132.9 %all-gather.9.cloned.1.call-start = ((), (), s32[]{:S(2)}) async-start(), calls=%async_computation.10 | async-start | bytes 9437184 | tf_op jit(solution)/shard_map/all_gather | solution.py:66
  37.2 18.8 %collective-permute-start = (bf16[128,2048]{1,0:T(8,128)(2,1)S(1)}, bf16[128,2048]{1,0:T(8,128)(2,1)S(1)}, u32[]{:S(2)}, u32[]{:S(2)}) collective-permute-start(bf16[128,2048]{1,0:T(8,128)(2,1)S(1)} %constant_dynamic-update-slice_fusion), channel_id=1, source_target_pairs={{1,3},{3,2},{2,0},{0,1},{5,7},{7,6},{6,4},{4,5},{9,11},{11,10},{10... | collective-permute-start | bytes 1572872 | tf_op jit(solution)/shard_map/ppermute | solution.py:49
  93.4 133.9 %all-gather.17.cloned.1.call-start = ((), (), s32[]{:S(2)}) async-start(), calls=%async_computation.17 | async-start | bytes 12976128 | tf_op jit(solution)/shard_map/all_gather | solution.py:66
  149.2 162.2 %reduce-scatter.4.cloned.1.call-start = ((), (), s32[]{:S(2)}) async-start(), calls=%async_computation.11 | async-start | bytes 2621440 | tf_op jit(solution)/shard_map/reduce_scatter | solution.py:639
  149.3 25.5 %collective-permute-start.7 = (bf16[128,2048]{1,0:T(8,128)(2,1)}, bf16[128,2048]{1,0:T(8,128)(2,1)}, u32[]{:S(2)}, u32[]{:S(2)}) collective-permute-start(bf16[128,2048]{1,0:T(8,128)(2,1)} %collective-permute-done.6.refs_5_), channel_id=1, source_target_pairs={{1,3},{3,2},{2,0},{0,1},{5,7},{7,6},{6,4},{4,5},{9,11},{11,10},{10... | collective-permute-start | bytes 1572872 | tf_op jit(solution)/shard_map/ppermute | solution.py:49
  176.1 22.7 %collective-permute-start.9 = (bf16[128,2048]{1,0:T(8,128)(2,1)}, bf16[128,2048]{1,0:T(8,128)(2,1)S(1)}, u32[]{:S(2)}, u32[]{:S(2)}) collective-permute-start(bf16[128,2048]{1,0:T(8,128)(2,1)} %collective-permute-done.7.refs_6_), channel_id=1, source_target_pairs={{1,3},{3,2},{2,0},{0,1},{5,7},{7,6},{6,4},{4,5},{9,11},{11,10},{10... | collective-permute-start | bytes 1572872 | tf_op jit(solution)/shard_map/ppermute | solution.py:49
  274.5 50.4 %collective-permute-start.16 = (bf16[176,2048]{1,0:T(8,128)(2,1)}, bf16[176,2048]{1,0:T(8,128)(2,1)}, u32[]{:S(2)}, u32[]{:S(2)}) collective-permute-start(bf16[176,2048]{1,0:T(8,128)(2,1)} %get-tuple-element.365), channel_id=1, source_target_pairs={{0,4},{4,0},{1,5},{5,1},{2,6},{6,2},{3,7},{7,3},{8,12},{12,8},{9,1... | collective-permute-start | bytes 2162696 | tf_op jit(solution)/shard_map/ppermute | solution.py:39
  274.7 50.2 %collective-permute-start.17 = (bf16[176,2048]{1,0:T(8,128)(2,1)}, bf16[176,2048]{1,0:T(8,128)(2,1)}, u32[]{:S(2)}, u32[]{:S(2)}) collective-permute-start(bf16[176,2048]{1,0:T(8,128)(2,1)} %get-tuple-element.366), channel_id=1, source_target_pairs={{0,4},{4,0},{1,5},{5,1},{2,6},{6,2},{3,7},{7,3},{8,12},{12,8},{9,1... | collective-permute-start | bytes 2162696 | tf_op jit(solution)/shard_map/ppermute | solution.py:39
  275.0 49.9 %collective-permute-start.18 = (bf16[176,2048]{1,0:T(8,128)(2,1)}, bf16[176,2048]{1,0:T(8,128)(2,1)}, u32[]{:S(2)}, u32[]{:S(2)}) collective-permute-start(bf16[176,2048]{1,0:T(8,128)(2,1)} %get-tuple-element.367), channel_id=1, source_target_pairs={{0,4},{4,0},{1,5},{5,1},{2,6},{6,2},{3,7},{7,3},{8,12},{12,8},{9,1... | collective-permute-start | bytes 2162696 | tf_op jit(solution)/shard_map/ppermute | solution.py:39
  289.5 20.1 %collective-permute-start.13 = (bf16[256,1536]{1,0:T(8,128)(2,1)}, bf16[256,1536]{1,0:T(8,128)(2,1)}, u32[]{:S(2)}, u32[]{:S(2)}) collective-permute-start(bf16[256,1536]{1,0:T(8,128)(2,1)} %get-tuple-element.340), channel_id=1, source_target_pairs={{0,8},{8,0},{16,24},{24,16},{1,9},{9,1},{17,25},{25,17},{2,10},{10... | collective-permute-start | bytes 2359304 | tf_op jit(solution)/shard_map/ppermute | solution.py:39
  290.5 20.9 %collective-permute-start.14 = (bf16[256,1536]{1,0:T(8,128)(2,1)}, bf16[256,1536]{1,0:T(8,128)(2,1)}, u32[]{:S(2)}, u32[]{:S(2)}) collective-permute-start(bf16[256,1536]{1,0:T(8,128)(2,1)} %get-tuple-element.341), channel_id=1, source_target_pairs={{0,16},{8,24},{16,0},{24,8},{1,17},{9,25},{17,1},{25,9},{2,18},{10... | collective-permute-start | bytes 2359304 | tf_op jit(solution)/shard_map/ppermute | solution.py:39
  312.5 24.0 %collective-permute-start.15 = (bf16[256,1536]{1,0:T(8,128)(2,1)}, bf16[256,1536]{1,0:T(8,128)(2,1)}, u32[]{:S(2)}, u32[]{:S(2)}) collective-permute-start(bf16[256,1536]{1,0:T(8,128)(2,1)} %get-tuple-element.357), channel_id=1, source_target_pairs={{0,24},{8,16},{16,8},{24,0},{1,25},{9,17},{17,9},{25,1},{2,26},{10... | collective-permute-start | bytes 2359304 | tf_op jit(solution)/shard_map/ppermute | solution.py:39
  324.9 28.6 %all-to-all-start.4 = ((bf16[4,128,512]{2,1,0:T(8,128)(2,1)}), bf16[4,128,512]{2,1,0:T(8,128)(2,1)S(1)}, u32[]{:S(2)}, u32[]{:S(2)}) async-start(bf16[4,128,512]{2,1,0:T(8,128)(2,1)} %heads_product.1), calls=%async_computation.5 | async-start | bytes 1048576 | tf_op jit(solution)/shard_map/all_to_all | solution.py:101
  329.5 91.6 %all-gather.11.cloned.1.call-start = ((), (), s32[]{:S(2)}) async-start(), calls=%async_computation.14 | async-start | bytes 2621440 | tf_op jit(solution)/shard_map/all_gather | solution.py:660
  338.2 116.7 %reduce-scatter.8.cloned.1.call-start = ((), (), s32[]{:S(2)}) async-start(), calls=%async_computation.13 | async-start | bytes 2621440 | tf_op jit(solution)/shard_map/reduce_scatter | solution.py:639
  377.0 41.2 %all-to-all-start.3 = ((bf16[4,64,1536]{2,1,0:T(8,128)(2,1)}), bf16[4,64,1536]{2,1,0:T(8,128)(2,1)S(1)}, u32[]{:S(2)}, u32[]{:S(2)}) async-start(bf16[4,64,1536]{2,1,0:T(8,128)(2,1)} %bitcast.25), calls=%async_computation.4 | async-start | bytes 1572864 | tf_op jit(solution)/shard_map/all_to_all | solution.py:101
  399.3 18.7 %collective-permute-start.24 = (bf16[256,1536]{1,0:T(8,128)(2,1)}, bf16[256,1536]{1,0:T(8,128)(2,1)S(1)}, u32[]{:S(2)}, u32[]{:S(2)}) collective-permute-start(bf16[256,1536]{1,0:T(8,128)(2,1)} %get-tuple-element.425), channel_id=1, source_target_pairs={{0,8},{8,0},{16,24},{24,16},{1,9},{9,1},{17,25},{25,17},{2,10},{10... | collective-permute-start | bytes 2359304 | tf_op jit(solution)/shard_map/ppermute | solution.py:39
  399.9 18.3 %collective-permute-start.25 = (bf16[256,1536]{1,0:T(8,128)(2,1)}, bf16[256,1536]{1,0:T(8,128)(2,1)S(1)}, u32[]{:S(2)}, u32[]{:S(2)}) collective-permute-start(bf16[256,1536]{1,0:T(8,128)(2,1)} %get-tuple-element.426), channel_id=1, source_target_pairs={{0,16},{8,24},{16,0},{24,8},{1,17},{9,25},{17,1},{25,9},{2,18},{10... | collective-permute-start | bytes 2359304 | tf_op jit(solution)/shard_map/ppermute | solution.py:39
  424.9 23.4 %collective-permute-start.27 = (bf16[256,2048]{1,0:T(8,128)(2,1)}, bf16[256,2048]{1,0:T(8,128)(2,1)}, u32[]{:S(2)}, u32[]{:S(2)}) collective-permute-start(bf16[256,2048]{1,0:T(8,128)(2,1)} %rows_product.12), channel_id=1, source_target_pairs={{0,4},{4,0},{1,5},{5,1},{2,6},{6,2},{3,7},{7,3},{8,12},{12,8},{9,1... | collective-permute-start | bytes 3145736 | tf_op jit(solution)/shard_map/ppermute | solution.py:39
  424.9 21.2 %collective-permute-start.26 = (bf16[256,1536]{1,0:T(8,128)(2,1)}, bf16[256,1536]{1,0:T(8,128)(2,1)}, u32[]{:S(2)}, u32[]{:S(2)}) collective-permute-start(bf16[256,1536]{1,0:T(8,128)(2,1)} %get-tuple-element.447), channel_id=1, source_target_pairs={{0,24},{8,16},{16,8},{24,0},{1,25},{9,17},{17,9},{25,1},{2,26},{10... | collective-permute-start | bytes 2359304 | tf_op jit(solution)/shard_map/ppermute | solution.py:39
  426.5 28.4 %all-to-all-start.5 = ((bf16[4,64,1280]{2,1,0:T(8,128)(2,1)}), bf16[4,64,1280]{2,1,0:T(8,128)(2,1)S(1)}, u32[]{:S(2)}, u32[]{:S(2)}) async-start(bf16[4,64,1280]{2,1,0:T(8,128)(2,1)} %bitcast.27), calls=%async_computation.8 | async-start | bytes 1310720 | tf_op jit(solution)/shard_map/all_to_all | solution.py:101
  431.2 88.7 %reduce-scatter.6.cloned.1.call-start = ((), (), s32[]{:S(2)}) async-start(), calls=%async_computation.12 | async-start | bytes 2621440 | tf_op jit(solution)/shard_map/reduce_scatter | solution.py:639
  446.1 21.3 %collective-permute-start.38 = (bf16[176,2048]{1,0:T(8,128)(2,1)}, bf16[176,2048]{1,0:T(8,128)(2,1)}, u32[]{:S(2)}, u32[]{:S(2)}) collective-permute-start(bf16[176,2048]{1,0:T(8,128)(2,1)} %add_convert_fusion.4), channel_id=1, source_target_pairs={{0,8},{8,0},{16,24},{24,16},{1,9},{9,1},{17,25},{25,17},{2,10},{10... | collective-permute-start | bytes 2162696 | tf_op jit(solution)/shard_map/ppermute | solution.py:39
  447.5 20.8 %collective-permute-start.39 = (bf16[176,2048]{1,0:T(8,128)(2,1)}, bf16[176,2048]{1,0:T(8,128)(2,1)}, u32[]{:S(2)}, u32[]{:S(2)}) collective-permute-start(bf16[176,2048]{1,0:T(8,128)(2,1)} %add_convert_fusion.3), channel_id=1, source_target_pairs={{0,16},{8,24},{16,0},{24,8},{1,17},{9,25},{17,1},{25,9},{2,18},{10... | collective-permute-start | bytes 2162696 | tf_op jit(solution)/shard_map/ppermute | solution.py:39
  454.9 56.0 %all-to-all-start.6 = ((bf16[4,64,1536]{2,1,0:T(8,128)(2,1)}), bf16[4,64,1536]{2,1,0:T(8,128)(2,1)S(1)}, u32[]{:S(2)}, u32[]{:S(2)}) async-start(bf16[4,64,1536]{2,1,0:T(8,128)(2,1)} %bitcast.30), calls=%async_computation.9 | async-start | bytes 1572864 | tf_op jit(solution)/shard_map/all_to_all | solution.py:101
  470.9 43.2 %collective-permute-start.41 = (bf16[176,2048]{1,0:T(8,128)(2,1)}, bf16[176,2048]{1,0:T(8,128)(2,1)S(1)}, u32[]{:S(2)}, u32[]{:S(2)}) collective-permute-start(bf16[176,2048]{1,0:T(8,128)(2,1)} %add_convert_fusion.2), channel_id=1, source_target_pairs={{0,24},{8,16},{16,8},{24,0},{1,25},{9,17},{17,9},{25,1},{2,26},{10... | collective-permute-start | bytes 2162696 | tf_op jit(solution)/shard_map/ppermute | solution.py:39
  472.3 46.3 %collective-permute-start.34 = (f32[2,2048]{1,0:T(2,128)S(1)}, f32[2,2048]{1,0:T(2,128)S(1)}, u32[]{:S(2)}, u32[]{:S(2)}) collective-permute-start(f32[2,2048]{1,0:T(2,128)S(1)} %add_add_fusion.1), channel_id=1, source_target_pairs={{0,3},{1,2},{2,1},{3,0},{4,7},{5,6},{6,5},{7,4},{8,11},{9,10},{10,... | collective-permute-start | bytes 49160 | tf_op jit(solution)/shard_map/ppermute | solution.py:39
  476.6 42.1 %collective-permute-start.33 = (f32[2,2048]{1,0:T(2,128)S(1)}, f32[2,2048]{1,0:T(2,128)S(1)}, u32[]{:S(2)}, u32[]{:S(2)}) collective-permute-start(f32[2,2048]{1,0:T(2,128)S(1)} %add_add_fusion.1), channel_id=1, source_target_pairs={{0,2},{1,3},{2,0},{3,1},{4,6},{5,7},{6,4},{7,5},{8,10},{9,11},{10,... | collective-permute-start | bytes 49160 | tf_op jit(solution)/shard_map/ppermute | solution.py:39
  479.6 39.1 %collective-permute-start.32 = (f32[2,2048]{1,0:T(2,128)S(1)}, f32[2,2048]{1,0:T(2,128)S(1)}, u32[]{:S(2)}, u32[]{:S(2)}) collective-permute-start(f32[2,2048]{1,0:T(2,128)S(1)} %add_add_fusion.1), channel_id=1, source_target_pairs={{0,1},{1,0},{2,3},{3,2},{4,5},{5,4},{6,7},{7,6},{8,9},{9,8},{10,11... | collective-permute-start | bytes 49160 | tf_op jit(solution)/shard_map/ppermute | solution.py:39
  483.3 34.1 %collective-permute-start.40 = (bf16[64,2048]{1,0:T(8,128)(2,1)S(1)}, bf16[64,2048]{1,0:T(8,128)(2,1)S(1)}, u32[]{:S(2)}, u32[]{:S(2)}) collective-permute-start(bf16[64,2048]{1,0:T(8,128)(2,1)S(1)} %add_convert_fusion.7), channel_id=1, source_target_pairs={{0,0},{1,8},{2,16},{3,24},{8,1},{9,9},{10,17},{11,25},{16,2},{17,1... | collective-permute-start | bytes 786440 | tf_op jit(solution)/shard_map/ppermute | solution.py:717
  (61 other events, 791.5 us)
Sparse Core Ops, SparseCore 0:
  9.9 43.5 all-gather.12
  55.4 45.4 all-gather.14
  103.4 54.3 all-gather.8
  159.6 67.6 all-gather.16
  266.6 44.7 reduce-scatter.3
  338.3 48.1 all-gather.10
  388.9 44.8 reduce-scatter.7
  436.1 62.4 reduce-scatter.5
